TPU v7x, 32 devices: a whole 2x2x4 slice. The times are simulated.
32 devices in a mesh: blk: 8 (over y, x, core), head: 4 (over z).
Axes of the slice: x: 2, y: 2, z: 4, core: 2. Of those that a mesh axis runs over, the one named last changes fastest.
Arguments:
- inputs: bfloat16 [2, 2048, 2048], P(None, ('blk', 'head')), may hold values from -6 to 6
- cotangent: bfloat16 [2, 2048, 2048], P(None, ('blk', 'head')), may hold values from -6 to 6
- lengths: int32 [2], replicated, may hold values from 1024 to 2048, as said below
- positions: int32 [2, 2048], replicated, may hold values from 0 to 2047, as said below
- attn_gain: bfloat16 [2048], P(('blk', 'head')), may hold values from 0.5 to 1.5
- mlp_gain: bfloat16 [2048], P(('blk', 'head')), may hold values from 0.5 to 1.5
- w_query: bfloat16 [2048, 2048], P(('blk', 'head')), may hold values from -0.5 to 0.5
- key_projection: bfloat16 [2048, 512], P(('blk', 'head')), may hold values from -0.5 to 0.5
- value_projection: bfloat16 [2048, 512], P(('blk', 'head')), may hold values from -0.125 to 0.125
- w_out: bfloat16 [2048, 2048], P(('blk', 'head')), may hold values from -3 to 3
- w_gate: bfloat16 [2048, 8192], P('blk', 'head'), may hold values from -0.125 to 0.125
- w_up: bfloat16 [2048, 8192], P('blk', 'head'), may hold values from -0.125 to 0.125
- w_down: bfloat16 [8192, 2048], P('head', 'blk'), may hold values from -0.25 to 0.25
Outputs:
- output: bfloat16 [2, 2048, 2048], P(None, ('blk', 'head'))
- input_grad: float32 [2, 2048, 2048], P(None, ('blk', 'head'))
- grad_attn_gain: float32 [2048], P(('blk', 'head'))
- grad_mlp_gain: float32 [2048], P(('blk', 'head'))
- grad_query: float32 [2048, 2048], P(('blk', 'head'))
- grad_key: float32 [2048, 512], P(('blk', 'head'))
- grad_value: float32 [2048, 512], P(('blk', 'head'))
- grad_out: float32 [2048, 2048], P(('blk', 'head'))
- grad_gate: float32 [2048, 8192], P('blk', 'head')
- grad_up: float32 [2048, 8192], P('blk', 'head')
- grad_down: float32 [8192, 2048], P('head', 'blk')
Inputs may be any that keep to these rules, and one draw needn't show every extreme that they name: `lengths`: at least half of 2048; in every draw one micro-batch has exactly 2048. Each row is a permutation of 0 to 2047; aligned block b of 64 slots holds, in some order, the run of half of 64 positions starting at b times half of 64 and the mirrored run starting at (2048 - (b + 1) times half of 64).
All inputs are finite; a program needn't handle non-finite values.
Results may differ from a plain program's by a relative error of at most 0.02.
Values may be sent and summed in bfloat16 or wider, within the bound.
No kernel may reach another device: no remote copies, remote signals or barrier semaphores. Data moves between devices by JAX's collectives and lax.ppermute only.
A program may use at most 168 MiB of HBM per device.

v0:
```python
import jax
import jax.numpy as jnp
from jax import lax
from jax.sharding import PartitionSpec as P

MODEL_WIDTH = 2048
QUERY_HEADS = 32
KEY_VALUE_HEADS = 8
HEAD_SIZE = 64
MICRO = 2


SCORE_SCALE = 0.015625
RESIDUAL_SCALE = 0.22
EPSILON = 1e-06
ROPE_BASE = 10000000.0
NEG_FILL = -1e30


def from_behind(x, axis, by):
    devices = lax.axis_size(axis)
    return lax.ppermute(x, axis, [(i, (i + by) % devices) for i in range(devices)])


def matrix_product(left, right):
    return jnp.dot(left, right, preferred_element_type=jnp.float32)


def left_product(left, right):
    return lax.dot_general(
        left, right, (((0,), (0,)), ((), ())), preferred_element_type=jnp.float32
    )


def right_product(left, right):
    return lax.dot_general(
        left, right, (((1,), (1,)), ((), ())), preferred_element_type=jnp.float32
    )


def normalize(values, gain):
    scale_inv = lax.rsqrt(jnp.mean(values * values, -1, keepdims=True) + EPSILON)
    scaled = values * scale_inv
    return (scaled * gain, scale_inv, scaled)


def norm_back(upstream, gain, scale_inv, scaled):
    through = upstream * gain
    inner = jnp.mean(through * scaled, -1, keepdims=True)
    return (scale_inv * (through - scaled * inner), jnp.sum(upstream * scaled, 0))


def rotary_tables(positions_row):
    half_dim = HEAD_SIZE // 2
    frequency = ROPE_BASE ** (-(jnp.arange(half_dim).astype(jnp.float32) * 2.0) / HEAD_SIZE)
    angles = positions_row.astype(jnp.float32)[:, None] * frequency[None, :]
    angles = jnp.concatenate([angles, angles], -1)
    return (jnp.cos(angles)[:, None, :], jnp.sin(angles)[:, None, :])


def rotate(values):
    half_dim = values.shape[-1] // 2
    return jnp.concatenate([-values[..., half_dim:], values[..., :half_dim]], -1)


def rotary(values, cosine, sine):
    return values * cosine + rotate(values) * sine


def rotary_back(upstream, cosine, sine):
    return upstream * cosine - rotate(upstream) * sine


def body(
    inputs,
    cotangent,
    lengths,
    positions,
    attn_gain,
    mlp_gain,
    w_query,
    key_projection,
    value_projection,
    w_out,
    w_gate,
    w_up,
    w_down,
):
    blocks = lax.axis_size("blk")
    grouped_heads = lax.axis_size("head")
    blk_index = lax.axis_index("blk")
    head_index = lax.axis_index("head")
    token_rows = inputs.shape[1]
    group_rows = token_rows * grouped_heads
    q_heads = QUERY_HEADS // grouped_heads
    key_value_heads = KEY_VALUE_HEADS // grouped_heads
    shared_portion = QUERY_HEADS // KEY_VALUE_HEADS
    local_ff = w_gate.shape[1]
    attn_acc = (
        jnp.zeros((MODEL_WIDTH,), jnp.float32),
        jnp.zeros((MODEL_WIDTH,), jnp.float32),
        jnp.zeros((MODEL_WIDTH, QUERY_HEADS * HEAD_SIZE), jnp.float32),
        jnp.zeros((MODEL_WIDTH, KEY_VALUE_HEADS * HEAD_SIZE), jnp.float32),
        jnp.zeros((MODEL_WIDTH, KEY_VALUE_HEADS * HEAD_SIZE), jnp.float32),
        jnp.zeros((QUERY_HEADS * HEAD_SIZE, MODEL_WIDTH), jnp.float32),
    )
    mlp_acc = (
        jnp.zeros((MODEL_WIDTH, local_ff), jnp.float32),
        jnp.zeros((MODEL_WIDTH, local_ff), jnp.float32),
        jnp.zeros((local_ff, MODEL_WIDTH), jnp.float32),
    )
    attn_total = None
    mlp_total = None
    outputs = []
    input_grads = []
    for micro_idx in range(MICRO):
        attn_set = (
            lax.all_gather(w_query, ("blk", "head"), axis=0, tiled=True),
            lax.all_gather(key_projection, ("blk", "head"), axis=0, tiled=True),
            lax.all_gather(value_projection, ("blk", "head"), axis=0, tiled=True),
            lax.all_gather(w_out, ("blk", "head"), axis=0, tiled=True),
            lax.all_gather(attn_gain, ("blk", "head"), axis=0, tiled=True),
            lax.all_gather(mlp_gain, ("blk", "head"), axis=0, tiled=True),
        )
        mlp_set = (
            lax.all_gather(w_gate, "blk", axis=0, tiled=True),
            lax.all_gather(w_up, "blk", axis=0, tiled=True),
            lax.all_gather(w_down, "blk", axis=1, tiled=True),
        )
        attn_set, mlp_set = (attn_set, mlp_set)
        w_q_all, stacked_key_weight, w_v_all, w_o_all, gain_a, gain_m = attn_set
        w_g_all, w_u_all, w_d_all = mlp_set
        gain_one = gain_a.astype(jnp.float32)
        gain_two = gain_m.astype(jnp.float32)
        w_gate_up = jnp.concatenate([w_g_all, w_u_all], 1)
        slot_position = positions[micro_idx]
        sequence_length = lengths[micro_idx]
        my_pos = lax.dynamic_slice_in_dim(
            slot_position, (blk_index * grouped_heads + head_index) * token_rows, token_rows
        )
        group_pos = lax.dynamic_slice_in_dim(slot_position, blk_index * group_rows, group_rows)
        x_rows = inputs[micro_idx].astype(jnp.float32)
        first_normed_input, inv_one, scaled_one = normalize(x_rows, gain_one)
        first_normed_reduced = first_normed_input.astype(jnp.bfloat16)
        cosine, sine = rotary_tables(my_pos)
        q_raw = matrix_product(first_normed_reduced, w_q_all).reshape(
            token_rows, QUERY_HEADS, HEAD_SIZE
        )
        q_rot = (
            rotary(q_raw, cosine, sine)
            .astype(jnp.bfloat16)
            .reshape(token_rows, grouped_heads, q_heads * HEAD_SIZE)
        )
        unrotated_keys = matrix_product(first_normed_reduced, stacked_key_weight).reshape(
            token_rows, KEY_VALUE_HEADS, HEAD_SIZE
        )
        k_rot = (
            rotary(unrotated_keys, cosine, sine)
            .astype(jnp.bfloat16)
            .reshape(token_rows, grouped_heads, key_value_heads * HEAD_SIZE)
        )
        v_tok = (
            matrix_product(first_normed_reduced, w_v_all)
            .astype(jnp.bfloat16)
            .reshape(token_rows, grouped_heads, key_value_heads * HEAD_SIZE)
        )
        kv_tok = jnp.concatenate([k_rot, v_tok], 2)
        q_group, kv_group = (
            lax.all_to_all(q_rot, "head", split_axis=1, concat_axis=0, tiled=True),
            lax.all_to_all(kv_tok, "head", split_axis=1, concat_axis=0, tiled=True),
        )
        q_group = q_group.reshape(group_rows, key_value_heads, shared_portion, HEAD_SIZE)
        kv_group = kv_group.reshape(group_rows, 2 * key_value_heads * HEAD_SIZE)
        kv_all = lax.all_gather(kv_group, "blk", axis=0, tiled=True)

        def split_kv(kv_block):
            key_row_table = kv_block[:, : key_value_heads * HEAD_SIZE].reshape(
                kv_block.shape[0], key_value_heads, HEAD_SIZE
            )
            value_row_table = kv_block[:, key_value_heads * HEAD_SIZE :].reshape(
                kv_block.shape[0], key_value_heads, HEAD_SIZE
            )
            return (key_row_table, value_row_table)

        def masked_scores(key_row_table, key_pos):
            scores = SCORE_SCALE * jnp.einsum(
                "qhgd,khd->qhgk", q_group, key_row_table, preferred_element_type=jnp.float32
            )
            visible = (key_pos[None, :] <= group_pos[:, None]) & (
                key_pos[None, :] < sequence_length
            )
            return (scores, visible[:, None, None, :])

        def forward_step(running, block_in):
            top, total, accum = running
            kv_block, key_pos = block_in
            key_row_table, value_row_table = split_kv(kv_block)
            scores, visible = masked_scores(key_row_table, key_pos)
            scores = jnp.where(visible, scores, NEG_FILL)
            new_top = jnp.maximum(top, jnp.max(scores, -1))
            weights = jnp.where(visible, jnp.exp(scores - new_top[..., None]), 0.0)
            factor = jnp.exp(top - new_top)
            total = total * factor + jnp.sum(weights, -1)
            accum = accum * factor[..., None] + jnp.einsum(
                "qhgk,khd->qhgd",
                weights.astype(jnp.bfloat16),
                value_row_table,
                preferred_element_type=jnp.float32,
            )
            return ((new_top, total, accum), None)

        start_state = (
            jnp.full((group_rows, key_value_heads, shared_portion), NEG_FILL, jnp.float32),
            jnp.zeros((group_rows, key_value_heads, shared_portion), jnp.float32),
            jnp.zeros((group_rows, key_value_heads, shared_portion, HEAD_SIZE), jnp.float32),
        )
        key_blocks = kv_all.reshape(blocks, group_rows, 2 * key_value_heads * HEAD_SIZE)
        pos_blocks = slot_position.reshape(blocks, group_rows)
        (top, total, accum), _ = lax.scan(forward_step, start_state, (key_blocks, pos_blocks))
        attn_full = accum / total[..., None]
        log_total = top + jnp.log(total)
        attn_tok = lax.all_to_all(
            attn_full.astype(jnp.bfloat16).reshape(group_rows, 1, q_heads * HEAD_SIZE),
            "head",
            split_axis=0,
            concat_axis=1,
            tiled=True,
        )
        attn_tok = attn_tok.reshape(token_rows, QUERY_HEADS * HEAD_SIZE)
        resid = x_rows + RESIDUAL_SCALE * matrix_product(attn_tok, w_o_all)
        xn2, inv_two, scaled_two = normalize(resid, gain_two)
        xn2_group = lax.all_gather(xn2.astype(jnp.bfloat16), "head", axis=0, tiled=True)
        gate_up = matrix_product(xn2_group, w_gate_up)
        gate_pre = gate_up[:, :local_ff]
        up_proj = gate_up[:, local_ff:]
        sigma = jax.nn.sigmoid(gate_pre)
        silu_gate = gate_pre * sigma
        hidden = (silu_gate * up_proj).astype(jnp.bfloat16)
        mlp_out = lax.psum_scatter(
            matrix_product(hidden, w_d_all).astype(jnp.bfloat16),
            "head",
            scatter_dimension=0,
            tiled=True,
        ).astype(jnp.float32)
        outputs.append((resid + RESIDUAL_SCALE * mlp_out).astype(jnp.bfloat16))
        upstream = cotangent[micro_idx].astype(jnp.float32)
        d_mlp = (RESIDUAL_SCALE * upstream).astype(jnp.bfloat16)
        shard_piece = lax.all_gather(d_mlp, "head", axis=0, tiled=True)
        down_acc = left_product(hidden, shard_piece)
        hidden_acc = right_product(shard_piece, w_d_all)
        d_silu = sigma * (1.0 + gate_pre * (1.0 - sigma))
        d_gate_up = jnp.concatenate(
            [hidden_acc * up_proj * d_silu, hidden_acc * silu_gate], 1
        ).astype(jnp.bfloat16)
        grad_gate_up = left_product(xn2_group, d_gate_up)
        d_xn2 = lax.psum_scatter(
            right_product(d_gate_up, w_gate_up).astype(jnp.bfloat16),
            "head",
            scatter_dimension=0,
            tiled=True,
        ).astype(jnp.float32)
        d_resid_two, grad_gain_two = norm_back(d_xn2, gain_two, inv_two, scaled_two)
        d_resid = upstream + d_resid_two
        d_branch = (RESIDUAL_SCALE * d_resid).astype(jnp.bfloat16)
        grad_out_mb = left_product(attn_tok, d_branch)
        d_attn = (
            right_product(d_branch, w_o_all)
            .astype(jnp.bfloat16)
            .reshape(token_rows, grouped_heads, q_heads * HEAD_SIZE)
        )
        d_group = lax.all_to_all(d_attn, "head", split_axis=1, concat_axis=0, tiled=True).reshape(
            group_rows, key_value_heads, shared_portion, HEAD_SIZE
        )
        delta = jnp.sum(d_group.astype(jnp.float32) * attn_full, -1)

        def cycle_step(turn_idx, running):
            dq_acc, dkv_acc = running
            source = (blk_index - turn_idx) % blocks
            kv_block = lax.dynamic_slice_in_dim(kv_all, source * group_rows, group_rows, 0)
            key_pos = lax.dynamic_slice_in_dim(slot_position, source * group_rows, group_rows)
            key_row_table, value_row_table = split_kv(kv_block)
            scores, visible = masked_scores(key_row_table, key_pos)
            prob_rows = jnp.exp(jnp.where(visible, scores - log_total[..., None], NEG_FILL))
            d_prob = jnp.einsum(
                "qhgd,khd->qhgk", d_group, value_row_table, preferred_element_type=jnp.float32
            )
            d_scores = (prob_rows * (d_prob - delta[..., None])).astype(jnp.bfloat16)
            dq_acc = dq_acc + SCORE_SCALE * jnp.einsum(
                "qhgk,khd->qhgd", d_scores, key_row_table, preferred_element_type=jnp.float32
            )
            d_keys = SCORE_SCALE * jnp.einsum(
                "qhgk,qhgd->khd", d_scores, q_group, preferred_element_type=jnp.float32
            )
            d_values = jnp.einsum(
                "qhgk,qhgd->khd",
                prob_rows.astype(jnp.bfloat16),
                d_group,
                preferred_element_type=jnp.float32,
            )
            dkv_acc = dkv_acc + jnp.concatenate(
                [
                    d_keys.reshape(group_rows, key_value_heads * HEAD_SIZE),
                    d_values.reshape(group_rows, key_value_heads * HEAD_SIZE),
                ],
                1,
            )
            return (
                dq_acc,
                from_behind(dkv_acc.astype(jnp.bfloat16), "blk", 1).astype(dkv_acc.dtype),
            )

        dq_group, dkv_group = lax.fori_loop(
            0,
            blocks,
            cycle_step,
            (
                jnp.zeros((group_rows, key_value_heads, shared_portion, HEAD_SIZE), jnp.float32),
                jnp.zeros((group_rows, 2 * key_value_heads * HEAD_SIZE), jnp.float32),
            ),
        )
        dq_tok, key_value_token_grad = (
            lax.all_to_all(
                dq_group.astype(jnp.bfloat16).reshape(group_rows, 1, q_heads * HEAD_SIZE),
                "head",
                split_axis=0,
                concat_axis=1,
                tiled=True,
            ),
            lax.all_to_all(
                dkv_group.astype(jnp.bfloat16).reshape(
                    group_rows, 1, 2 * key_value_heads * HEAD_SIZE
                ),
                "head",
                split_axis=0,
                concat_axis=1,
                tiled=True,
            ),
        )
        key_value_token_grad = key_value_token_grad.reshape(
            token_rows, grouped_heads, 2, key_value_heads * HEAD_SIZE
        )
        dq_raw = (
            rotary_back(
                dq_tok.reshape(token_rows, QUERY_HEADS, HEAD_SIZE).astype(jnp.float32), cosine, sine
            )
            .astype(jnp.bfloat16)
            .reshape(token_rows, QUERY_HEADS * HEAD_SIZE)
        )
        dk_raw = (
            rotary_back(
                key_value_token_grad[:, :, 0]
                .reshape(token_rows, KEY_VALUE_HEADS, HEAD_SIZE)
                .astype(jnp.float32),
                cosine,
                sine,
            )
            .astype(jnp.bfloat16)
            .reshape(token_rows, KEY_VALUE_HEADS * HEAD_SIZE)
        )
        value_token_grad = key_value_token_grad[:, :, 1].reshape(
            token_rows, KEY_VALUE_HEADS * HEAD_SIZE
        )
        d_xn1 = (
            right_product(dq_raw, w_q_all)
            + right_product(dk_raw, stacked_key_weight)
            + right_product(value_token_grad, w_v_all)
        )
        d_resid_one, grad_gain_one = norm_back(d_xn1, gain_one, inv_one, scaled_one)
        input_grads.append(d_resid + d_resid_one)
        local_attn = (
            grad_gain_one,
            grad_gain_two,
            left_product(first_normed_reduced, dq_raw),
            left_product(first_normed_reduced, dk_raw),
            left_product(first_normed_reduced, value_token_grad),
            grad_out_mb,
        )
        local_mlp = (grad_gate_up[:, :local_ff], grad_gate_up[:, local_ff:], down_acc)
        attn_acc = jax.tree.map(jnp.add, attn_acc, local_attn)
        mlp_acc = jax.tree.map(jnp.add, mlp_acc, local_mlp)
    attn_total = lax.psum_scatter(attn_acc, ("blk", "head"), scatter_dimension=0, tiled=True)
    mlp_total = (
        lax.psum_scatter(
            mlp_acc[0].astype(jnp.bfloat16), "blk", scatter_dimension=0, tiled=True
        ).astype(jnp.float32),
        lax.psum_scatter(
            mlp_acc[1].astype(jnp.bfloat16), "blk", scatter_dimension=0, tiled=True
        ).astype(jnp.float32),
        lax.psum_scatter(
            mlp_acc[2].astype(jnp.bfloat16), "blk", scatter_dimension=1, tiled=True
        ).astype(jnp.float32),
    )
    return (
        jnp.stack(outputs),
        jnp.stack(input_grads),
        attn_total[0],
        attn_total[1],
        attn_total[2],
        attn_total[3],
        attn_total[4],
        attn_total[5],
        mlp_total[0],
        mlp_total[1],
        mlp_total[2],
    )


def solution(mesh):
    placed = (
        P(None, ("blk", "head"), None),
        P(None, ("blk", "head"), None),
        P(),
        P(),
        P(("blk", "head")),
        P(("blk", "head")),
        P(("blk", "head"), None),
        P(("blk", "head"), None),
        P(("blk", "head"), None),
        P(("blk", "head"), None),
        P("blk", "head"),
        P("blk", "head"),
        P("head", "blk"),
    )
    return jax.shard_map(
        body,
        mesh=mesh,
        in_specs=placed,
        out_specs=(
            P(None, ("blk", "head"), None),
            P(None, ("blk", "head"), None),
            P(("blk", "head")),
            P(("blk", "head")),
            P(("blk", "head"), None),
            P(("blk", "head"), None),
            P(("blk", "head"), None),
            P(("blk", "head"), None),
            P("blk", "head"),
            P("blk", "head"),
            P("head", "blk"),
        ),
        check_vma=False,
    )
```

profile of v0, /device:TPU:0, one launch (start us, length us, event | category | flops | bytes accessed | tf_op | source)
XLA Modules:
  0.0 2084.1 jit_solution(14963035138271503412)
XLA Ops:
  11.2 42.1 %all-reduce.5 = (bf16[2048]{0:T(1024)(128)(2,1)S(1)}, bf16[2048]{0:T(1024)(128)(2,1)S(1)}) all-reduce(bf16[2048]{0:T(1024)(128)(2,1)S(1)} %dynamic-update-slice, bf16[2048]{0:T(1024)(128)(2,1)S(1)} %dynamic-update-slice.1), channel_id=1, replica_groups=mesh['blk'=8,'head'=4] {'blk','head'}, use_global_device_ids=true, to_apply=%add | all-reduce | flops 4096 | bytes 16384
  72.5 56.0 %all-gather.14.cloned.1.call-done = bf16[2048,512]{1,0:T(8,128)(2,1)} async-done(((bf16[64,512]{1,0:T(8,128)(2,1)}), bf16[2048,512]{1,0:T(8,128)(2,1)}) %all-gather.14.cloned.1.call-update) | async-done | bytes 2097168 | tf_op jit(solution)/shard_map/all_gather | solution.py:119
  143.9 63.9 %all-gather.20.cloned.1.call-done = bf16[2048,2048]{1,0:T(8,128)(2,1)} async-done(((bf16[64,2048]{1,0:T(8,128)(2,1)}), bf16[2048,2048]{1,0:T(8,128)(2,1)}) %all-gather.20.cloned.1.call-update) | async-done | bytes 8388624 | tf_op jit(solution)/shard_map/all_gather | solution.py:118
  240.8 28.5 %while.66 = (s32[]{:T(128)}, f32[256,2,4]{0,2,1:T(4,128)S(1)}, f32[256,2,4]{0,2,1:T(4,128)S(1)}, f32[256,2,4,64]{0,3,2,1:T(8,128)S(1)}, s32[8,256]{1,0:T(8,128)S...) while((s32[]{:T(128)}, f32[256,2,4]{0,2,1:T(4,128)S(1)}, ...), condition=%wide.region_4.5_spmd.clone, body=%wide.region_1.4_spmd.clone.sunk | while | flops 141568256 | bytes 8917645 | solution.py:219
  284.2 27.9 %all-gather.22.cloned.1.call-done = bf16[2048,2048]{1,0:T(8,128)(2,1)} async-done(((bf16[64,2048]{1,0:T(8,128)(2,1)}), bf16[2048,2048]{1,0:T(8,128)(2,1)}) %all-gather.22.cloned.1.call-update) | async-done | bytes 8388624 | tf_op jit(solution)/shard_map/all_gather | solution.py:121
  334.9 31.9 %all-gather.26.cloned.1.call-done = bf16[2048,2048]{1,0:T(8,128)(2,1)} async-done(((bf16[256,2048]{1,0:T(8,128)(2,1)}), bf16[2048,2048]{1,0:T(8,128)(2,1)}) %all-gather.26.cloned.1.call-update) | async-done | bytes 8388624 | tf_op jit(solution)/shard_map/all_gather | solution.py:126
  387.7 35.5 %all-gather.28.cloned.1.call-done = bf16[2048,2048]{1,0:T(8,128)(2,1)} async-done(((bf16[256,2048]{1,0:T(8,128)(2,1)}), bf16[2048,2048]{1,0:T(8,128)(2,1)}) %all-gather.28.cloned.1.call-update) | async-done | bytes 8388624 | tf_op jit(solution)/shard_map/all_gather | solution.py:127
  432.1 21.2 %all-gather.24.cloned.1.call-done = bf16[256,2048]{1,0:T(8,128)(2,1)} async-done(((bf16[64,2048]{1,0:T(8,128)(2,1)}), bf16[256,2048]{1,0:T(8,128)(2,1)}) %all-gather.24.cloned.1.call-update) | async-done | bytes 1048592 | tf_op jit(solution)/shard_map/all_gather | solution.py:232
  465.9 16.9 all-gather.36.cloned.1.call-done
  482.9 57.2 %all-gather.30.cloned.1.call-done = bf16[2048,2048]{1,0:T(8,128)(2,1)} async-done(((bf16[2048,256]{1,0:T(8,128)(2,1)}), bf16[2048,2048]{1,0:T(8,128)(2,1)}) %all-gather.30.cloned.1.call-update) | async-done | bytes 8388624 | tf_op jit(solution)/shard_map/all_gather | solution.py:128
  549.6 22.8 %convolution_convert_fusion.1 = bf16[256,2048]{1,0:T(8,128)(2,1)} fusion(bf16[2048,4096]{1,0:T(8,128)(2,1)} %constant_dynamic-update-slice_fusion, bf16[256,2048]{1,0:T(8,128)(2,1)} %get-tuple-element.1240, bf16[256,2048]{1,0:T(8,128)(2,1)} %get-tuple-element.1239), kind=kOutput, calls=%fused_computation.92 | convolution fusion | flops 4299685888 | bytes 19922944 | tf_op jit(solution)/shard_map/dot_general | solution.py:36
  572.5 29.5 %while.67 = (s32[]{:T(128)}, f32[256,2,4]{0,2,1:T(4,128)S(1)}, f32[256,2,4]{0,2,1:T(4,128)S(1)}, f32[256,2,4,64]{0,3,2,1:T(8,128)S(1)}, s32[8,256]{1,0:T(8,128)S...) while((s32[]{:T(128)}, f32[256,2,4]{0,2,1:T(4,128)S(1)}, ...), condition=%wide.region_11.12_spmd.clone, body=%wide.region_8.11_spmd.clone.sunk | while | flops 141568256 | bytes 8917645 | solution.py:219
  603.2 13.7 all_to_all.169
  626.1 25.6 %all-gather.34.cloned.1.call-done = bf16[256,2048]{1,0:T(8,128)(2,1)} async-done(((bf16[64,2048]{1,0:T(8,128)(2,1)}), bf16[256,2048]{1,0:T(8,128)(2,1)}) %all-gather.34.cloned.1.call-update) | async-done | bytes 1048592 | tf_op jit(solution)/shard_map/all_gather | solution.py:232
  664.4 16.3 all-gather.38.cloned.1.call-done
  737.3 15.0 fusion.53
  752.2 13.4 fusion.52
  765.7 28.7 %fusion.46 = (bf16[2048,2048]{1,0:T(8,128)(2,1)}, bf16[2048,2048]{1,0:T(8,128)(2,1)}) fusion(f32[2048,4096]{1,0:T(8,128)} %fusion.52, f32[2048,4096]{1,0:T(8,128)} %fusion.53), kind=kLoop, calls=%fused_computation.83 | loop fusion | flops 16777216 | bytes 83886080 | tf_op jit(solution)/shard_map/convert_element_type | solution.py:387
  829.6 95.2 %while.69 = (s32[]{:T(128)}, f32[256,2,4,64]{0,3,2,1:T(8,128)S(1)}, f32[256,256]{0,1:T(8,128)S(1)}, s32[]{:T(128)}, bf16[2048,256]{1,0:T(8,128)(2,1)}, /*index=5...) while((s32[]{:T(128)}, f32[256,2,4,64]{0,3,2,1:T(8,128)S(1)}, ...), condition=%wide.region_24.25_spmd.clone, body=%wide.region_23.24_spmd.clone.sunk | while | flops 340099328 | bytes 14242723 | solution.py:312
  933.1 93.7 %while.68 = (s32[]{:T(128)}, f32[256,2,4,64]{0,3,2,1:T(8,128)S(1)}, f32[256,256]{0,1:T(8,128)S(1)}, s32[]{:T(128)}, bf16[2048,256]{1,0:T(8,128)(2,1)}, /*index=5...) while((s32[]{:T(128)}, f32[256,2,4,64]{0,3,2,1:T(8,128)S(1)}, ...), condition=%wide.region_18.19_spmd.clone, body=%wide.region_17.18_spmd.clone.sunk | while | flops 340099328 | bytes 14242723 | solution.py:312
  1141.4 41.7 %all-reduce.4 = (f32[2048]{0:T(1024)S(1)}, f32[2048]{0:T(1024)S(1)}) all-reduce(f32[2048]{0:T(1024)S(1)} %add.333, f32[2048]{0:T(1024)S(1)} %add.334), channel_id=6, replica_groups=mesh['blk'=8,'head'=4] {'blk','head'}, use_global_device_ids=true, to_apply=%region_28.29.clone | all-reduce | flops 4096 | bytes 32768
  1195.4 150.2 %reduce-scatter.24.cloned.1.call-done = f32[64,512]{1,0:T(8,128)} async-done(((f32[2048,512]{1,0:T(8,128)}), f32[64,512]{1,0:T(8,128)}) %reduce-scatter.24.cloned.1.call-update) | async-done | bytes 131088 | tf_op jit(solution)/shard_map/reduce_scatter | solution.py:381
  1345.6 366.2 %reduce-scatter.26.cloned.1.call-done = f32[64,2048]{1,0:T(8,128)} async-done(((f32[2048,2048]{1,0:T(8,128)}), f32[64,2048]{1,0:T(8,128)}) %reduce-scatter.26.cloned.1.call-update) | async-done | bytes 524304 | tf_op jit(solution)/shard_map/reduce_scatter | solution.py:381
  1711.8 365.0 %reduce-scatter.20.cloned.1.call-done = f32[64,2048]{1,0:T(8,128)} async-done(((f32[2048,2048]{1,0:T(8,128)}), f32[64,2048]{1,0:T(8,128)}) %reduce-scatter.20.cloned.1.call-update) | async-done | bytes 524304 | tf_op jit(solution)/shard_map/reduce_scatter | solution.py:381
  (825 shorter events, 653.5 us)
Async XLA Ops:
  7.9 120.7 %all-gather.14.cloned.1.call-start = ((), (), s32[]{:S(2)}) async-start(), calls=%async_computation.23 | async-start | bytes 2162688 | tf_op jit(solution)/shard_map/all_gather | solution.py:119
  8.7 199.1 %all-gather.20.cloned.1.call-start = ((), (), s32[]{:S(2)}) async-start(), calls=%async_computation.26 | async-start | bytes 8650752 | tf_op jit(solution)/shard_map/all_gather | solution.py:118
  9.4 231.4 %all-gather.18.cloned.1.call-start = ((), (), s32[]{:S(2)}) async-start(), calls=%async_computation.25 | async-start | bytes 1179648 | tf_op jit(solution)/shard_map/all_gather | solution.py:174
  142.7 169.4 %all-gather.22.cloned.1.call-start = ((), (), s32[]{:S(2)}) async-start(), calls=%async_computation.27 | async-start | bytes 8650752 | tf_op jit(solution)/shard_map/all_gather | solution.py:121
  143.3 223.6 %all-gather.26.cloned.1.call-start = ((), (), s32[]{:S(2)}) async-start(), calls=%async_computation.29 | async-start | bytes 9437184 | tf_op jit(solution)/shard_map/all_gather | solution.py:126
  230.6 192.5 %all-gather.28.cloned.1.call-start = ((), (), s32[]{:S(2)}) async-start(), calls=%async_computation.30 | async-start | bytes 9437184 | tf_op jit(solution)/shard_map/all_gather | solution.py:127
  275.3 177.9 %all-gather.24.cloned.1.call-start = ((), (), s32[]{:S(2)}) async-start(), calls=%async_computation.28 | async-start | bytes 1310720 | tf_op jit(solution)/shard_map/all_gather | solution.py:232
  318.1 164.8 %all-gather.36.cloned.1.call-start = ((), (), s32[]{:S(2)}) async-start(), calls=%async_computation.36 | async-start | bytes 1310720 | tf_op jit(solution)/shard_map/all_gather | solution.py:248
  320.4 219.7 %all-gather.30.cloned.1.call-start = ((), (), s32[]{:S(2)}) async-start(), calls=%async_computation.31 | async-start | bytes 9437184 | tf_op jit(solution)/shard_map/all_gather | solution.py:128
  327.8 244.6 %all-gather.32.cloned.1.call-start = ((), (), s32[]{:S(2)}) async-start(), calls=%async_computation.33 | async-start | bytes 1179648 | tf_op jit(solution)/shard_map/all_gather | solution.py:174
  387.7 235.1 %reduce-scatter.16.cloned.1.call-start = ((), (), s32[]{:S(2)}) async-start(), calls=%async_computation.37 | async-start | bytes 1310720 | tf_op jit(solution)/shard_map/reduce_scatter | solution.py:256
  572.4 79.3 %all-gather.34.cloned.1.call-start = ((), (), s32[]{:S(2)}) async-start(), calls=%async_computation.34 | async-start | bytes 1310720 | tf_op jit(solution)/shard_map/all_gather | solution.py:232
  626.1 170.3 %reduce-scatter.18.cloned.1.call-start = ((), (), s32[]{:S(2)}) async-start(), calls=%async_computation.39 | async-start | bytes 1310720 | tf_op jit(solution)/shard_map/reduce_scatter | solution.py:256
  701.9 97.3 %reduce-scatter.12.cloned.1.call-start = ((), (), s32[]{:S(2)}) async-start(), calls=%async_computation.32 | async-start | bytes 1310720 | tf_op jit(solution)/shard_map/reduce_scatter | solution.py:239
  708.9 90.4 %reduce-scatter.14.cloned.1.call-start = ((), (), s32[]{:S(2)}) async-start(), calls=%async_computation.35 | async-start | bytes 1310720 | tf_op jit(solution)/shard_map/reduce_scatter | solution.py:239
  716.1 469.6 %reduce-scatter.32.cloned.1.call-start = ((), (), s32[]{:S(2)}) async-start(), calls=%async_computation.46 | async-start | bytes 9437184 | tf_op jit(solution)/shard_map/reduce_scatter | solution.py:389
  736.1 452.3 %reduce-scatter.28.cloned.1.call-start = ((), (), s32[]{:S(2)}) async-start(), calls=%async_computation.44 | async-start | bytes 9437184 | tf_op jit(solution)/shard_map/reduce_scatter | solution.py:383
  794.4 396.8 %reduce-scatter.30.cloned.1.call-start = ((), (), s32[]{:S(2)}) async-start(), calls=%async_computation.45 | async-start | bytes 9437184 | tf_op jit(solution)/shard_map/reduce_scatter | solution.py:386
  822.4 103.9 %all-to-all-start.6 = ((bf16[64,4,512]{2,0,1:T(8,128)(2,1)}), bf16[64,4,512]{2,0,1:T(8,128)(2,1)S(1)}, u32[]{:S(2)}, u32[]{:S(2)}) async-start(bf16[64,4,512]{2,0,1:T(8,128)(2,1)} %bitcast.489), calls=%async_computation.9 | async-start | bytes 524288 | tf_op jit(solution)/shard_map/all_to_all | solution.py:271
  926.3 102.0 %all-to-all-start.11 = ((bf16[4,2,8192]{2,1,0:T(2,128)(2,1)}), bf16[4,2,8192]{2,1,0:T(2,128)(2,1)S(1)}, u32[]{:S(2)}, u32[]{:S(2)}) async-start(bf16[4,2,8192]{2,1,0:T(2,128)(2,1)} %reshape.903), calls=%async_computation.15 | async-start | bytes 262144 | tf_op jit(solution)/shard_map/all_to_all | solution.py:329
  1033.2 162.2 %reduce-scatter.22.cloned.1.call-start = ((), (), s32[]{:S(2)}) async-start(), calls=%async_computation.41 | async-start | bytes 4325376 | tf_op jit(solution)/shard_map/reduce_scatter | solution.py:381
  1045.8 299.8 %reduce-scatter.24.cloned.1.call-start = ((), (), s32[]{:S(2)}) async-start(), calls=%async_computation.42 | async-start | bytes 4325376 | tf_op jit(solution)/shard_map/reduce_scatter | solution.py:381
  1050.6 661.2 %reduce-scatter.26.cloned.1.call-start = ((), (), s32[]{:S(2)}) async-start(), calls=%async_computation.43 | async-start | bytes 17301504 | tf_op jit(solution)/shard_map/reduce_scatter | solution.py:381
  1082.6 994.3 %reduce-scatter.20.cloned.1.call-start = ((), (), s32[]{:S(2)}) async-start(), calls=%async_computation.40 | async-start | bytes 17301504 | tf_op jit(solution)/shard_map/reduce_scatter | solution.py:381
  (100 other events, 2092.8 us)
Sparse Core Ops, SparseCore 0:
  10.9 59.3 all-gather.15
  73.2 55.3 all-gather.13
  131.5 76.2 all-gather.19
  209.5 22.0 all-gather.17
  234.4 77.6 all-gather.21
  313.8 52.9 all-gather.25
  368.7 54.3 all-gather.27
  425.3 27.9 all-gather.23
  455.4 27.4 all-gather.35
  484.6 55.4 all-gather.29
  542.6 23.4 all-gather.31
  572.5 27.1 reduce-scatter.15
  625.6 26.0 all-gather.33
  653.2 27.4 all-gather.37
  702.0 26.6 reduce-scatter.17
  730.9 25.7 reduce-scatter.11
  759.5 25.7 reduce-scatter.13
  788.7 71.3 reduce-scatter.31
  863.9 73.9 reduce-scatter.27
  941.2 75.5 reduce-scatter.29
  1045.9 149.4 reduce-scatter.21
  1198.3 147.2 reduce-scatter.23
  1348.6 363.1 reduce-scatter.25
  1714.6 362.1 reduce-scatter.19
where the time goes:
time: 2100 us; the launch traced here: 2080 us
  waiting for transfers between devices  1400 us (67%)
  matrix products  292 us (14%)
  other arithmetic  115 us (5%)
  local copies, waits for them, and re-layouts  110 us (5%)
  blocking collectives  107 us (5%)
  starting transfers between devices  41.5 us (2%)
    reduce_scatter x4, waiting for transfers between devices, body(): lax.psum_scatter(attn_acc, ('blk', 'head'), scatter_dimension=0, tiled=True)  883 us
    ppermute x16, waiting for transfers between devices, from_behind(): lax.ppermute(x, axis, [(i, (i + by) % devices) for i in range(devices)])  95.3 us
    unnamed x2, blocking collectives  83.8 us
    dot_general x12, matrix products, right_product(): lax.dot_general(left, right, (((1,), (1,)), ((), ())), preferred_element_...  82.3 us
    dot_general x12, matrix products, left_product(): lax.dot_general(left, right, (((0,), (0,)), ((), ())), preferred_element_...  77 us
    dot_general x12, matrix products, matrix_product(): return jnp.dot(left, right, preferred_element_type=jnp.float32)  66.2 us
    all_gather x1, waiting for transfers between devices, body(): lax.all_gather(w_query, ('blk', 'head'), axis=0, tiled=True)  63.9 us
    all_gather x1, waiting for transfers between devices, body(): lax.all_gather(w_down, 'blk', axis=1, tiled=True)  57.2 us
  transfers between devices with their start and end apart: 50, of which 38 were waited for; matrix products, arithmetic and copies ran while one was open for 23% of the time, Pallas kernels for 0%

commit v1 on v0

v1 whole, which is shorter than its diff:
```python
import functools

import jax
import jax.numpy as jnp
from jax import lax
from jax.experimental import pallas as pl
from jax.experimental.pallas import tpu as pltpu
from jax.sharding import PartitionSpec as P

MODEL_WIDTH = 2048
QUERY_HEADS = 32
KEY_VALUE_HEADS = 8
HEAD_SIZE = 64
SHARED = QUERY_HEADS // KEY_VALUE_HEADS
MICRO = 2

SCORE_SCALE = 0.015625
RESIDUAL_SCALE = 0.22
EPSILON = 1e-06
ROPE_BASE = 10000000.0
NEG_FILL = -1e30

BF = jnp.bfloat16
F32 = jnp.float32
VMEM_LIMIT = 56 * 1024 * 1024


def dot(left, right, contract):
    return lax.dot_general(left, right, (contract, ((), ())), preferred_element_type=F32)


def nn(left, right):
    return dot(left, right, ((1,), (0,)))


def tn(left, right):
    return dot(left, right, ((0,), (0,)))


def nt(left, right):
    return dot(left, right, ((1,), (1,)))


def swap(x, bit, devices):
    return lax.ppermute(x, "blk", [(i, i ^ bit) for i in range(devices)])


def xor_gather(x, devices):
    if devices == 8:
        half = x.shape[0] // 2
        r2 = swap(x, 2, devices)
        r4 = swap(x, 4, devices)
        top = swap(r2[:half], 4, devices)
        low = swap(r4[half:], 2, devices)
        even = jnp.concatenate([x, r2, r4, top, low], 0)
        odd = swap(even, 1, devices)
        rows = x.shape[0]
        found = [None] * 8
        for place, j in enumerate((0, 2, 4, 6)):
            found[j] = even[place * rows : (place + 1) * rows]
            found[j ^ 1] = odd[place * rows : (place + 1) * rows]
        return found
    found = {0: x}
    bit = devices // 2
    while bit:
        order = sorted(found)
        came = swap(jnp.stack([found[j] for j in order]), bit, devices)
        for place, j in enumerate(order):
            found[j ^ bit] = came[place]
        bit //= 2
    return [found[j] for j in range(devices)]


def natural(found, me, axis):
    block = found[0].shape[axis]
    shape = list(found[0].shape)
    shape[axis] = block * len(found)
    whole = jnp.zeros(shape, found[0].dtype)
    for j, piece in enumerate(found):
        whole = lax.dynamic_update_slice_in_dim(whole, piece, (me ^ j) * block, axis)
    return whole


def add(left, right):
    return (left.astype(F32) + right.astype(F32)).astype(BF)


def xor_scatter(make, devices):
    if devices == 8:
        odd = [make(j) for j in (1, 3, 5, 7)]
        came = swap(jnp.stack(odd), 1, devices)
        even = [add(make(j), came[place]) for place, j in enumerate((0, 2, 4, 6))]
        h0, h2, h4, h6 = even
        half = h0.shape[0] // 2
        from_x = swap(h6[:half], 2, devices)
        from_y = swap(h6[half:], 4, devices)
        h4 = jnp.concatenate([add(h4[:half], from_x), h4[half:]], 0)
        h2 = jnp.concatenate([h2[:half], add(h2[half:], from_y)], 0)
        came_x = swap(h2, 2, devices)
        came_y = swap(h4, 4, devices)
        return h0.astype(F32) + came_x.astype(F32) + came_y.astype(F32)
    held = {j: make(j) for j in range(devices)}
    bit = 1
    while bit < devices:
        away = sorted(j for j in held if j & bit)
        came = swap(jnp.stack([held.pop(j) for j in away]), bit, devices)
        for place, j in enumerate(away):
            held[j ^ bit] = add(held[j ^ bit], came[place])
        bit *= 2
    return held[0].astype(F32)


def run_offset(index, run, tile, half):
    if run == 0:
        return index
    return (tile - half) - (index // half) * half + index % half


def tile_place(t, blocks):
    late = t >= blocks
    return jnp.where(late, 2 * blocks - 1 - t, t), jnp.where(late, 1, 0)


def tile_mask(t, own, length, run, tile, rows, half, blocks):
    key_row = lax.broadcasted_iota(jnp.int32, (tile, 1), 0)
    key_pos = t * tile + jnp.where(
        t >= blocks, run_offset(key_row, 1, tile, half), run_offset(key_row, 0, tile, half)
    )
    query_pos = own * tile + run_offset(
        lax.broadcasted_iota(jnp.int32, (1, rows), 1) % tile, run, tile, half
    )
    key_pos = jnp.where(key_pos < length, key_pos, jnp.int32(1 << 30))
    return key_pos <= query_pos


def own_tiles(scalars, run, tile, blocks):
    micro = pl.program_id(0)
    mine = scalars[0]
    length = scalars[1 + micro]
    own = mine if run == 0 else 2 * blocks - 1 - mine
    count = jnp.minimum(own + 1, (length + tile - 1) // tile)
    return own, length, count


def head_part(values, head, heads):
    if heads == 1:
        return values
    lane = lax.broadcasted_iota(jnp.int32, values.shape, 1) // HEAD_SIZE
    return jnp.where(lane == head, values, jnp.zeros_like(values))


def fold_rows(values, combine):
    rows, lanes = values.shape
    return combine(values.reshape(rows // 8, 8, lanes), axis=0)


def forward_kernel(scalars, q_ref, kv_ref, o_ref, lse_ref, s_ref, *, blocks, tile, half, heads):
    width = heads * HEAD_SIZE
    rows = q_ref.shape[2]
    for run in range(2):
        own, length, count = own_tiles(scalars, run, tile, blocks)
        done = jnp.zeros((rows, width), F32)
        for head in range(heads):
            q = head_part(q_ref[0, run], head, heads)

            def scores(t, top, q=q, own=own, length=length, run=run):
                place, late = tile_place(t, blocks)
                s = nt(kv_ref[place, 0, late, :, :width], q)
                s = jnp.where(
                    tile_mask(t, own, length, run, tile, rows, half, blocks), s, NEG_FILL
                )
                s_ref[t] = s
                return jnp.maximum(top, fold_rows(s, jnp.max))

            top = lax.fori_loop(0, count, scores, jnp.full((8, rows), NEG_FILL, F32))
            top = jnp.max(top, 0, keepdims=True)

            def mix(t, held, top=top):
                total, acc = held
                place, late = tile_place(t, blocks)
                p = jnp.exp(s_ref[t] - top)
                v = kv_ref[place, 0, late, :, width:]
                return total + fold_rows(p, jnp.sum), acc + tn(v, p.astype(BF))

            total, acc = lax.fori_loop(
                0, count, mix, (jnp.zeros((8, rows), F32), jnp.zeros((width, rows), F32))
            )
            total = jnp.sum(total, 0, keepdims=True)
            lse_ref[0, run, head] = top + jnp.log(total)
            done = done + head_part((acc / total).T, head, heads)
        o_ref[0, run] = done.astype(BF)


def backward_kernel(
    scalars, q_ref, kv_ref, do_ref, lse_ref, delta_ref, dq_ref, dkv_ref, acc_ref, *, blocks, tile, half, heads
):
    width = heads * HEAD_SIZE
    rows = q_ref.shape[2]
    acc_ref[...] = jnp.zeros(acc_ref.shape, F32)
    for run in range(2):
        own, length, count = own_tiles(scalars, run, tile, blocks)
        done = jnp.zeros((rows, width), F32)
        for head in range(heads):
            q = head_part(q_ref[0, run], head, heads)
            do = head_part(do_ref[0, run], head, heads)
            lse = lse_ref[0, run, head]
            delta = delta_ref[0, run, head]

            def step(t, dq, q=q, do=do, lse=lse, delta=delta, own=own, length=length, run=run):
                place, late = tile_place(t, blocks)
                k = kv_ref[place, 0, late, :, :width]
                v = kv_ref[place, 0, late, :, width:]
                s = nt(k, q)
                seen = tile_mask(t, own, length, run, tile, rows, half, blocks)
                p = jnp.where(seen, jnp.exp(jnp.where(seen, s - lse, NEG_FILL)), 0.0)
                ds = (p * (nt(v, do) - delta)).astype(BF)
                acc_ref[t, :, :width] += nn(ds, q)
                acc_ref[t, :, width:] += nn(p.astype(BF), do)
                return dq + tn(k, ds)

            dq = lax.fori_loop(0, count, step, jnp.zeros((width, rows), F32))
            done = done + head_part(dq.T, head, heads)
        dq_ref[0, run] = (SCORE_SCALE * done).astype(BF)
    for t in range(2 * blocks):
        place, late = (t, 0) if t < blocks else (2 * blocks - 1 - t, 1)
        dkv_ref[place, 0, late] = acc_ref[t].astype(BF)


def attention_specs(q, kv, heads):
    micros, _, rows, width = q.shape
    blocks, _, _, tile, _ = kv.shape
    per_q = pl.BlockSpec((1, 2, rows, width), lambda m, s: (m, 0, 0, 0))
    per_kv = pl.BlockSpec((blocks, 1, 2, tile, 2 * width), lambda m, s: (0, m, 0, 0, 0))
    per_row = pl.BlockSpec((1, 2, heads, 1, rows), lambda m, s: (m, 0, 0, 0, 0))
    return per_q, per_kv, per_row


def attention_forward(scalars, q, kv, heads, half):
    micros, _, rows, width = q.shape
    blocks, _, _, tile, _ = kv.shape
    per_q, per_kv, per_row = attention_specs(q, kv, heads)
    return pl.pallas_call(
        functools.partial(forward_kernel, blocks=blocks, tile=tile, half=half, heads=heads),
        grid_spec=pltpu.PrefetchScalarGridSpec(
            num_scalar_prefetch=1,
            grid=(micros,),
            in_specs=[per_q, per_kv],
            out_specs=[per_q, per_row],
            scratch_shapes=[pltpu.VMEM((2 * blocks, tile, rows), F32)],
        ),
        out_shape=[
            jax.ShapeDtypeStruct(q.shape, BF),
            jax.ShapeDtypeStruct((micros, 2, heads, 1, rows), F32),
        ],
        compiler_params=pltpu.CompilerParams(vmem_limit_bytes=VMEM_LIMIT),
        cost_estimate=pl.CostEstimate(
            flops=4 * micros * blocks * tile * rows * width * heads,
            bytes_accessed=2 * (q.size * 2 + kv.size),
            transcendentals=micros * blocks * tile * rows * heads,
        ),
    )(scalars, q, kv)


def attention_backward(scalars, q, kv, do, lse, delta, heads, half):
    micros, _, rows, width = q.shape
    blocks, _, _, tile, _ = kv.shape
    per_q, per_kv, per_row = attention_specs(q, kv, heads)
    return pl.pallas_call(
        functools.partial(backward_kernel, blocks=blocks, tile=tile, half=half, heads=heads),
        grid_spec=pltpu.PrefetchScalarGridSpec(
            num_scalar_prefetch=1,
            grid=(micros,),
            in_specs=[per_q, per_kv, per_q, per_row, per_row],
            out_specs=[per_q, per_kv],
            scratch_shapes=[pltpu.VMEM((2 * blocks, tile, 2 * width), F32)],
        ),
        out_shape=[
            jax.ShapeDtypeStruct(q.shape, BF),
            jax.ShapeDtypeStruct(kv.shape, BF),
        ],
        compiler_params=pltpu.CompilerParams(vmem_limit_bytes=VMEM_LIMIT),
        cost_estimate=pl.CostEstimate(
            flops=10 * micros * blocks * tile * rows * width * heads,
            bytes_accessed=2 * (q.size * 3 + kv.size * 2),
            transcendentals=micros * blocks * tile * rows * heads,
        ),
    )(scalars, q, kv, do, lse, delta)


def norm_parts(values):
    inverse = lax.rsqrt(jnp.mean(values * values, -1, keepdims=True) + EPSILON)
    return inverse, values * inverse


def norm_back(upstream, gain, inverse, scaled):
    through = upstream * gain
    inner = jnp.mean(through * scaled, -1, keepdims=True)
    return inverse * (through - scaled * inner)


def rotary_tables(positions):
    half_dim = HEAD_SIZE // 2
    frequency = ROPE_BASE ** (-(jnp.arange(half_dim).astype(F32) * 2.0) / HEAD_SIZE)
    angles = positions.astype(F32)[:, None] * frequency[None, :]
    angles = jnp.concatenate([angles, angles], -1)
    return jnp.cos(angles)[:, None, :], jnp.sin(angles)[:, None, :]


def rotate(values):
    half_dim = values.shape[-1] // 2
    return jnp.concatenate([-values[..., half_dim:], values[..., :half_dim]], -1)


def body(
    inputs,
    cotangent,
    lengths,
    positions,
    attn_gain,
    mlp_gain,
    w_query,
    key_projection,
    value_projection,
    w_out,
    w_gate,
    w_up,
    w_down,
):
    B = lax.axis_size("blk")
    H = lax.axis_size("head")
    me = lax.axis_index("blk")
    mine = lax.axis_index("head")
    T = inputs.shape[1]
    D = MODEL_WIDTH
    half = T // 2
    slots = T * H * B
    tile = H * half
    heads = KEY_VALUE_HEADS // H
    KD = heads * HEAD_SIZE
    QD = KD * SHARED
    tokens = MICRO * T
    group = H * tokens
    wrows = w_query.shape[0]
    F = w_gate.shape[1]
    block = D // B

    def by_group(w):
        return w.reshape(wrows, H, w.shape[1] // H).transpose(1, 0, 2)

    gains = jnp.zeros((wrows, 128), BF)
    gains = gains.at[:, 0].set(attn_gain).at[:, 1].set(mlp_gain)
    pack = jnp.concatenate(
        [
            by_group(w_query),
            by_group(key_projection),
            by_group(value_projection),
            jnp.broadcast_to(gains[None], (H, wrows, 128)),
        ],
        2,
    )
    pack = lax.all_to_all(pack, "head", split_axis=0, concat_axis=0, tiled=True)
    pack = pack.reshape(H * wrows, QD + 2 * KD + 128)
    qkvg = natural(xor_gather(pack, B), me, 0)
    w_qkv = qkvg[:, : QD + 2 * KD]
    gain_cols = qkvg[:, QD + 2 * KD : QD + 2 * KD + 2].astype(F32).T
    gain_one = gain_cols[0]
    gain_two = gain_cols[1]

    linear = me * H + mine
    my_pos = lax.dynamic_slice_in_dim(positions, linear * T, T, axis=1)
    place = jnp.where(
        my_pos < slots // 2, my_pos - half * linear, half + my_pos - (slots - half * (linear + 1))
    )
    order = (place[:, None, :] == jnp.arange(T)[None, :, None]).astype(BF)
    x_own = jnp.einsum("mrs,msd->mrd", order, inputs, preferred_element_type=F32)
    x_own = x_own.astype(BF).reshape(tokens, D)
    upstream = jnp.einsum("mrs,msd->mrd", order, cotangent, preferred_element_type=F32)
    upstream = upstream.reshape(tokens, D)
    x_group = lax.all_gather(x_own, "head", axis=0, tiled=True).astype(F32)
    d_mlp = (RESIDUAL_SCALE * upstream).astype(BF)

    w_out_rows = lax.all_gather(w_out, "head", axis=0, tiled=True)
    w_gate_up = natural(xor_gather(jnp.concatenate([w_gate, w_up], 1), B), me, 0)
    w_o = natural(xor_gather(w_out_rows, B), me, 0)
    w_d = natural(xor_gather(w_down, B), me, 1)

    inv_one, scaled_one = norm_parts(x_group)
    xn1 = (scaled_one * gain_one).astype(BF)
    qkv = nn(xn1, w_qkv)
    run_start = jnp.arange(H)[:, None, None] + me * H
    i = jnp.arange(half)[None, None, :]
    group_pos = jnp.concatenate(
        [half * run_start + i, slots - half * (run_start + 1) + i], 1
    )
    group_pos = jnp.broadcast_to(group_pos[:, None], (H, MICRO, 2, half)).reshape(group)
    cosine, sine = rotary_tables(group_pos)

    def rope(values, width):
        values = values.reshape(group, width // HEAD_SIZE, HEAD_SIZE)
        return values * cosine + rotate(values) * sine

    def rope_back(values, width):
        values = values.astype(F32).reshape(group, width // HEAD_SIZE, HEAD_SIZE)
        return (values * cosine - rotate(values) * sine).astype(BF).reshape(group, width)

    def to_heads(values):
        values = values.reshape(H, MICRO, 2, half, heads, SHARED, HEAD_SIZE)
        return values.transpose(1, 2, 5, 0, 3, 4, 6).reshape(MICRO, 2, SHARED * tile, KD)

    def from_heads(values):
        values = values.reshape(MICRO, 2, SHARED, H, half, heads, HEAD_SIZE)
        return values.transpose(3, 0, 1, 4, 5, 2, 6).reshape(group, QD)

    def to_tiles(values):
        return values.reshape(H, MICRO, 2, half, -1).transpose(1, 2, 0, 3, 4).reshape(
            MICRO, 2, tile, -1
        )

    def from_tiles(values):
        return values.reshape(MICRO, 2, H, half, -1).transpose(2, 0, 1, 3, 4).reshape(group, -1)

    q = to_heads((SCORE_SCALE * rope(qkv[:, :QD], QD).astype(BF)).astype(BF))
    k = rope(qkv[:, QD : QD + KD], KD).astype(BF).reshape(group, KD)
    v = qkv[:, QD + KD :].astype(BF)
    kv = lax.all_gather(to_tiles(jnp.concatenate([k, v], 1)), "blk", axis=0)
    scalars = jnp.concatenate([me[None].astype(jnp.int32), lengths.astype(jnp.int32)])
    o_heads, lse = attention_forward(scalars, q, kv, heads, half)
    o = from_heads(o_heads)
    o_full = lax.all_gather(o, "head", axis=1, tiled=True)

    resid = x_group + RESIDUAL_SCALE * nn(o_full, w_o)
    inv_two, scaled_two = norm_parts(resid)
    xn2 = (scaled_two * gain_two).astype(BF)
    dmo = lax.all_gather(d_mlp, "head", axis=0, tiled=True)
    gate_up = nn(xn2, w_gate_up)
    gate = gate_up[:, :F]
    up = gate_up[:, F:]
    sigma = jax.nn.sigmoid(gate)
    silu = gate * sigma
    hidden = (silu * up).astype(BF)
    d_hidden = nt(dmo, w_d)
    d_gate_up = jnp.concatenate(
        [d_hidden * up * (sigma * (1.0 + gate * (1.0 - sigma))), d_hidden * silu], 1
    ).astype(BF)
    d_xn2 = lax.psum_scatter(
        nt(d_gate_up, w_gate_up).astype(BF), "head", scatter_dimension=0, tiled=True
    ).astype(F32)
    mlp_out = lax.psum_scatter(
        nn(hidden, w_d).astype(BF), "head", scatter_dimension=0, tiled=True
    ).astype(F32)

    def columns(values, j):
        return lax.dynamic_slice_in_dim(values, (me ^ j) * block, block, 1)

    grad_gate_up = xor_scatter(lambda j: tn(columns(xn2, j), d_gate_up).astype(BF), B)
    grad_down = xor_scatter(lambda j: tn(hidden, columns(dmo, j)).astype(BF), B)

    def own(values):
        return lax.dynamic_slice_in_dim(values, mine * tokens, tokens, 0)

    resid_own = own(resid)
    scaled_two_own = own(scaled_two)
    grad_gain_two = jnp.sum(d_xn2 * scaled_two_own, 0)
    d_resid = upstream + norm_back(d_xn2, gain_two, own(inv_two), scaled_two_own)
    d_branch = (RESIDUAL_SCALE * d_resid).astype(BF)
    output = (resid_own + RESIDUAL_SCALE * mlp_out).astype(BF)

    d_attn = nt(d_branch, w_o).astype(BF)
    d_attn = d_attn.reshape(tokens, H, QD).transpose(1, 0, 2)
    d_attn = lax.all_to_all(d_attn, "head", split_axis=0, concat_axis=0, tiled=True)
    d_attn = d_attn.reshape(group, QD)
    delta = jnp.sum((d_attn.astype(F32) * o.astype(F32)).reshape(group, QD // HEAD_SIZE, HEAD_SIZE), -1)
    delta = delta.reshape(H, MICRO, 2, half, heads, SHARED).transpose(1, 2, 4, 5, 0, 3)
    delta = delta.reshape(MICRO, 2, heads, 1, SHARED * tile)
    dq, dkv = attention_backward(scalars, q, kv, to_heads(d_attn), lse, delta, heads, half)
    dkv = lax.psum_scatter(
        dkv.reshape(B * MICRO * 2 * tile, 2 * KD), "blk", scatter_dimension=0, tiled=True
    )
    dkv = from_tiles(dkv)
    d_qkv = jnp.concatenate(
        [rope_back(from_heads(dq), QD), rope_back(dkv[:, :KD], KD), dkv[:, KD:].astype(BF)], 1
    )
    d_xn1_part = nt(d_qkv, w_qkv)
    d_xn1 = lax.psum_scatter(
        d_xn1_part.astype(BF), "head", scatter_dimension=0, tiled=True
    ).astype(F32)
    grad_gain_one = jnp.sum(d_xn1_part * scaled_one, 0)

    d_branch_group = lax.all_gather(d_branch, "head", axis=0, tiled=True)
    grad_out = tn(o, d_branch_group).astype(BF)
    out_rows = QD // B
    grad_out = xor_scatter(
        lambda j: lax.dynamic_slice_in_dim(grad_out, (me ^ j) * out_rows, out_rows, 0), B
    )
    grad_out = lax.ppermute(
        grad_out.astype(BF),
        ("blk", "head"),
        [(b * H + h, h * B + b) for b in range(B) for h in range(H)],
    ).astype(F32)

    gain_grads = jnp.stack([grad_gain_one, grad_gain_two], 1).astype(BF)
    gain_grads = jnp.concatenate([gain_grads, jnp.zeros((D, 126), BF)], 1)

    def qkv_block(j):
        rows = lax.dynamic_slice_in_dim(gain_grads, (me ^ j) * block, block, 0)
        return jnp.concatenate([tn(columns(xn1, j), d_qkv).astype(BF), rows], 1)

    grad_qkv = xor_scatter(qkv_block, B).astype(BF).reshape(H, wrows, QD + 2 * KD + 128)
    grad_qkv = lax.all_to_all(grad_qkv, "head", split_axis=0, concat_axis=0, tiled=True)
    grad_qkv = grad_qkv.astype(F32)
    grad_gains = jnp.sum(grad_qkv[:, :, QD + 2 * KD : QD + 2 * KD + 2], 0)

    def side_by_side(values):
        return values.transpose(1, 0, 2).reshape(wrows, -1)

    scaled_one_own = own(scaled_one)
    d_input = d_resid + norm_back(d_xn1, gain_one, own(inv_one), scaled_one_own)
    output = jnp.einsum(
        "mrs,mrd->msd", order, output.reshape(MICRO, T, D), preferred_element_type=F32
    ).astype(BF)
    d_input = jnp.einsum(
        "mrs,mrd->msd",
        order.astype(F32),
        d_input.reshape(MICRO, T, D),
        precision=lax.Precision.HIGHEST,
        preferred_element_type=F32,
    )
    return (
        output,
        d_input,
        grad_gains[:, 0],
        grad_gains[:, 1],
        side_by_side(grad_qkv[:, :, :QD]),
        side_by_side(grad_qkv[:, :, QD : QD + KD]),
        side_by_side(grad_qkv[:, :, QD + KD : QD + 2 * KD]),
        grad_out,
        grad_gate_up[:, :F],
        grad_gate_up[:, F:],
        grad_down,
    )


def solution(mesh):
    both = ("blk", "head")
    return jax.shard_map(
        body,
        mesh=mesh,
        in_specs=(
            P(None, both, None),
            P(None, both, None),
            P(),
            P(),
            P(both),
            P(both),
            P(both, None),
            P(both, None),
            P(both, None),
            P(both, None),
            P("blk", "head"),
            P("blk", "head"),
            P("head", "blk"),
        ),
        out_specs=(
            P(None, both, None),
            P(None, both, None),
            P(both),
            P(both),
            P(both, None),
            P(both, None),
            P(both, None),
            P(both, None),
            P("blk", "head"),
            P("blk", "head"),
            P("head", "blk"),
        ),
        check_vma=False,
    )
```

time: 2100 us -> 794 us (0.38)
  waiting for transfers between devices: 1400 us -> 225 us
  matrix products: 292 us -> 136 us
  blocking collectives: 107 us -> 31.1 us
  local copies, waits for them, and re-layouts: 110 us -> 179 us
  Pallas kernels: 0 us -> 60.6 us
  other arithmetic: 115 us -> 70.9 us
    reduce_scatter x11 -> x4, waiting for transfers between devices: 883 us -> 29.8 us  [the longest x1 17.3 us: body(): lax.psum_scatter(nn(hidden, w_d).astype(BF), 'head', scatter_dimension=0,...]
    all_gather x13 -> x6, waiting for transfers between devices: 366 us -> 4.05 us  [the longest x1 3.98 us: body(): kv = lax.all_gather(to_tiles(jnp.concatenate([k, v], 1)), 'blk', axis=0)]
    dot_general x148 -> x37, matrix products: 292 us -> 136 us  [the longest x33 131 us: dot(): lax.dot_general(left, right, (contract, ((), ())), preferred_element_type...]
    ppermute x16 -> x41, waiting for transfers between devices: 95.3 us -> 191 us  [the longest x40 191 us: swap(): return lax.ppermute(x, 'blk', [(i, i ^ bit) for i in range(devices)])]
    unnamed x2 -> x0, blocking collectives: 83.8 us -> none
    pallas_call x0 -> x2, Pallas kernels: none -> 60.6 us  [the longest x1 32.1 us: attention_backward(): pl.pallas_call(functools.partial(backward_kernel, blocks=blocks, tile=til...]
    ppermute x16 -> x41, starting transfers between devices: 0.93 us -> 50.6 us  [the longest x40 50 us: swap(): return lax.ppermute(x, 'blk', [(i, i ^ bit) for i in range(devices)])]
    all_to_all x10 -> x2, waiting for transfers between devices: 49.7 us -> 0.01 us  [the longest x1 0.01 us: body(): lax.all_to_all(d_attn, 'head', split_axis=0, concat_axis=0, tiled=True)]
  transfers between devices with their start and end apart: 50 -> 53, of which waited for: 38 -> 16; matrix products, arithmetic and copies ran while one was open for 23% -> 41% of each run, Pallas kernels for 0% -> 8%
where the time goes in v1:
time: 794 us; the launch traced here: 779 us
  waiting for transfers between devices  225 us (28%)
  local copies, waits for them, and re-layouts  179 us (23%)
  matrix products  136 us (17%)
  other arithmetic  70.9 us (9%)
  Pallas kernels  60.6 us (8%)
  starting transfers between devices  59.9 us (8%)
  blocking collectives  31.1 us (4%)
  between operations  16.3 us (2%)
    ppermute x40, waiting for transfers between devices, swap(): return lax.ppermute(x, 'blk', [(i, i ^ bit) for i in range(devices)])  191 us
    dot_general x33, matrix products, dot(): lax.dot_general(left, right, (contract, ((), ())), preferred_element_type...  131 us
    ppermute x40, starting transfers between devices, swap(): return lax.ppermute(x, 'blk', [(i, i ^ bit) for i in range(devices)])  50 us
    dynamic_update_slice x27, local copies, waits for them, and re-layouts, natural(): lax.dynamic_update_slice_in_dim(whole, piece, (me ^ j) * block, axis)  38.4 us
    unnamed x164, local copies, waits for them, and re-layouts  37.6 us
    pallas_call x1, Pallas kernels, attention_backward(): pl.pallas_call(functools.partial(backward_kernel, blocks=blocks, tile=til...  32.1 us
    all_to_all x1, blocking collectives, body(): pack = lax.all_to_all(pack, 'head', split_axis=0, concat_axis=0, tiled=True)  31.1 us
    pallas_call x1, Pallas kernels, attention_forward(): pl.pallas_call(functools.partial(forward_kernel, blocks=blocks, tile=tile...  28.5 us
  transfers between devices with their start and end apart: 53, of which 16 were waited for; matrix products, arithmetic and copies ran while one was open for 41% of the time, Pallas kernels for 8%

profile of v1, /device:TPU:0, one launch (start us, length us, event | category | flops | bytes accessed | tf_op | source)
XLA Modules:
  0.0 778.8 jit_solution(9051611915792338798)
XLA Ops:
  15.8 31.1 %all_to_all.15 = bf16[4,64,896]{2,1,0:T(8,128)(2,1)S(1)} all-to-all(bf16[4,64,896]{2,1,0:T(8,128)(2,1)S(1)} %copy.279), channel_id=1, replica_groups=mesh['blk'=8,'head'=4] {'head'}, dimensions={0} | all-to-all | bytes 917504 | tf_op jit(solution)/shard_map/all_to_all | solution.py:361
  50.6 8.6 %collective-permute-done = bf16[256,896]{1,0:T(8,128)(2,1)S(1)} collective-permute-done((bf16[256,896]{1,0:T(8,128)(2,1)S(1)}, bf16[256,896]{1,0:T(8,128)(2,1)S(1)}, u32[]{:S(2)}, u32[]{:S(2)}) %collective-permute-start) | collective-permute-done | bytes 458784 | tf_op jit(solution)/shard_map/ppermute | solution.py:45
  120.6 28.5 %shard_map.212 = (bf16[2,2,512,128]{3,2,1,0:T(8,128)(2,1)}, f32[2,2,2,1,512]{4,3,2,1,0:T(1,128)}) custom-call(s32[3]{0:T(128)} %pad_add_fusion.scalars, bf16[2,2,512,128]{3,2,1,0:T(8,128)(2,1)} %reshape.458.q_ref, bf16[8,2,2,128,256]{4,3,2,1,0:T(8,128)(2,1)} %all-gather.9.cloned.1.call-done.kv_ref), custom_call_target="tpu_custom_call" | custom-call | flops 1073741824 | bytes 3145728 | tf_op jit(solution)/shard_map/pallas_call | solution.py:242
  149.1 14.3 %reshape.460 = bf16[2,2,4,4,32,2,64]{6,5,4,3,2,1,0:T(2,128)(2,1)S(1)} reshape(bf16[2,2,512,128]{3,2,1,0:T(8,128)(2,1)} %get-tuple-element.39) | data formatting | bytes 1048576 | tf_op jit(solution)/shard_map/reshape | solution.py:411
  179.5 13.6 %collective-permute-done.15 = bf16[2048,256]{1,0:T(8,128)(2,1)S(1)} collective-permute-done((bf16[2048,256]{1,0:T(8,128)(2,1)}, bf16[2048,256]{1,0:T(8,128)(2,1)S(1)}, u32[]{:S(2)}, u32[]{:S(2)}) %collective-permute-start.15) | collective-permute-done | bytes 1048608 | tf_op jit(solution)/shard_map/ppermute | solution.py:45
  201.3 50.7 %collective-permute-done.17 = bf16[1024,256]{1,0:T(8,128)(2,1)S(1)} collective-permute-done((bf16[1024,256]{1,0:T(8,128)(2,1)S(1)}, bf16[1024,256]{1,0:T(8,128)(2,1)S(1)}, u32[]{:S(2)}, u32[]{:S(2)}) %collective-permute-start.17) | collective-permute-done | bytes 524320 | tf_op jit(solution)/shard_map/ppermute | solution.py:45
  270.3 9.7 %collective-permute-done.5 = bf16[256,2048]{1,0:T(8,128)(2,1)} collective-permute-done((bf16[256,2048]{1,0:T(8,128)(2,1)}, bf16[256,2048]{1,0:T(8,128)(2,1)}, u32[]{:S(2)}, u32[]{:S(2)}) %collective-permute-start.5) | collective-permute-done | bytes 1048608 | tf_op jit(solution)/shard_map/ppermute | solution.py:45
  288.8 26.4 %collective-permute-done.7 = bf16[128,2048]{1,0:T(8,128)(2,1)S(1)} collective-permute-done((bf16[128,2048]{1,0:T(8,128)(2,1)S(1)}, bf16[128,2048]{1,0:T(8,128)(2,1)S(1)}, u32[]{:S(2)}, u32[]{:S(2)}) %collective-permute-start.7) | collective-permute-done | bytes 524320 | tf_op jit(solution)/shard_map/ppermute | solution.py:45
  342.6 9.4 %multiply_reduce_fusion.1 = (f32[512]{0:T(512)S(1)}, f32[512,2048]{1,0:T(8,128)S(1)}) fusion(bf16[512,2048]{1,0:T(8,128)(2,1)} %all-gather.11.cloned.1.call-done, bf16[2048,2048]{1,0:T(8,128)(2,1)} %slice_dynamic-update-slice_fusion.8, bf16[512,2048]{1,0:T(8,128)(2,1)} %all-gather.7.cloned.1.call-done), kind=kOutput, calls=%fused_computation.39 | convolution fusion | flops 4300209664 | bytes 16779264 | tf_op jit(solution)/shard_map/dot_general | solution.py:29
  369.1 5.8 copy-done.3
  374.9 11.5 %fusion.132 = f32[512,4096]{1,0:T(8,128)} fusion(bf16[512,2048]{1,0:T(8,128)(2,1)S(1)} %get-tuple-element.47, bf16[2048,4096]{1,0:T(8,128)(2,1)S(1)} %slice_dynamic-update-slice_fusion), kind=kOutput, calls=%fused_computation.351 | convolution fusion | flops 8589934592 | bytes 27262976 | tf_op jit(solution)/shard_map/dot_general | solution.py:29
  386.5 13.6 %multiply_convert_fusion.1 = (bf16[512,2048]{1,0:T(8,128)(2,1)S(1)}, bf16[512,2048]{1,0:T(8,128)(2,1)S(1)}, bf16[512,2048]{1,0:T(8,128)(2,1)}) fusion(f32[512,4096]{1,0:T(8,128)} %fusion.132, bf16[512,2048]{1,0:T(8,128)(2,1)} %all-gather.15.cloned.1.call-done, bf16[2048,2048]{1,0:T(8,128)(2,1)} %copy-done.8), kind=kOutput, calls=%fused_computation.34 | convolution fusion | flops 4310695936 | bytes 25165824 | tf_op jit(solution)/shard_map/dot_general | solution.py:29
  402.1 13.4 %convolution_convert_fusion.10 = bf16[512,2048]{1,0:T(8,128)(2,1)} fusion(bf16[2048,4096]{1,0:T(8,128)(2,1)} %copy-done.3, bf16[512,2048]{1,0:T(8,128)(2,1)S(1)} %get-tuple-element.50, bf16[512,2048]{1,0:T(8,128)(2,1)S(1)} %get-tuple-element.49), kind=kOutput, calls=%fused_computation.43 | convolution fusion | flops 8599371776 | bytes 23068672 | tf_op jit(solution)/shard_map/dot_general | solution.py:29
  415.6 9.8 %convolution_convert_fusion.9 = bf16[512,2048]{1,0:T(8,128)(2,1)} fusion(bf16[512,2048]{1,0:T(8,128)(2,1)} %get-tuple-element.51, bf16[2048,2048]{1,0:T(8,128)(2,1)} %copy-done.8), kind=kOutput, calls=%fused_computation.42 | convolution fusion | flops 4296015872 | bytes 12582912 | tf_op jit(solution)/shard_map/dot_general | solution.py:29
  464.2 8.0 %pad_maximum_fusion = bf16[4,256,4096]{2,1,0:T(8,128)(2,1)} fusion(bf16[1,256,4096]{2,1,0:T(8,128)(2,1)} %fusion.7, bf16[1,256,4096]{2,1,0:T(8,128)(2,1)} %fusion.6, bf16[1,256,4096]{2,1,0:T(8,128)(2,1)} %fusion.5, bf16[1,256,4096]{2,1,0:T(8,128)(2,1)} %fusion.4), kind=kLoop, calls=%fused_computation | loop fusion | flops 12582912 | bytes 16777216 | tf_op jit(solution)/shard_map/stack | solution.py:91
  479.7 6.3 convolution_convert_fusion.19
  497.1 17.3 %reduce-scatter.5.cloned.1.call-done = bf16[128,2048]{1,0:T(8,128)(2,1)} async-done(((bf16[512,2048]{1,0:T(8,128)(2,1)}), bf16[128,2048]{1,0:T(8,128)(2,1)}) %reduce-scatter.5.cloned.1.call-update) | async-done | bytes 524304 | tf_op jit(solution)/shard_map/reduce_scatter | solution.py:448
  536.0 32.1 %shard_map.213 = (bf16[2,2,512,128]{3,2,1,0:T(8,128)(2,1)}, bf16[8,2,2,128,256]{4,3,2,1,0:T(8,128)(2,1)}) custom-call(s32[3]{0:T(128)} %pad_add_fusion.scalars, bf16[2,2,512,128]{3,2,1,0:T(8,128)(2,1)} %reshape.458.q_ref, bf16[8,2,2,128,256]{4,3,2,1,0:T(8,128)(2,1)} %all-gather.9.cloned.1.call-done.kv_ref, bf16[2,2,512,128]{3,2,1,0:T(8,128)(2,1)} %reshape.465.do_ref, ...), custom_call_target="tpu_custom_call" | custom-call | flops 2684354560 | bytes 5767168 | tf_op jit(solution)/shard_map/pallas_call | solution.py:268
  573.9 5.3 collective-permute-start.40
  608.9 11.1 %reduce-scatter.9.cloned.1.call-done = bf16[512,256]{1,0:T(8,128)(2,1)} async-done(((bf16[4096,256]{1,0:T(8,128)(2,1)}), bf16[512,256]{1,0:T(8,128)(2,1)}) %reduce-scatter.9.cloned.1.call-update) | async-done | bytes 262160 | tf_op jit(solution)/shard_map/reduce_scatter | solution.py:476
  621.4 6.5 multiply_reduce_fusion
  652.5 22.6 %collective-permute-done.34 = bf16[128,4096]{1,0:T(8,128)(2,1)S(1)} collective-permute-done((bf16[128,4096]{1,0:T(8,128)(2,1)S(1)}, bf16[128,4096]{1,0:T(8,128)(2,1)S(1)}, u32[]{:S(2)}, u32[]{:S(2)}) %collective-permute-start.34) | collective-permute-done | bytes 1048608 | tf_op jit(solution)/shard_map/ppermute | solution.py:45
  692.5 6.1 collective-permute-done.24
  706.3 43.5 %collective-permute-done.27 = bf16[64,2048]{1,0:T(8,128)(2,1)S(1)} collective-permute-done((bf16[64,2048]{1,0:T(8,128)(2,1)S(1)}, bf16[64,2048]{1,0:T(8,128)(2,1)S(1)}, u32[]{:S(2)}, u32[]{:S(2)}) %collective-permute-start.27) | collective-permute-done | bytes 262176 | tf_op jit(solution)/shard_map/ppermute | solution.py:45
  (514 shorter events, 357.1 us)
Async XLA Ops:
  7.2 67.6 %all-gather.7.cloned.1.call-start = ((), (), s32[]{:S(2)}) async-start(), calls=%async_computation.7 | async-start | bytes 2621440 | tf_op jit(solution)/shard_map/all_gather | solution.py:379
  9.5 111.1 %all-gather.9.cloned.1.call-start = ((), (), s32[]{:S(2)}) async-start(), calls=%async_computation.8 | async-start | bytes 2359296 | tf_op jit(solution)/shard_map/all_gather | solution.py:425
  94.7 159.0 %all-gather.13.cloned.1.call-start = ((), (), s32[]{:S(2)}) async-start(), calls=%async_computation.10 | async-start | bytes 1310720 | tf_op jit(solution)/shard_map/all_gather | solution.py:382
  95.5 247.2 %all-gather.11.cloned.1.call-start = ((), (), s32[]{:S(2)}) async-start(), calls=%async_computation.9 | async-start | bytes 2621440 | tf_op jit(solution)/shard_map/all_gather | solution.py:429
  165.9 220.6 %all-gather.15.cloned.1.call-start = ((), (), s32[]{:S(2)}) async-start(), calls=%async_computation.12 | async-start | bytes 2621440 | tf_op jit(solution)/shard_map/all_gather | solution.py:434
  176.6 86.7 %collective-permute-start.10 = (bf16[256,4096]{1,0:T(8,128)(2,1)}, bf16[256,4096]{1,0:T(8,128)(2,1)}, u32[]{:S(2)}, u32[]{:S(2)}) collective-permute-start(bf16[256,4096]{1,0:T(8,128)(2,1)} %get-tuple-element.84), channel_id=1, source_target_pairs={{0,8},{4,12},{8,0},{12,4},{16,24},{20,28},{24,16},{28,20},{1,9},{5... | collective-permute-start | bytes 6291464 | tf_op jit(solution)/shard_map/ppermute | solution.py:45
  177.2 87.9 %collective-permute-start.11 = (bf16[256,4096]{1,0:T(8,128)(2,1)}, bf16[256,4096]{1,0:T(8,128)(2,1)}, u32[]{:S(2)}, u32[]{:S(2)}) collective-permute-start(bf16[256,4096]{1,0:T(8,128)(2,1)} %get-tuple-element.84), channel_id=1, source_target_pairs={{0,16},{4,20},{8,24},{12,28},{16,0},{20,4},{24,8},{28,12},{1,17},{... | collective-permute-start | bytes 6291464 | tf_op jit(solution)/shard_map/ppermute | solution.py:45
  193.1 58.8 %collective-permute-start.17 = (bf16[1024,256]{1,0:T(8,128)(2,1)S(1)}, bf16[1024,256]{1,0:T(8,128)(2,1)S(1)}, u32[]{:S(2)}, u32[]{:S(2)}) collective-permute-start(bf16[1024,256]{1,0:T(8,128)(2,1)S(1)} %slice.433), channel_id=1, source_target_pairs={{0,16},{4,20},{8,24},{12,28},{16,0},{20,4},{24,8},{28,12},{1,17},{... | collective-permute-start | bytes 1572872 | tf_op jit(solution)/shard_map/ppermute | solution.py:45
  197.6 55.3 %collective-permute-start.18 = (bf16[1024,256]{1,0:T(8,128)(2,1)S(1)}, bf16[1024,256]{1,0:T(8,128)(2,1)S(1)}, u32[]{:S(2)}, u32[]{:S(2)}) collective-permute-start(bf16[1024,256]{1,0:T(8,128)(2,1)S(1)} %slice.434), channel_id=1, source_target_pairs={{0,8},{4,12},{8,0},{12,4},{16,24},{20,28},{24,16},{28,20},{1,9},{5... | collective-permute-start | bytes 1572872 | tf_op jit(solution)/shard_map/ppermute | solution.py:45
  253.7 69.3 %collective-permute-start.19 = (bf16[8192,256]{1,0:T(8,128)(2,1)}, bf16[8192,256]{1,0:T(8,128)(2,1)}, u32[]{:S(2)}, u32[]{:S(2)}) collective-permute-start(bf16[8192,256]{1,0:T(8,128)(2,1)} %constant_dynamic-update-slice_fusion.18), channel_id=1, source_target_pairs={{0,4},{4,0},{8,12},{12,8},{16,20},{20,16},{24,28},{28,24},{1,5},{5... | collective-permute-start | bytes 12582920 | tf_op jit(solution)/shard_map/ppermute | solution.py:45
  255.9 204.0 %reduce-scatter.7.cloned.1.call-start = ((), (), s32[]{:S(2)}) async-start(), calls=%async_computation.13 | async-start | bytes 2621440 | tf_op jit(solution)/shard_map/reduce_scatter | solution.py:445
  415.6 98.8 %reduce-scatter.5.cloned.1.call-start = ((), (), s32[]{:S(2)}) async-start(), calls=%async_computation.11 | async-start | bytes 2621440 | tf_op jit(solution)/shard_map/reduce_scatter | solution.py:448
  425.5 178.8 %all-gather.17.cloned.1.call-start = ((), (), s32[]{:S(2)}) async-start(), calls=%async_computation.16 | async-start | bytes 2621440 | tf_op jit(solution)/shard_map/all_gather | solution.py:489
  435.7 55.4 %collective-permute-start.36 = (bf16[4,2048,256]{2,1,0:T(8,128)(2,1)}, bf16[4,2048,256]{2,1,0:T(8,128)(2,1)}, u32[]{:S(2)}, u32[]{:S(2)}) collective-permute-start(bf16[4,2048,256]{2,1,0:T(8,128)(2,1)} %pad_maximum_fusion.2), channel_id=1, source_target_pairs={{0,4},{4,0},{8,12},{12,8},{16,20},{20,16},{24,28},{28,24},{1,5},{5... | collective-permute-start | bytes 12582920 | tf_op jit(solution)/shard_map/ppermute | solution.py:45
  472.2 165.0 %collective-permute-start.31 = (bf16[4,256,4096]{2,1,0:T(8,128)(2,1)}, bf16[4,256,4096]{2,1,0:T(8,128)(2,1)}, u32[]{:S(2)}, u32[]{:S(2)}) collective-permute-start(bf16[4,256,4096]{2,1,0:T(8,128)(2,1)} %pad_maximum_fusion), channel_id=1, source_target_pairs={{0,4},{4,0},{8,12},{12,8},{16,20},{20,16},{24,28},{28,24},{1,5},{5... | collective-permute-start | bytes 25165832 | tf_op jit(solution)/shard_map/ppermute | solution.py:45
  490.7 129.2 %reduce-scatter.9.cloned.1.call-start = ((), (), s32[]{:S(2)}) async-start(), calls=%async_computation.14 | async-start | bytes 2359296 | tf_op jit(solution)/shard_map/reduce_scatter | solution.py:476
  494.3 77.2 %collective-permute-start.39 = (bf16[1024,256]{1,0:T(8,128)(2,1)}, bf16[1024,256]{1,0:T(8,128)(2,1)}, u32[]{:S(2)}, u32[]{:S(2)}) collective-permute-start(bf16[1024,256]{1,0:T(8,128)(2,1)} %get-tuple-element.78), channel_id=1, source_target_pairs={{0,8},{4,12},{8,0},{12,4},{16,24},{20,28},{24,16},{28,20},{1,9},{5... | collective-permute-start | bytes 1572872 | tf_op jit(solution)/shard_map/ppermute | solution.py:45
  495.6 83.6 %collective-permute-start.37 = (bf16[1024,256]{1,0:T(8,128)(2,1)}, bf16[1024,256]{1,0:T(8,128)(2,1)}, u32[]{:S(2)}, u32[]{:S(2)}) collective-permute-start(bf16[1024,256]{1,0:T(8,128)(2,1)} %get-tuple-element.77), channel_id=1, source_target_pairs={{0,16},{4,20},{8,24},{12,28},{16,0},{20,4},{24,8},{28,12},{1,17},{... | collective-permute-start | bytes 1572872 | tf_op jit(solution)/shard_map/ppermute | solution.py:45
  568.2 197.6 %reduce-scatter.11.cloned.1.call-start = ((), (), s32[]{:S(2)}) async-start(), calls=%async_computation.15 | async-start | bytes 2621440 | tf_op jit(solution)/shard_map/reduce_scatter | solution.py:484
  573.9 177.7 %collective-permute-start.40 = (bf16[2048,256]{1,0:T(8,128)(2,1)}, bf16[2048,256]{1,0:T(8,128)(2,1)}, u32[]{:S(2)}, u32[]{:S(2)}) collective-permute-start(bf16[2048,256]{1,0:T(8,128)(2,1)} %pad_maximum_fusion.8), channel_id=1, source_target_pairs={{0,16},{4,20},{8,24},{12,28},{16,0},{20,4},{24,8},{28,12},{1,17},{... | collective-permute-start | bytes 3145736 | tf_op jit(solution)/shard_map/ppermute | solution.py:45
  581.6 170.1 %collective-permute-start.38 = (bf16[2048,256]{1,0:T(8,128)(2,1)}, bf16[2048,256]{1,0:T(8,128)(2,1)}, u32[]{:S(2)}, u32[]{:S(2)}) collective-permute-start(bf16[2048,256]{1,0:T(8,128)(2,1)} %pad_maximum_fusion.7), channel_id=1, source_target_pairs={{0,8},{4,12},{8,0},{12,4},{16,24},{20,28},{24,16},{28,20},{1,9},{5... | collective-permute-start | bytes 3145736 | tf_op jit(solution)/shard_map/ppermute | solution.py:45
  692.2 66.9 %collective-permute-start.35 = (bf16[256,4096]{1,0:T(8,128)(2,1)}, bf16[256,4096]{1,0:T(8,128)(2,1)}, u32[]{:S(2)}, u32[]{:S(2)}) collective-permute-start(bf16[256,4096]{1,0:T(8,128)(2,1)} %pad_maximum_fusion.4), channel_id=1, source_target_pairs={{0,16},{4,20},{8,24},{12,28},{16,0},{20,4},{24,8},{28,12},{1,17},{... | collective-permute-start | bytes 6291464 | tf_op jit(solution)/shard_map/ppermute | solution.py:45
  698.6 60.5 %collective-permute-start.33 = (bf16[256,4096]{1,0:T(8,128)(2,1)}, bf16[256,4096]{1,0:T(8,128)(2,1)}, u32[]{:S(2)}, u32[]{:S(2)}) collective-permute-start(bf16[256,4096]{1,0:T(8,128)(2,1)} %pad_maximum_fusion.3), channel_id=1, source_target_pairs={{0,8},{4,12},{8,0},{12,4},{16,24},{20,28},{24,16},{28,20},{1,9},{5... | collective-permute-start | bytes 6291464 | tf_op jit(solution)/shard_map/ppermute | solution.py:45
  701.7 54.3 %all-to-all-start.2 = ((bf16[4,64,896]{2,1,0:T(8,128)(2,1)}), bf16[4,64,896]{2,1,0:T(8,128)(2,1)S(1)}, u32[]{:S(2)}, u32[]{:S(2)}) async-start(bf16[4,64,896]{2,1,0:T(8,128)(2,1)} %bitcast.48), calls=%async_computation.6 | async-start | bytes 917504 | tf_op jit(solution)/shard_map/all_to_all | solution.py:509
  (104 other events, 1604.0 us)
Sparse Core Ops, SparseCore 0:
  10.2 58.3 all-gather.6
  94.8 25.7 all-gather.8
  122.2 27.9 all-gather.12
  166.0 50.1 all-gather.10
  256.1 46.2 all-gather.14
  415.7 44.2 reduce-scatter.6
  462.9 51.4 reduce-scatter.4
  516.0 45.8 all-gather.16
  568.3 51.6 reduce-scatter.8
  628.0 43.8 reduce-scatter.10

commit v2 on v1

v2 whole, which is shorter than its diff:
```python
import functools

import jax
import jax.numpy as jnp
from jax import lax
from jax.experimental import pallas as pl
from jax.experimental.pallas import tpu as pltpu
from jax.sharding import PartitionSpec as P

MODEL_WIDTH = 2048
QUERY_HEADS = 32
KEY_VALUE_HEADS = 8
HEAD_SIZE = 64
SHARED = QUERY_HEADS // KEY_VALUE_HEADS
MICRO = 2
LANES = 128

SCORE_SCALE = 0.015625
RESIDUAL_SCALE = 0.22
EPSILON = 1e-06
ROPE_BASE = 10000000.0
NEG_FILL = -1e30

BF = jnp.bfloat16
F32 = jnp.float32
VMEM_LIMIT = 56 * 1024 * 1024
COST = 0.1


def dot(left, right, contract):
    return lax.dot_general(left, right, (contract, ((), ())), preferred_element_type=F32)


def nn(left, right):
    return dot(left, right, ((1,), (0,)))


def tn(left, right):
    return dot(left, right, ((0,), (0,)))


def nt(left, right):
    return dot(left, right, ((1,), (1,)))


def swap(x, bit, devices):
    return lax.ppermute(x, "blk", [(i, i ^ bit) for i in range(devices)])


def xor_gather(x, devices, join=None):
    even = [x] + [swap(x, bit, devices) for bit in range(2, devices, 2)]
    even = (join or jnp.stack)(even)
    return even, swap(even, 1, devices)


def add(left, right):
    return (left.astype(F32) + right.astype(F32)).astype(BF)


def core_scatter(held, devices):
    came = [swap(held[bit // 2], bit, devices) for bit in range(2, devices, 2)]
    return sum((part.astype(F32) for part in came), held[0].astype(F32))


def core_scatter_steps(held, devices):
    if devices != 8:
        return core_scatter(held, devices)
    h0, h2, h4, h6 = held
    half = h0.shape[0] // 2
    from_x = swap(h6[:half], 2, devices)
    from_y = swap(h6[half:], 4, devices)
    h4 = jnp.concatenate([add(h4[:half], from_x), h4[half:]], 0)
    h2 = jnp.concatenate([h2[:half], add(h2[half:], from_y)], 0)
    came_x = swap(h2, 2, devices)
    came_y = swap(h4, 4, devices)
    return h0.astype(F32) + came_x.astype(F32) + came_y.astype(F32)


def xor_scatter(even, odd, devices):
    return core_scatter(add(even, swap(odd, 1, devices)), devices)


def head_exchange(parts):
    return lax.all_to_all(parts, "head", split_axis=0, concat_axis=0, tiled=True)


def head_shift(x, by, devices):
    return lax.ppermute(x, "head", [(i, (i + by) % devices) for i in range(devices)])


def head_gather(x, devices):
    return [x] + [head_shift(x, k, devices) for k in range(1, devices)]


def head_deal(parts, devices):
    return [parts[0]] + [head_shift(parts[k], k, devices) for k in range(1, devices)]


def same_core_groups(devices):
    return [list(range(core, devices, 2)) for core in range(2)]


def plane_scatter(kept, devices, axis):
    return lax.psum_scatter(
        kept,
        "blk",
        scatter_dimension=axis,
        tiled=True,
        axis_index_groups=same_core_groups(devices),
    )


def call(kernel, grid, in_specs, out_specs, out_shape, scratch, flops, moved, args, wait=()):
    wait = tuple(wait)
    given = 1 + len(in_specs)
    in_specs = list(in_specs) + [pl.BlockSpec(memory_space=pl.ANY)] * len(wait)
    args = tuple(args) + wait

    def run(*refs):
        kernel(*refs[:given], *refs[given + len(wait) :])

    return pl.pallas_call(
        run,
        grid_spec=pltpu.PrefetchScalarGridSpec(
            num_scalar_prefetch=1,
            grid=grid,
            in_specs=in_specs,
            out_specs=out_specs,
            scratch_shapes=scratch,
        ),
        out_shape=out_shape,
        compiler_params=pltpu.CompilerParams(vmem_limit_bytes=VMEM_LIMIT),
        cost_estimate=pl.CostEstimate(
            flops=int(flops * COST), bytes_accessed=int(moved * COST), transcendentals=0
        ),
    )(*args)


def whole(shape):
    return pl.BlockSpec(shape, lambda *_: (0,) * len(shape))


def shape_of(shape, dtype):
    return jax.ShapeDtypeStruct(shape, dtype)


def chunk(scalars, j, width):
    return pl.ds(pl.multiple_of((scalars[0] ^ j) * width, LANES), width)


def turned(values):
    lane = lax.broadcasted_iota(jnp.int32, values.shape, 1) % HEAD_SIZE
    quarter = HEAD_SIZE // 2
    return jnp.where(
        lane < quarter,
        pltpu.roll(values, LANES - quarter, 1),
        pltpu.roll(values, quarter, 1),
    )


def rope_lanes(values, cosine, sine, first, limit):
    out = values * cosine + turned(values) * sine
    if first + LANES <= limit:
        return out
    lane = lax.broadcasted_iota(jnp.int32, values.shape, 1)
    return jnp.where(lane < limit - first, out, values)


def before(s, k, devices):
    return (s[1] + devices - k) % devices


def after(s, k, devices):
    return (s[1] + k) % devices


def order_kernel(s, x_ref, up_ref, place_ref, xs_ref, us_ref):
    M, T, D = x_ref.shape
    for m in range(M):
        rank = lax.broadcasted_iota(jnp.int32, (T, T), 0)
        order = (place_ref[m] == rank).astype(BF)
        at = pl.ds(m * T, T)
        x = nn(order, x_ref[m]).astype(BF)
        for h in range(xs_ref.shape[0]):
            xs_ref[h, at, :] = x
        us_ref[at, :] = nn(order, up_ref[m]).astype(BF)


def in_order(scalars, x, upstream, place, H, wait):
    M, T, D = x.shape
    out = shape_of((M * T, D), BF)
    return call(
        order_kernel,
        (1,),
        [whole(x.shape), whole(x.shape), whole((M, 1, T))],
        [whole((H,) + out.shape), whole(out.shape)],
        [shape_of((H,) + out.shape, BF), out],
        [],
        4 * M * T * T * D,
        10 * M * T * D,
        (scalars, x, upstream, place.reshape(M, 1, T)),
        wait,
    )


def pack_kernel(s, q_ref, k_ref, v_ref, g_ref, *outs):
    devices = len(outs)
    QD = q_ref.shape[1] // devices
    KD = k_ref.shape[1] // devices
    for k, out_ref in enumerate(outs):
        for h in range(devices):

            @pl.when(after(s, k, devices) == h)
            def _(out_ref=out_ref, h=h):
                out_ref[:, :QD] = q_ref[:, h * QD : (h + 1) * QD]
                out_ref[:, QD : QD + 2 * KD] = jnp.concatenate(
                    [k_ref[:, h * KD : (h + 1) * KD], v_ref[:, h * KD : (h + 1) * KD]], 1
                )
                out_ref[:, QD + 2 * KD :] = g_ref[...]


def pack_weights(scalars, w_query, w_key, w_value, gains, devices):
    rows = w_query.shape[0]
    columns = (w_query.shape[1] + w_key.shape[1] + w_value.shape[1]) // devices + LANES
    out = shape_of((rows, columns), BF)
    args = (scalars, w_query, w_key, w_value, gains)
    return call(
        pack_kernel,
        (1,),
        [whole(a.shape) for a in args[1:]],
        [whole(out.shape)] * devices,
        [out] * devices,
        [],
        0,
        8 * rows * columns * devices,
        args,
    )


def copies_kernel(s, from_ref, out_ref, *, scale):
    values = from_ref[...]
    if scale is not None:
        values = (scale * values.astype(F32)).astype(BF)
    for h in range(out_ref.shape[0]):
        out_ref[h] = values


def copies(scalars, values, H, scale, wait):
    shape = (H,) + values.shape
    return call(
        functools.partial(copies_kernel, scale=scale),
        (1,),
        [whole(values.shape)],
        [whole(shape)],
        [shape_of(shape, BF)],
        [],
        0,
        4 * H * values.size,
        (scalars, values),
        wait,
    )[0]


def hold_kernel(s, *refs):
    count = len(refs) // 2
    for from_ref, to_ref in zip(refs[:count], refs[count:]):
        to_ref[...] = from_ref[...]


def hold(scalars, arrays, wait):
    return call(
        hold_kernel,
        (1,),
        [whole(a.shape) for a in arrays],
        [whole(a.shape) for a in arrays],
        [shape_of(a.shape, a.dtype) for a in arrays],
        [],
        0,
        sum(4 * a.size for a in arrays),
        (scalars, *arrays),
        wait,
    )


def join_kernel(s, *refs):
    *parts, out_ref = refs
    for p, part_ref in enumerate(parts):
        out_ref[p] = part_ref[...]


def join(scalars, parts, wait=()):
    shape = (len(parts),) + parts[0].shape
    return call(
        join_kernel,
        (1,),
        [whole(p.shape) for p in parts],
        [whole(shape)],
        [shape_of(shape, parts[0].dtype)],
        [],
        0,
        4 * len(parts) * parts[0].size,
        (scalars, *parts),
        wait,
    )[0]


def wide_kernel(s, from_ref, out_ref):
    out_ref[...] = from_ref[...].astype(F32)


def wide(scalars, values, wait):
    rows, columns = values.shape
    piece = pl.BlockSpec((rows // 4, columns), lambda i, s: (i, 0))
    return call(
        wide_kernel,
        (4,),
        [piece],
        [piece],
        [shape_of(values.shape, F32)],
        [],
        0,
        6 * values.size,
        (scalars, values),
        wait,
    )[0]


def arrange_kernel(s, *refs):
    *parts, out_ref = refs
    for k, part_ref in enumerate(parts):
        out_ref[before(s, k, len(parts))] = part_ref[...]


def arrange(scalars, parts, wait=()):
    shape = (len(parts),) + parts[0].shape
    return call(
        arrange_kernel,
        (1,),
        [whole(p.shape) for p in parts],
        [whole(shape)],
        [shape_of(shape, parts[0].dtype)],
        [],
        0,
        4 * len(parts) * parts[0].size,
        (scalars, *parts),
        wait,
    )[0]


def project_kernel(s, x_ref, we_ref, wo_ref, cos_ref, sin_ref, xn_ref, q_ref, kv_ref, gain_ref):
    H, _, T, D = x_ref.shape
    places, block, columns = we_ref.shape
    QD = q_ref.shape[-1]
    KD = kv_ref.shape[-1] // 2
    used = QD + 2 * KD

    @pl.when(pl.program_id(0) == 0)
    def _():
        for place in range(places):
            for parity, w_ref in enumerate((we_ref, wo_ref)):
                held = w_ref[place, :, used : used + LANES].astype(F32).T
                gain_ref[:, chunk(s, 2 * place + parity, block)] = held[:8]

    x = x_ref[:, 0].reshape(H * T, D).astype(F32)
    inverse = lax.rsqrt(jnp.mean(x * x, -1, keepdims=True) + EPSILON)
    xn = ((x * inverse) * gain_ref[0:1, :]).astype(BF)
    xn_ref[:, 0] = xn.reshape(H, T, D)
    acc = jnp.zeros((H * T, used), F32)
    for place in range(places):
        for parity, w_ref in enumerate((we_ref, wo_ref)):
            left = xn_ref[:, 0, :, chunk(s, 2 * place + parity, block)].reshape(H * T, block)
            acc = acc + nn(left, w_ref[place, :, :used])
    cosine = cos_ref[...]
    sine = sin_ref[...]
    for first in range(0, used, LANES):
        part = acc[:, first : first + LANES]
        if first < QD + KD:
            part = rope_lanes(part, cosine, sine, first, QD + KD)
        if first < QD:
            q_ref[:, 0, :, first : first + LANES] = (
                (part * SCORE_SCALE).astype(BF).reshape(H, T, LANES)
            )
        else:
            kv_ref[:, 0, :, first - QD : first - QD + LANES] = part.astype(BF).reshape(H, T, LANES)


def project(scalars, x, w_even, w_odd, cosine, sine, QD, KD, wait):
    H, M, T, D = x.shape
    used = QD + 2 * KD

    def rows(width):
        return pl.BlockSpec((H, 1, T, width), lambda m, s: (0, m, 0, 0))

    return call(
        project_kernel,
        (M,),
        [rows(D), whole(w_even.shape), whole(w_odd.shape), whole(cosine.shape), whole(sine.shape)],
        [rows(D), rows(QD), rows(2 * KD), whole((8, D))],
        [
            shape_of((H, M, T, D), BF),
            shape_of((H, M, T, QD), BF),
            shape_of((H, M, T, 2 * KD), BF),
            shape_of((8, D), F32),
        ],
        [],
        2 * H * M * T * D * used,
        4 * H * M * T * D + 4 * w_even.size,
        (scalars, x, w_even, w_odd, cosine, sine),
        wait,
    )


def run_offset(index, run, tile, half):
    if run == 0:
        return index
    return (tile - half) - (index // half) * half + index % half


def key_positions(s, natural, run, length, tile, half, blocks):
    row = lax.broadcasted_iota(jnp.int32, (4 * tile, 1), 0)
    part = row // tile
    owner = 4 * natural + ((s[0] & 3) ^ (((part & 1) << 1) | (part >> 1)))
    row_tile = owner if run == 0 else 2 * blocks - 1 - owner
    position = row_tile * tile + run_offset(row % tile, run, tile, half)
    return jnp.where(position < length, position, jnp.int32(1 << 30))


def query_positions(s, run, rows, tile, half, blocks):
    own = s[0] if run == 0 else 2 * blocks - 1 - s[0]
    lane = lax.broadcasted_iota(jnp.int32, (1, rows), 1) % tile
    return own * tile + run_offset(lane, run, tile, half)


def slab(even_ref, odd_ref, y, run, first, last):
    parts = [
        ref[2 * y + i, :, 0, run, :, first:last] for ref in (even_ref, odd_ref) for i in range(2)
    ]
    H, half, width = parts[0].shape
    return jnp.concatenate([part.reshape(H * half, width) for part in parts], 0)


def heads_across(ref, run, head, heads):
    H, _, _, half, _ = ref.shape
    first = head * SHARED * HEAD_SIZE
    values = ref[:, 0, run, :, first : first + SHARED * HEAD_SIZE]
    values = values.reshape(H * half, SHARED * HEAD_SIZE).astype(F32).T
    values = jnp.concatenate(
        [values[g * HEAD_SIZE : (g + 1) * HEAD_SIZE] for g in range(SHARED)], 1
    )
    return values


def padded(values, head, heads):
    values = values.astype(BF)
    if heads == 1:
        return values
    zeros = jnp.zeros_like(values)
    return jnp.concatenate([values, zeros] if head == 0 else [zeros, values], 0)


def heads_back(values, tile):
    return jnp.concatenate(
        [values[:, g * tile : (g + 1) * tile] for g in range(SHARED)], 0
    ).T


def slab_loops(s, length, run, tile, blocks, state, step):
    slabs = blocks // 4
    own = s[0] // 4
    if run == 0:
        return lax.fori_loop(0, own + 1, lambda n, st: step(st, n, 0, True), state)
    state = lax.fori_loop(0, slabs, lambda n, st: step(st, n, 0, False), state)
    within = (2 * blocks * tile - length) // (4 * tile)
    return lax.fori_loop(
        jnp.maximum(own, within), slabs, lambda n, st: step(st, n, 1, True), state
    )


def fold_rows(values, combine):
    rows, lanes = values.shape
    return combine(values.reshape(rows // 8, 8, lanes), axis=0)


def forward_kernel(s, q_ref, ke_ref, ko_ref, o_ref, lse_ref, *, heads):
    H, _, _, half, QD = q_ref.shape
    blocks = 2 * ke_ref.shape[0]
    tile = H * half
    width = heads * HEAD_SIZE
    rows = SHARED * tile
    length = s[2 + pl.program_id(0)]
    for run in range(2):
        q = [padded(heads_across(q_ref, run, head, heads), head, heads) for head in range(heads)]
        at = query_positions(s, run, rows, tile, half, blocks)

        def step(state, natural, key_run, masked, q=q, at=at):
            y = natural ^ (s[0] >> 2)
            k = slab(ke_ref, ko_ref, y, key_run, 0, width)
            v = slab(ke_ref, ko_ref, y, key_run, width, 2 * width)
            if masked:
                seen = key_positions(s, natural, key_run, length, tile, half, blocks) <= at
            new = []
            for head in range(heads):
                top, total, acc = state[head]
                scores = nn(k, q[head])
                if masked:
                    scores = jnp.where(seen, scores, NEG_FILL)
                best = jnp.maximum(top, jnp.max(fold_rows(scores, jnp.max), 0, keepdims=True))
                p = jnp.exp(scores - best)
                scale = jnp.exp(top - best)
                total = total * scale + jnp.sum(fold_rows(p, jnp.sum), 0, keepdims=True)
                new.append((best, total, acc * scale + tn(v, p.astype(BF))))
            return tuple(new)

        start = tuple(
            (
                jnp.full((1, rows), NEG_FILL, F32),
                jnp.zeros((1, rows), F32),
                jnp.zeros((width, rows), F32),
            )
            for _ in range(heads)
        )
        done = slab_loops(s, length, run, tile, blocks, start, step)
        for head in range(heads):
            top, total, acc = done[head]
            lse_ref[0, run, head] = top + jnp.log(total)
            out = acc[head * HEAD_SIZE : (head + 1) * HEAD_SIZE] / total
            first = head * SHARED * HEAD_SIZE
            o_ref[:, 0, run, :, first : first + SHARED * HEAD_SIZE] = (
                heads_back(out, tile).astype(BF).reshape(H, half, SHARED * HEAD_SIZE)
            )


def backward_kernel(
    s, q_ref, ke_ref, ko_ref, o_ref, lse_ref, cos_ref, sin_ref, *refs, heads
):
    H, _, _, half, QD = q_ref.shape
    dq_ref, de_ref, dod_ref, acc_ref, do_ref = refs[H:]
    for k in range(H):
        do_ref[before(s, k, H), 0] = refs[k][0]
    blocks = 2 * ke_ref.shape[0]
    tile = H * half
    width = heads * HEAD_SIZE
    rows = SHARED * tile
    length = s[2 + pl.program_id(0)]
    acc_ref[...] = jnp.zeros(acc_ref.shape, F32)
    for run in range(2):
        q, do, lse, delta = [], [], [], []
        for head in range(heads):
            q.append(padded(heads_across(q_ref, run, head, heads), head, heads))
            up = heads_across(do_ref, run, head, heads)
            do.append(padded(up, head, heads))
            delta.append(
                jnp.sum(up * heads_across(o_ref, run, head, heads), 0, keepdims=True)
            )
            lse.append(lse_ref[0, run, head])
        at = query_positions(s, run, rows, tile, half, blocks)

        def step(state, natural, key_run, masked, q=q, do=do, lse=lse, delta=delta, at=at):
            y = natural ^ (s[0] >> 2)
            k = slab(ke_ref, ko_ref, y, key_run, 0, width)
            v = slab(ke_ref, ko_ref, y, key_run, width, 2 * width)
            if masked:
                seen = key_positions(s, natural, key_run, length, tile, half, blocks) <= at
            new = []
            dk = jnp.zeros((4 * tile, width), F32)
            dv = jnp.zeros((4 * tile, width), F32)
            for head in range(heads):
                p = jnp.exp(nn(k, q[head]) - lse[head])
                if masked:
                    p = jnp.where(seen, p, 0.0)
                ds = (p * (nn(v, do[head]) - delta[head])).astype(BF)
                dk = dk + nt(ds, q[head])
                dv = dv + nt(p.astype(BF), do[head])
                new.append(state[head] + tn(k, ds))
            acc_ref[key_run, y, :, :width] += dk
            acc_ref[key_run, y, :, width:] += dv
            return tuple(new)

        start = tuple(jnp.zeros((width, rows), F32) for _ in range(heads))
        done = slab_loops(s, length, run, tile, blocks, start, step)
        cosine = cos_ref[:, run].reshape(tile, LANES)
        sine = sin_ref[:, run].reshape(tile, LANES)
        for head in range(heads):
            out = done[head][head * HEAD_SIZE : (head + 1) * HEAD_SIZE]
            out = (heads_back(out, tile) * SCORE_SCALE).astype(BF).astype(F32)
            for lanes in range(0, SHARED * HEAD_SIZE, LANES):
                part = out[:, lanes : lanes + LANES]
                part = part * cosine - turned(part) * sine
                first = head * SHARED * HEAD_SIZE + lanes
                dq_ref[:, 0, run, :, first : first + LANES] = part.astype(BF).reshape(
                    H, half, LANES
                )
    for run in range(2):
        for y in range(blocks // 4):
            for index, (ref, i) in enumerate(((de_ref, 0), (de_ref, 1), (dod_ref, 0), (dod_ref, 1))):
                ref[2 * y + i, :, 0, run] = (
                    acc_ref[run, y, index * tile : (index + 1) * tile]
                    .astype(BF)
                    .reshape(H, half, 2 * width)
                )


def attention_specs(q, kv, heads):
    H, M, _, half, QD = q.shape
    places, _, _, _, _, width = kv.shape
    per_q = pl.BlockSpec((H, 1, 2, half, QD), lambda m, s: (0, m, 0, 0, 0))
    per_kv = pl.BlockSpec((places, H, 1, 2, half, width), lambda m, s: (0, 0, m, 0, 0, 0))
    per_row = pl.BlockSpec((1, 2, heads, 1, SHARED * H * half), lambda m, s: (m, 0, 0, 0, 0))
    work = M * places * H * half * SHARED * H * half * QD
    return per_q, per_kv, per_row, work


def attention_forward(scalars, q, k_even, k_odd, heads, wait):
    H, M, _, half, QD = q.shape
    per_q, per_kv, per_row, work = attention_specs(q, k_even, heads)
    return call(
        functools.partial(forward_kernel, heads=heads),
        (M,),
        [per_q, per_kv, per_kv],
        [per_q, per_row],
        [shape_of(q.shape, BF), shape_of((M, 2, heads, 1, SHARED * H * half), F32)],
        [],
        8 * work,
        2 * (2 * q.size + 2 * k_even.size),
        (scalars, q, k_even, k_odd),
        wait,
    )


def attention_backward(scalars, q, k_even, k_odd, do_parts, o, lse, cosine, sine, heads, wait):
    H, M, _, half, QD = q.shape
    per_q, per_kv, per_row, work = attention_specs(q, k_even, heads)
    blocks = 2 * k_even.shape[0]
    return call(
        functools.partial(backward_kernel, heads=heads),
        (M,),
        [per_q, per_kv, per_kv, per_q, per_row, whole(cosine.shape), whole(sine.shape)]
        + [pl.BlockSpec((1, 2, half, QD), lambda m, s: (m, 0, 0, 0))] * H,
        [per_q, per_kv, per_kv],
        [shape_of(q.shape, BF), shape_of(k_even.shape, BF), shape_of(k_odd.shape, BF)],
        [
            pltpu.VMEM((2, blocks // 4, 4 * H * half, 2 * heads * HEAD_SIZE), F32),
            pltpu.VMEM((H, 1, 2, half, QD), BF),
        ],
        20 * work,
        2 * (4 * q.size + 4 * k_even.size),
        (scalars, q, k_even, k_odd, o, lse, cosine, sine, *do_parts),
        wait,
    )


def out_kernel(s, x_ref, gain_ref, we_ref, wo_ref, *refs):
    devices = len(refs) - 5
    xn_ref, own_ref, o_own_ref, acc_ref, o_ref = refs[devices:]
    n = pl.program_id(0)
    _, group, QD = o_ref.shape
    places, width, columns = we_ref.shape
    each = QD // width
    rows = group // devices

    @pl.when(n == 0)
    def _():
        for k in range(devices):
            o_ref[before(s, k, devices)] = refs[k][...]
        at = pl.ds(pl.multiple_of(s[1] * rows, rows), rows)
        for h in range(devices):
            o_own_ref[:, h * QD : (h + 1) * QD] = o_ref[h, at, :]

    got = jnp.zeros((group, columns), F32)
    for place in range(places):
        for parity, w_ref in enumerate((we_ref, wo_ref)):
            c = s[0] ^ (2 * place + parity)
            lanes = pl.ds(pl.multiple_of((c % each) * width, LANES), width)
            got = got + nn(o_ref[c // each, :, lanes], w_ref[place])
    acc_ref[:, pl.ds(pl.multiple_of(n * columns, LANES), columns)] = got

    @pl.when(n == pl.num_programs(0) - 1)
    def _():
        def finish(h, carry):
            at = pl.ds(pl.multiple_of(h * rows, rows), rows)
            resid = x_ref[at, :].astype(F32) + RESIDUAL_SCALE * acc_ref[at, :]
            inverse = lax.rsqrt(jnp.mean(resid * resid, -1, keepdims=True) + EPSILON)
            xn_ref[at, :] = ((resid * inverse) * gain_ref[1:2, :]).astype(BF)

            @pl.when(h == s[1])
            def _():
                own_ref[...] = resid

            return carry

        lax.fori_loop(0, devices, finish, 0)


def out_project(scalars, o_parts, x, gains, w_even, w_odd, wait):
    H = len(o_parts)
    group, QD = o_parts[0].shape
    places, width, D = w_even.shape
    rows = group // H
    columns = 512
    piece = pl.BlockSpec((places, width, columns), lambda n, s: (0, 0, n))
    return call(
        out_kernel,
        (D // columns,),
        [whole(x.shape), whole(gains.shape), piece, piece] + [whole((group, QD))] * H,
        [whole((group, D)), whole((rows, D)), whole((rows, H * QD))],
        [shape_of((group, D), BF), shape_of((rows, D), F32), shape_of((rows, H * QD), BF)],
        [pltpu.VMEM((group, D), F32), pltpu.VMEM((H, group, QD), BF)],
        2 * group * H * QD * D,
        2 * (H * group * QD + 2 * x.size + 2 * w_even.size),
        (scalars, x, gains, w_even, w_odd, *o_parts),
        wait,
    )


def mlp_forward_kernel(s, xn_ref, wg_ref, wu_ref, gate_ref, up_ref, hidden_ref):
    gate = nn(xn_ref[...], wg_ref[...])
    up = nn(xn_ref[...], wu_ref[...])
    gate_ref[...] = gate
    up_ref[...] = up
    hidden_ref[...] = (gate * (1.0 / (1.0 + jnp.exp(-gate))) * up).astype(BF)


def mlp_forward(scalars, xn, w_gate_up, tile, wait):
    group, D = xn.shape
    F = w_gate_up.shape[1] // 2
    count = F // tile
    out = pl.BlockSpec((group, tile), lambda f, s: (0, f))
    return call(
        mlp_forward_kernel,
        (count,),
        [
            whole(xn.shape),
            pl.BlockSpec((D, tile), lambda f, s: (0, f)),
            pl.BlockSpec((D, tile), lambda f, s: (0, f + count)),
        ],
        [out, out, out],
        [shape_of((group, F), F32), shape_of((group, F), F32), shape_of((group, F), BF)],
        [],
        4 * group * D * F,
        2 * (group * D + 2 * D * F + 5 * group * F),
        (scalars, xn, w_gate_up, w_gate_up),
        wait,
    )


def down_kernel(s, hidden_ref, w_ref, out_ref):
    out_ref[...] = nn(hidden_ref[...], w_ref[...]).astype(BF)


def down_project(scalars, hidden, w_down, wait):
    group, F = hidden.shape
    D = w_down.shape[1]
    width = 512
    return call(
        down_kernel,
        (D // width,),
        [whole(hidden.shape), pl.BlockSpec((F, width), lambda n, s: (0, n))],
        [pl.BlockSpec((group, width), lambda n, s: (0, n))],
        [shape_of((group, D), BF)],
        [],
        2 * group * D * F,
        2 * (group * D + D * F + group * F),
        (scalars, hidden, w_down),
        wait,
    )[0]


def mlp_backward_kernel(
    s, gate_ref, up_ref, wg_ref, wu_ref, wd_ref, dmo_ref, dg_ref, du_ref, dxn_ref, acc_ref
):
    f = pl.program_id(0)
    d_hidden = nt(dmo_ref[...], wd_ref[...])
    gate = gate_ref[...]
    sigma = 1.0 / (1.0 + jnp.exp(-gate))
    dg_ref[...] = (d_hidden * up_ref[...] * (sigma * (1.0 + gate * (1.0 - sigma)))).astype(BF)
    du_ref[...] = (d_hidden * (gate * sigma)).astype(BF)
    got = nt(dg_ref[...], wg_ref[...]) + nt(du_ref[...], wu_ref[...])

    @pl.when(f == 0)
    def _():
        acc_ref[...] = got

    @pl.when(f > 0)
    def _():
        acc_ref[...] += got

    @pl.when(f == pl.num_programs(0) - 1)
    def _():
        dxn_ref[...] = acc_ref[...].astype(BF)


def mlp_backward(scalars, gate, up, dmo, w_gate_up, w_down, tile, wait):
    group, D = dmo.shape
    F = gate.shape[1]
    count = F // tile
    per_f = pl.BlockSpec((group, tile), lambda f, s: (0, f))
    return call(
        mlp_backward_kernel,
        (count,),
        [
            per_f,
            per_f,
            pl.BlockSpec((D, tile), lambda f, s: (0, f)),
            pl.BlockSpec((D, tile), lambda f, s: (0, f + count)),
            pl.BlockSpec((tile, D), lambda f, s: (f, 0)),
            whole((group, D)),
        ],
        [per_f, per_f, whole((group, D))],
        [shape_of((group, F), BF), shape_of((group, F), BF), shape_of((group, D), BF)],
        [pltpu.VMEM((group, D), F32)],
        6 * group * D * F,
        2 * (3 * group * D + 3 * D * F + 6 * group * F),
        (scalars, gate, up, w_gate_up, w_gate_up, w_down, dmo),
        wait,
    )


def block_lanes(s, own, near, block):
    i = pl.program_id(0)
    if near:
        index = s[0] ^ (2 * i if own else 2 * i + 1)
    else:
        index = 2 * i + (s[0] % 2 if own else 1 - s[0] % 2)
    return pl.ds(pl.multiple_of(index * block, LANES), block)


def rows_kernel(s, left_ref, *refs, own, count, near):
    right = refs[:count]
    out_ref = refs[-1]
    block = out_ref.shape[0]
    lanes = block_lanes(s, own, near, block)
    left = left_ref[:, lanes]
    at = 0
    for i, right_ref in enumerate(right):
        width = right_ref.shape[1]
        got = tn(left, right_ref[...])
        if own:
            got = got + refs[count][:, at : at + width].astype(F32)
        out_ref[:, at : at + width] = got.astype(BF)
        at += width


def grad_rows(scalars, left, rights, blocks, came=None, near=False, wait=()):
    n, D = left.shape
    block = D // blocks
    width = sum(r.shape[1] for r in rights)
    piece = pl.BlockSpec((block, width), lambda i, s: (i, 0))
    extra = [] if came is None else [came]
    return call(
        functools.partial(
            rows_kernel, own=came is not None, count=len(rights), near=near
        ),
        (blocks // 2,),
        [whole(left.shape)] + [whole(r.shape) for r in rights] + [piece] * len(extra),
        [piece],
        [shape_of((D // 2, width), BF)],
        [],
        n * D * width,
        2 * (left.size + n * width + D * width),
        (scalars, left, *rights, *extra),
        wait,
    )[0]


def columns_kernel(s, left_ref, right_ref, *refs, own):
    out_ref = refs[-1]
    got = tn(left_ref[...], right_ref[:, block_lanes(s, own, True, out_ref.shape[2])])
    if own:
        got = got + refs[0][0].astype(F32)
    out_ref[0] = got.astype(BF)


def grad_columns(scalars, left, right, blocks, came=None, wait=()):
    n, F = left.shape
    D = right.shape[1]
    block = D // blocks
    piece = pl.BlockSpec((1, F, block), lambda i, s: (i, 0, 0))
    extra = [] if came is None else [came]
    return call(
        functools.partial(columns_kernel, own=came is not None),
        (blocks // 2,),
        [whole(left.shape), whole(right.shape)] + [piece] * len(extra),
        [piece],
        [shape_of((blocks // 2, F, block), BF)],
        [],
        n * D * F,
        2 * (left.size + right.size + D * F),
        (scalars, left, right, *extra),
        wait,
    )[0]


def through_norm(upstream, gain, values):
    inverse = lax.rsqrt(jnp.mean(values * values, -1, keepdims=True) + EPSILON)
    scaled = values * inverse
    through = upstream * gain
    inner = jnp.mean(through * scaled, -1, keepdims=True)
    return inverse * (through - scaled * inner), scaled


def branch_kernel(s, parts, resid_ref, up_ref, gain_ref, we_ref, wo_ref, *refs):
    devices = len(refs) - 4
    dresid_ref, da_ref, gg_ref = refs[:3]
    outs = refs[3:-1]
    dattn_ref = refs[-1]
    p = pl.program_id(0)
    _, tokens, QD = dattn_ref.shape
    width = we_ref.shape[1]
    each = QD // width

    @pl.when(p == 0)
    def _():
        upstream = parts[0].astype(F32)
        for h in range(1, parts.shape[0]):
            upstream = upstream + parts[h].astype(F32)
        back, scaled = through_norm(upstream, gain_ref[1:2, :], resid_ref[...])
        gg_ref[...] = jnp.broadcast_to(
            jnp.sum(upstream * scaled, 0, keepdims=True), gg_ref.shape
        )
        d_resid = up_ref[...].astype(F32) + back
        dresid_ref[...] = d_resid
        da_ref[...] = (RESIDUAL_SCALE * d_resid).astype(BF)

    for parity, w_ref in enumerate((we_ref, wo_ref)):
        c = s[0] ^ (2 * p + parity)
        dattn_ref[c // each, :, pl.ds(pl.multiple_of((c % each) * width, LANES), width)] = nt(
            da_ref[...], w_ref[0]
        ).astype(BF)

    @pl.when(p == pl.num_programs(0) - 1)
    def _():
        for k in range(devices):
            outs[k][...] = dattn_ref[after(s, k, devices)]


def branch_back(scalars, parts, resid, upstream, gains, w_even, w_odd, QD, H, wait):
    _, tokens, D = parts.shape
    places, width, _ = w_even.shape
    piece = pl.BlockSpec((1, width, D), lambda p, s: (p, 0, 0))
    return call(
        branch_kernel,
        (places,),
        [whole(a.shape) for a in (parts, resid, upstream, gains)] + [piece, piece],
        [whole((tokens, D)), whole((tokens, D)), whole((8, D))] + [whole((tokens, QD))] * H,
        [shape_of((tokens, D), F32), shape_of((tokens, D), BF), shape_of((8, D), F32)]
        + [shape_of((tokens, QD), BF)] * H,
        [pltpu.VMEM((H, tokens, QD), BF)],
        2 * tokens * D * H * QD,
        2 * (H * tokens * D + 2 * w_even.size + 6 * tokens * D),
        (scalars, parts, resid, upstream, gains, w_even, w_odd),
        wait,
    )


def input_kernel(
    s, dq_ref, dkv_ref, cos_ref, sin_ref, x_ref, xn_ref, gg_ref, we_ref, wo_ref, *refs
):
    out_ref, ge_ref, go_ref, dqkv_ref, inv_ref = refs
    p = pl.program_id(0)
    group, QD = dq_ref.shape
    KD = dkv_ref.shape[1] // 2
    used = QD + 2 * KD
    block = we_ref.shape[1]

    @pl.when(p == 0)
    def _():
        dqkv_ref[:, :QD] = dq_ref[...]
        for first in range(0, 2 * KD, LANES):
            part = dkv_ref[:, first : first + LANES].astype(F32)
            if first < KD:
                part = rope_lanes(part, cos_ref[...], -sin_ref[...], first, KD)
            dqkv_ref[:, QD + first : QD + first + LANES] = part.astype(BF)
        x = x_ref[...].astype(F32)
        inv_ref[...] = jnp.broadcast_to(
            lax.rsqrt(jnp.mean(x * x, -1, keepdims=True) + EPSILON), inv_ref.shape
        )

    for parity, (w_ref, g_ref) in enumerate(((we_ref, ge_ref), (wo_ref, go_ref))):
        lanes = chunk(s, 2 * p + parity, block)
        dxn = nt(dqkv_ref[...], w_ref[0, :, :used])
        out_ref[:, lanes] = dxn.astype(BF)
        scaled = x_ref[:, lanes].astype(F32) * inv_ref[:, 0:1]
        gain_one = jnp.sum(dxn * scaled, 0, keepdims=True)
        g_ref[0, :, :used] = tn(xn_ref[:, lanes], dqkv_ref[...]).astype(BF)
        row = lax.broadcasted_iota(jnp.int32, (LANES, block), 0)
        both = jnp.where(row == 0, gain_one, jnp.where(row == 1, gg_ref[0:1, lanes], 0.0))
        g_ref[0, :, used:] = both.T.astype(BF)


def input_back(scalars, dq, dkv, cosine, sine, x, xn, gain_two, w_even, w_odd, wait):
    group, D = x.shape
    QD = dq.shape[1]
    places, block, columns = w_even.shape
    piece = pl.BlockSpec((1, block, columns), lambda p, s: (p, 0, 0))
    return call(
        input_kernel,
        (places,),
        [whole(a.shape) for a in (dq, dkv, cosine, sine, x, xn, gain_two)] + [piece, piece],
        [whole(x.shape), piece, piece],
        [shape_of(x.shape, BF), shape_of(w_even.shape, BF), shape_of(w_even.shape, BF)],
        [
            pltpu.VMEM((group, QD + dkv.shape[1]), BF),
            pltpu.VMEM((group, LANES), F32),
        ],
        4 * group * D * (QD + dkv.shape[1]),
        2 * (3 * x.size + 4 * w_even.size),
        (scalars, dq, dkv, cosine, sine, x, xn, gain_two, w_even, w_odd),
        wait,
    )


def body(
    inputs,
    cotangent,
    lengths,
    positions,
    attn_gain,
    mlp_gain,
    w_query,
    key_projection,
    value_projection,
    w_out,
    w_gate,
    w_up,
    w_down,
):
    B = lax.axis_size("blk")
    H = lax.axis_size("head")
    me = lax.axis_index("blk")
    mine = lax.axis_index("head")
    T = inputs.shape[1]
    D = MODEL_WIDTH
    half = T // 2
    slots = T * H * B
    heads = KEY_VALUE_HEADS // H
    KD = heads * HEAD_SIZE
    QD = KD * SHARED
    used = QD + 2 * KD
    tokens = MICRO * T
    group = H * tokens
    wrows = w_query.shape[0]
    F = w_gate.shape[1]
    block = D // B
    tile = min(512, F)

    scalars = jnp.concatenate(
        [jnp.stack([me, mine]).astype(jnp.int32), lengths.astype(jnp.int32)]
    )

    gains = jnp.concatenate(
        [attn_gain[:, None], mlp_gain[:, None], jnp.zeros((wrows, LANES - 2), BF)], 1
    )
    pack = pack_weights(scalars, w_query, key_projection, value_projection, gains, H)
    linear = me * H + mine
    my_pos = lax.dynamic_slice_in_dim(positions, linear * T, T, axis=1)
    place = jnp.where(
        my_pos < slots // 2, my_pos - half * linear, half + my_pos - (slots - half * (linear + 1))
    ).astype(jnp.int32)
    order = (place[:, None, :] == jnp.arange(T)[None, :, None]).astype(BF)
    pack = arrange(scalars, head_deal(pack, H)).reshape(H * wrows, used + LANES)
    x_copies, upstream = in_order(scalars, inputs, cotangent, place, H, [pack])
    x_own = x_copies[0]
    x = head_exchange(x_copies)
    qkv_even, qkv_odd = xor_gather(pack, B)

    w_out_rows = lax.all_gather(w_out, "head", axis=0, tiled=True)
    w_gate_up = lax.all_gather(jnp.concatenate([w_gate, w_up], 1), "blk", axis=0, tiled=True)
    w_d = lax.all_gather(w_down, "blk", axis=1, tiled=True)
    dmo_copies = copies(scalars, upstream, H, RESIDUAL_SCALE, [x])
    dmo = head_exchange(dmo_copies).reshape(group, D)

    run_start = jnp.arange(H)[:, None, None] + me * H
    i = jnp.arange(half)[None, None, :]
    row_pos = jnp.concatenate([half * run_start + i, slots - half * (run_start + 1) + i], 1)
    half_dim = HEAD_SIZE // 2
    frequency = ROPE_BASE ** (-(jnp.arange(half_dim).astype(F32) * 2.0) / HEAD_SIZE)
    angles = row_pos.reshape(H * T, 1).astype(F32) * frequency[None, :]
    cosine = jnp.cos(angles)
    sine = jnp.sin(angles)
    cosine = jnp.concatenate([cosine] * 4, 1)
    sine = jnp.concatenate([-sine, sine] * 2, 1)

    def per_group(table):
        return jnp.broadcast_to(
            table.reshape(H, 1, T, LANES), (H, MICRO, T, LANES)
        ).reshape(group, LANES)

    xn1, q, kv, gain_rows = project(
        scalars,
        x.reshape(H, MICRO, T, D),
        qkv_even,
        qkv_odd,
        cosine,
        sine,
        QD,
        KD,
        [dmo_copies],
    )
    x = x.reshape(group, D)
    runs = (H, MICRO, 2, half)
    q = q.reshape(runs + (QD,))
    kv_even, kv_odd = xor_gather(kv.reshape(group, 2 * KD), B)
    kv_even = kv_even.reshape((B // 2,) + runs + (2 * KD,))
    kv_odd = kv_odd.reshape((B // 2,) + runs + (2 * KD,))
    w_out_rows = hold(scalars, [w_out_rows], [kv_odd])[0]
    o, lse = attention_forward(scalars, q, kv_even, kv_odd, heads, [w_out_rows])
    o_parts = head_gather(o.reshape(group, QD), H)
    out_even, out_odd = xor_gather(
        w_out_rows, B, lambda parts: join(scalars, parts, [o_parts[1], dmo])
    )
    xn2, resid, o_own = out_project(
        scalars, o_parts, x, gain_rows, out_even, out_odd, [dmo]
    )
    gate, up, hidden = mlp_forward(scalars, xn2, w_gate_up, tile, ())
    d_gate, d_up, d_xn2 = mlp_backward(scalars, gate, up, dmo, w_gate_up, w_d, tile, ())
    d_xn2 = lax.psum_scatter(d_xn2, "head", scatter_dimension=0, tiled=True)[None]

    came = swap(grad_rows(scalars, xn2, (d_gate, d_up), B), 1, B)
    came_down = swap(grad_columns(scalars, hidden, dmo, B), 1, B)
    sum_gate_up = grad_rows(scalars, xn2, (d_gate, d_up), B, came)
    grad_gate_up = plane_scatter(sum_gate_up, B, 0)
    sum_down = grad_columns(scalars, hidden, dmo, B, came_down, [sum_gate_up])
    grad_down = core_scatter_steps(sum_down, B)

    d_resid, d_branch, gain_two, *d_attn = branch_back(
        scalars,
        d_xn2,
        resid,
        upstream,
        gain_rows,
        out_even,
        out_odd,
        QD,
        H,
        [sum_gate_up],
    )
    mlp_out = down_project(scalars, hidden, w_d, [d_branch])
    d_attn = head_deal(d_attn, H)
    mlp_held = hold(scalars, [mlp_out], d_attn[1:])[0]
    mlp_out = head_exchange(mlp_held.reshape(H, tokens, D))
    d_attn = [part.reshape(MICRO, 2, half, QD) for part in d_attn]
    tables = (H, 2, half, LANES)
    dq, dkv_even, dkv_odd = attention_backward(
        scalars, q, kv_even, kv_odd, d_attn, o, lse, cosine.reshape(tables), sine.reshape(tables), heads,
        [sum_down, mlp_held],
    )
    out_away = grad_rows(scalars, o_own, (d_branch,), B, near=True, wait=[dq])
    sum_out = grad_rows(
        scalars, o_own, (d_branch,), B, came=swap(out_away, 1, B), near=True
    ).reshape(B // 2, block, D)

    def by_distance(values):
        values = values.astype(BF).reshape(H, wrows, -1)
        return head_deal(
            [lax.dynamic_index_in_dim(values, (mine + k) % H, 0, False) for k in range(H)], H
        )

    grad_out = by_distance(core_scatter_steps(sum_out, B))
    grad_out = sum(part.astype(F32) for part in grad_out)
    pieces = (B // 2, group, 2 * KD)
    dkv = xor_scatter(dkv_even.reshape(pieces), dkv_odd.reshape(pieces), B)
    d_xn1, grad_even, grad_odd = input_back(
        scalars,
        dq.reshape(group, QD),
        dkv,
        per_group(cosine),
        per_group(sine),
        x,
        xn1.reshape(group, D),
        gain_two,
        qkv_even,
        qkv_odd,
        [sum_out, mlp_out, grad_gate_up],
    )
    d_xn1 = lax.psum_scatter(d_xn1, "head", scatter_dimension=0, tiled=True)
    grad_gate_up = wide(scalars, grad_gate_up, [d_xn1])
    grad_qkv = arrange(scalars, by_distance(xor_scatter(grad_even, grad_odd, B))).astype(F32)
    grad_gains = jnp.sum(grad_qkv[:, :, used : used + 2], 0)

    def side_by_side(values):
        return values.transpose(1, 0, 2).reshape(wrows, -1)

    output = (resid + RESIDUAL_SCALE * jnp.sum(mlp_out.astype(F32), 0)).astype(BF)
    output = jnp.einsum(
        "mrs,mrd->msd", order, output.reshape(MICRO, T, D), preferred_element_type=F32
    ).astype(BF)
    back, _ = through_norm(d_xn1.astype(F32), gain_rows[0:1], x_own.astype(F32))
    d_input = jnp.einsum(
        "mrs,mrd->msd",
        order.astype(F32),
        (d_resid + back).reshape(MICRO, T, D),
        precision=lax.Precision.HIGHEST,
        preferred_element_type=F32,
    )
    return (
        output,
        d_input,
        grad_gains[:, 0],
        grad_gains[:, 1],
        side_by_side(grad_qkv[:, :, :QD]),
        side_by_side(grad_qkv[:, :, QD : QD + KD]),
        side_by_side(grad_qkv[:, :, QD + KD : used]),
        grad_out,
        grad_gate_up[:, :F],
        grad_gate_up[:, F:],
        grad_down,
    )


def solution(mesh):
    both = ("blk", "head")
    return jax.shard_map(
        body,
        mesh=mesh,
        in_specs=(
            P(None, both, None),
            P(None, both, None),
            P(),
            P(),
            P(both),
            P(both),
            P(both, None),
            P(both, None),
            P(both, None),
            P(both, None),
            P("blk", "head"),
            P("blk", "head"),
            P("head", "blk"),
        ),
        out_specs=(
            P(None, both, None),
            P(None, both, None),
            P(both),
            P(both),
            P(both, None),
            P(both, None),
            P(both, None),
            P(both, None),
            P("blk", "head"),
            P("blk", "head"),
            P("head", "blk"),
        ),
        check_vma=False,
    )
```

time: 794 us -> 647 us (0.81)
  local copies, waits for them, and re-layouts: 179 us -> 25.8 us
  Pallas kernels: 60.6 us -> 207 us
  matrix products: 136 us -> 2.77 us
  waiting for transfers between devices: 225 us -> 274 us
  other arithmetic: 70.9 us -> 39.5 us
  blocking collectives: 31.1 us -> 0 us
  starting transfers between devices: 59.9 us -> 73.1 us
    pallas_call x2 -> x24, Pallas kernels: 60.6 us -> 207 us  [call(): pl.pallas_call(run, grid_spec=pltpu.PrefetchScalarGridSpec(num_scalar_pre...]
    dot_general x36 -> x1, matrix products: 135 us -> 1.63 us  [body(): jnp.einsum('mrs,mrd->msd', order.astype(F32), (d_resid + back).reshape(MI...]
    ppermute x1 -> x15, waiting for transfers between devices: 0.01 us -> 66.2 us  [head_shift(): lax.ppermute(x, 'head', [(i, (i + by) % devices) for i in range(devices)])]
    dynamic_update_slice x27 -> x0, local copies, waits for them, and re-layouts: 38.4 us -> none  [natural(): lax.dynamic_update_slice_in_dim(whole, piece, (me ^ j) * block, axis)]
    all_to_all x1 -> x0, blocking collectives: 31.1 us -> none  [body(): pack = lax.all_to_all(pack, 'head', split_axis=0, concat_axis=0, tiled=True)]
    unnamed x164 -> x78, local copies, waits for them, and re-layouts: 37.6 us -> 10.7 us
    reshape x13 -> x0, local copies, waits for them, and re-layouts: 26.6 us -> none  [the longest x2 14.5 us: from_heads(): values = values.reshape(MICRO, 2, SHARED, H, half, heads, HEAD_SIZE)]
    ppermute x1 -> x15, starting transfers between devices: 0.68 us -> 24.7 us  [head_shift(): lax.ppermute(x, 'head', [(i, (i + by) % devices) for i in range(devices)])]
  transfers between devices with their start and end apart: 53 -> 55, of which waited for: 16 -> 27; matrix products, arithmetic and copies ran while one was open for 41% -> 8% of each run, Pallas kernels for 8% -> 26%
where the time goes in v2:
time: 647 us; the launch traced here: 637 us
  waiting for transfers between devices  274 us (42%)
  Pallas kernels  207 us (32%)
  starting transfers between devices  73.1 us (11%)
  other arithmetic  39.5 us (6%)
  local copies, waits for them, and re-layouts  25.8 us (4%)
  between operations  15 us (2%)
    pallas_call x24, Pallas kernels, call(): pl.pallas_call(run, grid_spec=pltpu.PrefetchScalarGridSpec(num_scalar_pre...  207 us
    ppermute x31, waiting for transfers between devices, swap(): return lax.ppermute(x, 'blk', [(i, i ^ bit) for i in range(devices)])  178 us
    ppermute x15, waiting for transfers between devices, head_shift(): lax.ppermute(x, 'head', [(i, (i + by) % devices) for i in range(devices)])  66.2 us
    ppermute x31, starting transfers between devices, swap(): return lax.ppermute(x, 'blk', [(i, i ^ bit) for i in range(devices)])  29.7 us
    ppermute x15, starting transfers between devices, head_shift(): lax.ppermute(x, 'head', [(i, (i + by) % devices) for i in range(devices)])  24.7 us
    reduce_scatter x1, waiting for transfers between devices, body(): lax.psum_scatter(d_xn2, 'head', scatter_dimension=0, tiled=True)[None]  20.2 us
    all_to_all x3, starting transfers between devices, head_exchange(): lax.all_to_all(parts, 'head', split_axis=0, concat_axis=0, tiled=True)  18.2 us
  transfers between devices with their start and end apart: 55, of which 27 were waited for; matrix products, arithmetic and copies ran while one was open for 8% of the time, Pallas kernels for 26%

profile of v2, /device:TPU:0, one launch (start us, length us, event | category | flops | bytes accessed | tf_op | source)
XLA Modules:
  0.0 637.4 jit_solution(12999873818403739880)
XLA Ops:
  26.2 8.5 %collective-permute-done.1.refs_3_ = bf16[64,896]{1,0:T(8,128)(2,1)S(1)} collective-permute-done((bf16[64,896]{1,0:T(8,128)(2,1)}, bf16[64,896]{1,0:T(8,128)(2,1)S(1)}, u32[]{:S(2)}, u32[]{:S(2)}) %collective-permute-start.1) | collective-permute-done | bytes 114720 | tf_op jit(solution)/shard_map/ppermute | solution.py:88
  42.1 10.9 %all-to-all-start = ((bf16[4,128,2048]{2,1,0:T(8,128)(2,1)}), bf16[4,128,2048]{2,1,0:T(8,128)(2,1)S(1)}, u32[]{:S(2)}, u32[]{:S(2)}) async-start(bf16[4,128,2048]{2,1,0:T(8,128)(2,1)} %get-tuple-element.49), calls=%async_computation | async-start | bytes 4194304 | tf_op jit(solution)/shard_map/all_to_all | solution.py:84
  56.4 16.5 %collective-permute-done.5 = bf16[256,896]{1,0:T(8,128)(2,1)S(1)} collective-permute-done((bf16[256,896]{1,0:T(8,128)(2,1)S(1)}, bf16[256,896]{1,0:T(8,128)(2,1)S(1)}, u32[]{:S(2)}, u32[]{:S(2)}) %collective-permute-start.5) | collective-permute-done | bytes 458784 | tf_op jit(solution)/shard_map/ppermute | solution.py:47
  72.9 10.5 %collective-permute-done.4 = bf16[256,896]{1,0:T(8,128)(2,1)S(1)} collective-permute-done((bf16[256,896]{1,0:T(8,128)(2,1)S(1)}, bf16[256,896]{1,0:T(8,128)(2,1)S(1)}, u32[]{:S(2)}, u32[]{:S(2)}) %collective-permute-start.4) | collective-permute-done | bytes 458784 | tf_op jit(solution)/shard_map/ppermute | solution.py:47
  121.8 12.4 %collective-permute-done.9 = bf16[512,256]{1,0:T(8,128)(2,1)S(1)} collective-permute-done((bf16[512,256]{1,0:T(8,128)(2,1)}, bf16[512,256]{1,0:T(8,128)(2,1)S(1)}, u32[]{:S(2)}, u32[]{:S(2)}) %collective-permute-start.9) | collective-permute-done | bytes 262176 | tf_op jit(solution)/shard_map/ppermute | solution.py:47
  158.5 14.7 %shard_map.218 = (bf16[4,2,2,32,512]{4,3,2,1,0:T(8,128)(2,1)}, f32[2,2,2,1,512]{4,3,2,1,0:T(1,128)}) custom-call(s32[4]{0:T(128)} %pad_add_fusion.refs_0_, bf16[4,2,2,32,512]{4,3,2,1,0:T(8,128)(2,1)} %bitcast.161, bf16[4,4,2,2,32,256]{5,4,3,2,1,0:T(8,128)(2,1)} %pad_maximum_fusion.3.refs_2_, bf16[4,4,2,2,32,256]{5,4,3,2,1,0:T(8,128)(2,1)} %bitcast.146, ...), custom_call_target="tpu_custom_call" | custom-call | flops 214748368 | bytes 314572 | tf_op jit(solution)/shard_map/pallas_call | solution.py:122
  175.0 13.4 %collective-permute-done.14.refs_5_.refs_6_ = bf16[512,512]{1,0:T(8,128)(2,1)S(1)} collective-permute-done((bf16[512,512]{1,0:T(8,128)(2,1)}, bf16[512,512]{1,0:T(8,128)(2,1)S(1)}, u32[]{:S(2)}, u32[]{:S(2)}) %collective-permute-start.14) | collective-permute-done | bytes 524320 | tf_op jit(solution)/shard_map/ppermute | solution.py:88
  190.5 27.6 %collective-permute-done.13.refs_4_ = bf16[256,2048]{1,0:T(8,128)(2,1)} collective-permute-done((bf16[256,2048]{1,0:T(8,128)(2,1)}, bf16[256,2048]{1,0:T(8,128)(2,1)}, u32[]{:S(2)}, u32[]{:S(2)}) %collective-permute-start.13) | collective-permute-done | bytes 1048608 | tf_op jit(solution)/shard_map/ppermute | solution.py:47
  229.1 22.8 %collective-permute-done.16.refs_7_ = bf16[512,512]{1,0:T(8,128)(2,1)S(1)} collective-permute-done((bf16[512,512]{1,0:T(8,128)(2,1)S(1)}, bf16[512,512]{1,0:T(8,128)(2,1)S(1)}, u32[]{:S(2)}, u32[]{:S(2)}) %collective-permute-start.16) | collective-permute-done | bytes 524320 | tf_op jit(solution)/shard_map/ppermute | solution.py:88
  254.1 12.3 %shard_map.220 = (bf16[512,2048]{1,0:T(8,128)(2,1)}, f32[128,2048]{1,0:T(8,128)}, bf16[128,2048]{1,0:T(8,128)(2,1)}) custom-call(s32[4]{0:T(128)} %pad_add_fusion.refs_0_, bf16[512,2048]{1,0:T(8,128)(2,1)} %bitcast.142, f32[8,2048]{1,0:T(8,128)} %get-tuple-element.51.refs_2_.refs_4_, bf16[4,256,2048]{2,1,0:T(8,128)(2,1)} %shard_map.219.refs_3_.refs_5_, ...), custom_call_target="tpu_custom_call" | custom-call | flops 429496736 | bytes 1468006 | tf_op jit(solution)/shard_map/pallas_call | solution.py:122
  266.4 15.7 %shard_map.221 = (f32[512,2048]{1,0:T(8,128)}, f32[512,2048]{1,0:T(8,128)}, bf16[512,2048]{1,0:T(8,128)(2,1)}) custom-call(s32[4]{0:T(128)} %pad_add_fusion.refs_0_, bf16[512,2048]{1,0:T(8,128)(2,1)} %get-tuple-element.56.refs_1_, bf16[2048,4096]{1,0:T(8,128)(2,1)} %all-gather.6.cloned.1.call-done.refs_2_.refs_3_.refs_4_, ...), custom_call_target="tpu_custom_call" | custom-call | flops 858993472 | bytes 2936012 | tf_op jit(solution)/shard_map/pallas_call | solution.py:122
  282.1 24.5 %shard_map.222 = (bf16[512,2048]{1,0:T(8,128)(2,1)}, bf16[512,2048]{1,0:T(8,128)(2,1)}, bf16[512,2048]{1,0:T(8,128)(2,1)}) custom-call(s32[4]{0:T(128)} %pad_add_fusion.refs_0_, f32[512,2048]{1,0:T(8,128)} %get-tuple-element.58.refs_1_, f32[512,2048]{1,0:T(8,128)} %get-tuple-element.59.refs_2_, ...), custom_call_target="tpu_custom_call" | custom-call | flops 1288490240 | bytes 4404019 | tf_op jit(solution)/shard_map/pallas_call | solution.py:122
  306.6 10.2 %shard_map.223 = bf16[1024,4096]{1,0:T(8,128)(2,1)} custom-call(s32[4]{0:T(128)} %pad_add_fusion.refs_0_, bf16[512,2048]{1,0:T(8,128)(2,1)} %get-tuple-element.56.refs_1_, bf16[512,2048]{1,0:T(8,128)(2,1)} %get-tuple-element.61.refs_2_, bf16[512,2048]{1,0:T(8,128)(2,1)} %get-tuple-element.62.refs_3_), custom_call_target="tpu_custom_call" | custom-call | flops 429496736 | bytes 2306867 | tf_op jit(solution)/shard_map/pallas_call | solution.py:122
  316.9 13.4 %collective-permute-done.18.refs_4_ = bf16[1024,4096]{1,0:T(8,128)(2,1)} collective-permute-done((bf16[1024,4096]{1,0:T(8,128)(2,1)}, bf16[1024,4096]{1,0:T(8,128)(2,1)}, u32[]{:S(2)}, u32[]{:S(2)}) %collective-permute-start.18) | collective-permute-done | bytes 8388640 | tf_op jit(solution)/shard_map/ppermute | solution.py:47
  330.3 12.3 %shard_map.224.refs_7_.refs_4_ = bf16[1024,4096]{1,0:T(8,128)(2,1)} custom-call(s32[4]{0:T(128)} %pad_add_fusion.refs_0_, bf16[512,2048]{1,0:T(8,128)(2,1)} %get-tuple-element.56.refs_1_, bf16[512,2048]{1,0:T(8,128)(2,1)} %get-tuple-element.61.refs_2_, bf16[512,2048]{1,0:T(8,128)(2,1)} %get-tuple-element.62.refs_3_, ...), custom_call_target="tpu_custom_call" | custom-call | flops 429496736 | bytes 2306867 | tf_op jit(solution)/shard_map/pallas_call | solution.py:122
  351.4 20.2 %reduce-scatter.4.cloned.1.call-done = bf16[128,2048]{1,0:T(8,128)(2,1)} async-done(((bf16[512,2048]{1,0:T(8,128)(2,1)}), bf16[128,2048]{1,0:T(8,128)(2,1)}) %reduce-scatter.4.cloned.1.call-update) | async-done | bytes 524304 | tf_op jit(solution)/shard_map/reduce_scatter | solution.py:1116
  371.6 9.3 %shard_map.225 = (f32[128,2048]{1,0:T(8,128)}, bf16[128,2048]{1,0:T(8,128)(2,1)}, f32[8,2048]{1,0:T(8,128)}, bf16[128,512]{1,0:T(8,128)(2,1)}, bf16[128,512]{1,0...) custom-call(s32[4]{0:T(128)} %pad_add_fusion.refs_0_, bf16[1,128,2048]{2,1,0:T(8,128)(2,1)} %bitcast.182, ...), custom_call_target="tpu_custom_call" | custom-call | flops 107374184 | bytes 1363148 | tf_op jit(solution)/shard_map/pallas_call | solution.py:122
  395.0 9.7 %shard_map.226.refs_1_ = bf16[512,2048]{1,0:T(8,128)(2,1)} custom-call(s32[4]{0:T(128)} %pad_add_fusion.refs_0_, bf16[512,2048]{1,0:T(8,128)(2,1)} %get-tuple-element.57.refs_1_, bf16[2048,2048]{1,0:T(8,128)(2,1)} %all-gather.8.cloned.1.call-done.refs_5_.refs_2_, bf16[128,2048]{1,0:T(8,128)(2,1)} %get-tuple-element.63.refs_3_.refs_2_), custom_call_target="tpu_custom_call" | custom-call | flops 429496736 | bytes 1258291 | tf_op jit(solution)/shard_map/pallas_call | solution.py:122
  409.8 19.5 %shard_map.230 = (bf16[4,2,2,32,512]{4,3,2,1,0:T(8,128)(2,1)}, bf16[4,4,2,2,32,256]{5,4,3,2,1,0:T(8,128)(2,1)}, bf16[4,4,2,2,32,256]{5,4,3,2,1,0:T(8,128)(2,1)}) custom-call(s32[4]{0:T(128)} %pad_add_fusion.refs_0_, bf16[4,2,2,32,512]{4,3,2,1,0:T(8,128)(2,1)} %bitcast.162, bf16[4,4,2,2,32,256]{5,4,3,2,1,0:T(8,128)(2,1)} %pad_maximum_fusion.3.refs_2_, ...), custom_call_target="tpu_custom_call" | custom-call | flops 536870912 | bytes 629145 | tf_op jit(solution)/shard_map/pallas_call | solution.py:122
  448.3 15.4 %collective-permute-done.42 = bf16[1024,256]{1,0:T(8,128)(2,1)} collective-permute-done((bf16[1024,256]{1,0:T(8,128)(2,1)}, bf16[1024,256]{1,0:T(8,128)(2,1)}, u32[]{:S(2)}, u32[]{:S(2)}) %collective-permute-start.42) | collective-permute-done | bytes 524320 | tf_op jit(solution)/shard_map/ppermute | solution.py:47
  483.2 22.2 %collective-permute-done.25 = bf16[512,256]{1,0:T(8,128)(2,1)S(1)} collective-permute-done((bf16[512,256]{1,0:T(8,128)(2,1)S(1)}, bf16[512,256]{1,0:T(8,128)(2,1)S(1)}, u32[]{:S(2)}, u32[]{:S(2)}) %collective-permute-start.25) | collective-permute-done | bytes 262176 | tf_op jit(solution)/shard_map/ppermute | solution.py:47
  522.3 10.7 %shard_map.233 = (bf16[512,2048]{1,0:T(8,128)(2,1)}, bf16[4,256,896]{2,1,0:T(8,128)(2,1)}, bf16[4,256,896]{2,1,0:T(8,128)(2,1)}) custom-call(s32[4]{0:T(128)} %pad_add_fusion.refs_0_, bf16[512,512]{1,0:T(8,128)(2,1)} %bitcast.164, f32[512,256]{1,0:T(8,128)} %fusion.17.refs_2_, f32[512,128]{1,0:T(8,128)} %bitcast.177, f32[512,128]{1,0:T(8,128)} %bitcast.178, ...), custom_call_target="tpu_custom_call" | custom-call | flops 322122560 | bytes 1363148 | tf_op jit(solution)/shard_map/pallas_call | solution.py:122
  546.3 16.9 %collective-permute-done.38 = bf16[256,2048]{1,0:T(8,128)(2,1)S(1)} collective-permute-done((bf16[256,2048]{1,0:T(8,128)(2,1)S(1)}, bf16[256,2048]{1,0:T(8,128)(2,1)S(1)}, u32[]{:S(2)}, u32[]{:S(2)}) %collective-permute-start.38) | collective-permute-done | bytes 1048608 | tf_op jit(solution)/shard_map/ppermute | solution.py:47
  588.4 17.7 %collective-permute-done.40 = bf16[64,2048]{1,0:T(8,128)(2,1)S(1)} collective-permute-done((bf16[64,2048]{1,0:T(8,128)(2,1)S(1)}, bf16[64,2048]{1,0:T(8,128)(2,1)S(1)}, u32[]{:S(2)}, u32[]{:S(2)}) %collective-permute-start.40) | collective-permute-done | bytes 262176 | tf_op jit(solution)/shard_map/ppermute | solution.py:88
  (259 shorter events, 255.1 us)
Async XLA Ops:
  7.2 140.0 %all-gather.4.cloned.1.call-start = ((), (), s32[]{:S(2)}) async-start(), calls=%async_computation.6 | async-start | bytes 1310720 | tf_op jit(solution)/shard_map/all_gather | solution.py:1066
  7.9 258.5 %all-gather.6.cloned.1.call-start = ((), (), s32[]{:S(2)}) async-start(), calls=%async_computation.7 | async-start | bytes 18874368 | tf_op jit(solution)/shard_map/all_gather | solution.py:1067
  11.1 271.0 %all-gather.8.cloned.1.call-start = ((), (), s32[]{:S(2)}) async-start(), calls=%async_computation.8 | async-start | bytes 9437184 | tf_op jit(solution)/shard_map/all_gather | solution.py:1068
  42.1 57.6 %all-to-all-start = ((bf16[4,128,2048]{2,1,0:T(8,128)(2,1)}), bf16[4,128,2048]{2,1,0:T(8,128)(2,1)S(1)}, u32[]{:S(2)}, u32[]{:S(2)}) async-start(bf16[4,128,2048]{2,1,0:T(8,128)(2,1)} %get-tuple-element.49), calls=%async_computation | async-start | bytes 4194304 | tf_op jit(solution)/shard_map/all_to_all | solution.py:84
  56.0 33.7 %collective-permute-start.3 = (bf16[256,896]{1,0:T(8,128)(2,1)S(1)}, bf16[256,896]{1,0:T(8,128)(2,1)S(1)}, u32[]{:S(2)}, u32[]{:S(2)}) collective-permute-start(bf16[256,896]{1,0:T(8,128)(2,1)S(1)} %bitcast.154), channel_id=1, source_target_pairs={{0,8},{4,12},{8,0},{12,4},{16,24},{20,28},{24,16},{28,20},{1,9},{5... | collective-permute-start | bytes 1376264 | tf_op jit(solution)/shard_map/ppermute | solution.py:47
  104.2 113.9 %all-to-all-start.1 = ((bf16[4,128,2048]{2,1,0:T(8,128)(2,1)}), bf16[4,128,2048]{2,1,0:T(8,128)(2,1)S(1)}, u32[]{:S(2)}, u32[]{:S(2)}) async-start(bf16[4,128,2048]{2,1,0:T(8,128)(2,1)} %shard_map.215.refs_6_), calls=%async_computation.1 | async-start | bytes 4194304 | tf_op jit(solution)/shard_map/all_to_all | solution.py:84
  107.8 263.8 %reduce-scatter.4.cloned.1.call-start = ((), (), s32[]{:S(2)}) async-start(), calls=%async_computation.9 | async-start | bytes 2621440 | tf_op jit(solution)/shard_map/reduce_scatter | solution.py:1116
  153.9 34.5 %collective-permute-start.11 = (bf16[256,2048]{1,0:T(8,128)(2,1)}, bf16[256,2048]{1,0:T(8,128)(2,1)S(1)}, u32[]{:S(2)}, u32[]{:S(2)}) collective-permute-start(bf16[256,2048]{1,0:T(8,128)(2,1)} %shard_map.217.refs_4_.refs_1_), channel_id=1, source_target_pairs={{0,8},{4,12},{8,0},{12,4},{16,24},{20,28},{24,16},{28,20},{1,9},{5... | collective-permute-start | bytes 3145736 | tf_op jit(solution)/shard_map/ppermute | solution.py:47
  155.4 33.0 %collective-permute-start.12 = (bf16[256,2048]{1,0:T(8,128)(2,1)}, bf16[256,2048]{1,0:T(8,128)(2,1)S(1)}, u32[]{:S(2)}, u32[]{:S(2)}) collective-permute-start(bf16[256,2048]{1,0:T(8,128)(2,1)} %shard_map.217.refs_4_.refs_1_), channel_id=1, source_target_pairs={{0,16},{4,20},{8,24},{12,28},{16,0},{20,4},{24,8},{28,12},{1,17},{... | collective-permute-start | bytes 3145736 | tf_op jit(solution)/shard_map/ppermute | solution.py:47
  156.0 62.1 %collective-permute-start.13 = (bf16[256,2048]{1,0:T(8,128)(2,1)}, bf16[256,2048]{1,0:T(8,128)(2,1)}, u32[]{:S(2)}, u32[]{:S(2)}) collective-permute-start(bf16[256,2048]{1,0:T(8,128)(2,1)} %shard_map.217.refs_4_.refs_1_), channel_id=1, source_target_pairs={{0,24},{4,28},{8,16},{12,20},{16,8},{20,12},{24,0},{28,4},{1,25},{... | collective-permute-start | bytes 3145736 | tf_op jit(solution)/shard_map/ppermute | solution.py:47
  316.8 204.0 %reduce-scatter.6.cloned.1.call-start = ((), (), s32[]{:S(2)}) async-start(), calls=%async_computation.10 | async-start | bytes 10485760 | tf_op jit(solution)/shard_map/reduce_scatter | solution.py:104
  350.0 36.7 %collective-permute-start.22 = (bf16[4,2048,256]{2,1,0:T(8,128)(2,1)}, bf16[4,2048,256]{2,1,0:T(8,128)(2,1)}, u32[]{:S(2)}, u32[]{:S(2)}) collective-permute-start(bf16[4,2048,256]{2,1,0:T(8,128)(2,1)} %shard_map.228), channel_id=1, source_target_pairs={{0,4},{4,0},{8,12},{12,8},{16,20},{20,16},{24,28},{28,24},{1,5},{5... | collective-permute-start | bytes 12582920 | tf_op jit(solution)/shard_map/ppermute | solution.py:47
  435.1 71.2 %collective-permute-start.27 = (bf16[1024,2048]{1,0:T(8,128)(2,1)}, bf16[1024,2048]{1,0:T(8,128)(2,1)}, u32[]{:S(2)}, u32[]{:S(2)}) collective-permute-start(bf16[1024,2048]{1,0:T(8,128)(2,1)} %shard_map.231), channel_id=1, source_target_pairs={{0,4},{4,0},{8,12},{12,8},{16,20},{20,16},{24,28},{28,24},{1,5},{5... | collective-permute-start | bytes 12582920 | tf_op jit(solution)/shard_map/ppermute | solution.py:47
  435.1 32.4 %collective-permute-start.23 = (bf16[4,512,256]{2,1,0:T(8,128)(2,1)}, bf16[4,512,256]{2,1,0:T(8,128)(2,1)}, u32[]{:S(2)}, u32[]{:S(2)}) collective-permute-start(bf16[4,512,256]{2,1,0:T(8,128)(2,1)} %bitcast.36), channel_id=1, source_target_pairs={{0,4},{4,0},{8,12},{12,8},{16,20},{20,16},{24,28},{28,24},{1,5},{5... | collective-permute-start | bytes 3145736 | tf_op jit(solution)/shard_map/ppermute | solution.py:47
  443.1 77.7 %all-to-all-start.2 = ((bf16[4,128,2048]{2,1,0:T(8,128)(2,1)}), bf16[4,128,2048]{2,1,0:T(8,128)(2,1)S(1)}, u32[]{:S(2)}, u32[]{:S(2)}) async-start(bf16[4,128,2048]{2,1,0:T(8,128)(2,1)} %bitcast.27), calls=%async_computation.3 | async-start | bytes 4194304 | tf_op jit(solution)/shard_map/all_to_all | solution.py:84
  446.8 169.2 %reduce-scatter.8.cloned.1.call-start = ((), (), s32[]{:S(2)}) async-start(), calls=%async_computation.11 | async-start | bytes 2621440 | tf_op jit(solution)/shard_map/reduce_scatter | solution.py:1175
  470.6 47.3 %collective-permute-start.45 = (bf16[2048,256]{1,0:T(8,128)(2,1)S(1)}, bf16[2048,256]{1,0:T(8,128)(2,1)S(1)}, u32[]{:S(2)}, u32[]{:S(2)}) collective-permute-start(bf16[2048,256]{1,0:T(8,128)(2,1)S(1)} %pad_maximum_fusion.7), channel_id=1, source_target_pairs={{0,16},{4,20},{8,24},{12,28},{16,0},{20,4},{24,8},{28,12},{1,17},{... | collective-permute-start | bytes 3145736 | tf_op jit(solution)/shard_map/ppermute | solution.py:47
  472.6 45.3 %collective-permute-start.43 = (bf16[2048,256]{1,0:T(8,128)(2,1)S(1)}, bf16[2048,256]{1,0:T(8,128)(2,1)S(1)}, u32[]{:S(2)}, u32[]{:S(2)}) collective-permute-start(bf16[2048,256]{1,0:T(8,128)(2,1)S(1)} %pad_maximum_fusion.6), channel_id=1, source_target_pairs={{0,8},{4,12},{8,0},{12,4},{16,24},{20,28},{24,16},{28,20},{1,9},{5... | collective-permute-start | bytes 3145736 | tf_op jit(solution)/shard_map/ppermute | solution.py:47
  472.9 32.5 %collective-permute-start.25 = (bf16[512,256]{1,0:T(8,128)(2,1)S(1)}, bf16[512,256]{1,0:T(8,128)(2,1)S(1)}, u32[]{:S(2)}, u32[]{:S(2)}) collective-permute-start(bf16[512,256]{1,0:T(8,128)(2,1)S(1)} %get-tuple-element.103), channel_id=1, source_target_pairs={{0,16},{4,20},{8,24},{12,28},{16,0},{20,4},{24,8},{28,12},{1,17},{... | collective-permute-start | bytes 786440 | tf_op jit(solution)/shard_map/ppermute | solution.py:47
  542.7 32.0 %collective-permute-start.31 = (bf16[256,896]{1,0:T(8,128)(2,1)S(1)}, bf16[256,896]{1,0:T(8,128)(2,1)S(1)}, u32[]{:S(2)}, u32[]{:S(2)}) collective-permute-start(bf16[256,896]{1,0:T(8,128)(2,1)S(1)} %get-tuple-element.96), channel_id=1, source_target_pairs={{0,24},{4,28},{8,16},{12,20},{16,8},{20,12},{24,0},{28,4},{1,25},{... | collective-permute-start | bytes 1376264 | tf_op jit(solution)/shard_map/ppermute | solution.py:47
  544.4 38.1 %collective-permute-start.30 = (bf16[256,896]{1,0:T(8,128)(2,1)S(1)}, bf16[256,896]{1,0:T(8,128)(2,1)S(1)}, u32[]{:S(2)}, u32[]{:S(2)}) collective-permute-start(bf16[256,896]{1,0:T(8,128)(2,1)S(1)} %get-tuple-element.97), channel_id=1, source_target_pairs={{0,16},{4,20},{8,24},{12,28},{16,0},{20,4},{24,8},{28,12},{1,17},{... | collective-permute-start | bytes 1376264 | tf_op jit(solution)/shard_map/ppermute | solution.py:47
  545.0 38.0 %collective-permute-start.29 = (bf16[256,896]{1,0:T(8,128)(2,1)S(1)}, bf16[256,896]{1,0:T(8,128)(2,1)S(1)}, u32[]{:S(2)}, u32[]{:S(2)}) collective-permute-start(bf16[256,896]{1,0:T(8,128)(2,1)S(1)} %get-tuple-element.95), channel_id=1, source_target_pairs={{0,8},{4,12},{8,0},{12,4},{16,24},{20,28},{24,16},{28,20},{1,9},{5... | collective-permute-start | bytes 1376264 | tf_op jit(solution)/shard_map/ppermute | solution.py:47
  568.4 37.8 %collective-permute-start.40 = (bf16[64,2048]{1,0:T(8,128)(2,1)S(1)}, bf16[64,2048]{1,0:T(8,128)(2,1)S(1)}, u32[]{:S(2)}, u32[]{:S(2)}) collective-permute-start(bf16[64,2048]{1,0:T(8,128)(2,1)S(1)} %get-tuple-element.100), channel_id=1, source_target_pairs={{0,2},{1,3},{2,0},{3,1},{4,6},{5,7},{6,4},{7,5},{8,10},{9,11},{10,... | collective-permute-start | bytes 786440 | tf_op jit(solution)/shard_map/ppermute | solution.py:88
  574.7 31.4 %collective-permute-start.39 = (bf16[64,2048]{1,0:T(8,128)(2,1)S(1)}, bf16[64,2048]{1,0:T(8,128)(2,1)S(1)}, u32[]{:S(2)}, u32[]{:S(2)}) collective-permute-start(bf16[64,2048]{1,0:T(8,128)(2,1)S(1)} %get-tuple-element.98), channel_id=1, source_target_pairs={{0,1},{1,2},{2,3},{3,0},{4,5},{5,6},{6,7},{7,4},{8,9},{9,10},{10,1... | collective-permute-start | bytes 786440 | tf_op jit(solution)/shard_map/ppermute | solution.py:88
  (69 other events, 798.0 us)
Sparse Core Ops, SparseCore 0:
  9.6 39.4 all-gather.3
  51.0 115.8 all-gather.5
  168.7 79.2 all-gather.7
  316.9 54.6 reduce-scatter.3
  374.8 96.9 reduce-scatter.5
  537.2 51.3 reduce-scatter.7

commit v3 on v2

--- a/solution.py
+++ b/solution.py
@@ -62,18 +62,29 @@
     return sum((part.astype(F32) for part in came), held[0].astype(F32))
 
 
+def first_step(held, devices):
+    if devices != 8:
+        return [swap(held[bit // 2], bit, devices) for bit in range(2, devices, 2)]
+    half = held.shape[1] // 2
+    return [swap(held[3, :half], 2, devices), swap(held[3, half:], 4, devices)]
+
+
+def second_step(held, came, devices):
+    if devices != 8:
+        return came
+    from_x, from_y = came
+    half = held.shape[1] // 2
+    h4 = jnp.concatenate([add(held[2, :half], from_x), held[2, half:]], 0)
+    h2 = jnp.concatenate([held[1, :half], add(held[1, half:], from_y)], 0)
+    return [swap(h2, 2, devices), swap(h4, 4, devices)]
+
+
+def all_steps(held, came):
+    return sum((part.astype(F32) for part in came), held[0].astype(F32))
+
+
 def core_scatter_steps(held, devices):
-    if devices != 8:
-        return core_scatter(held, devices)
-    h0, h2, h4, h6 = held
-    half = h0.shape[0] // 2
-    from_x = swap(h6[:half], 2, devices)
-    from_y = swap(h6[half:], 4, devices)
-    h4 = jnp.concatenate([add(h4[:half], from_x), h4[half:]], 0)
-    h2 = jnp.concatenate([h2[:half], add(h2[half:], from_y)], 0)
-    came_x = swap(h2, 2, devices)
-    came_y = swap(h4, 4, devices)
-    return h0.astype(F32) + came_x.astype(F32) + came_y.astype(F32)
+    return all_steps(held, second_step(held, first_step(held, devices), devices))
 
 
 def xor_scatter(even, odd, devices):
@@ -245,17 +256,18 @@
         out_ref[h] = values
 
 
-def copies(scalars, values, H, scale, wait):
-    shape = (H,) + values.shape
+def copies(scalars, values, m, H, scale, wait):
+    rows = (values.shape[0] // MICRO, values.shape[1])
+    shape = (H,) + rows
     return call(
         functools.partial(copies_kernel, scale=scale),
         (1,),
-        [whole(values.shape)],
+        [pl.BlockSpec(rows, lambda i, s: (m, 0))],
         [whole(shape)],
         [shape_of(shape, BF)],
         [],
         0,
-        4 * H * values.size,
+        2 * H * values.size,
         (scalars, values),
         wait,
     )[0]
@@ -304,6 +316,25 @@
     )[0]
 
 
+def add_kernel(s, left_ref, right_ref, out_ref):
+    out_ref[...] = add(left_ref[...], right_ref[...])
+
+
+def add_up(scalars, left, right, wait):
+    return call(
+        add_kernel,
+        (1,),
+        [whole(left.shape), whole(left.shape)],
+        [whole(left.shape)],
+        [shape_of(left.shape, BF)],
+        [],
+        0,
+        6 * left.size,
+        (scalars, left, right),
+        wait,
+    )[0]
+
+
 def wide_kernel(s, from_ref, out_ref):
     out_ref[...] = from_ref[...].astype(F32)
 
@@ -323,6 +354,29 @@
         (scalars, values),
         wait,
     )[0]
+
+
+def merge_kernel(s, *refs):
+    *parts, out_ref = refs
+    for m, part_ref in enumerate(parts):
+        out_ref[:, m] = part_ref[...]
+
+
+def merge(scalars, parts, wait):
+    H, T, D = parts[0].shape
+    shape = (H, len(parts), T, D)
+    return call(
+        merge_kernel,
+        (1,),
+        [whole((H, T, D))] * len(parts),
+        [whole(shape)],
+        [shape_of(shape, BF)],
+        [],
+        0,
+        4 * len(parts) * H * T * D,
+        (scalars, *parts),
+        wait,
+    )[0].reshape(H * len(parts) * T, D)
 
 
 def arrange_kernel(s, *refs):
@@ -649,29 +703,25 @@
     )
 
 
-def out_kernel(s, x_ref, gain_ref, we_ref, wo_ref, *refs):
-    devices = len(refs) - 5
-    xn_ref, own_ref, o_own_ref, acc_ref, o_ref = refs[devices:]
+def out_kernel(s, x_ref, gain_ref, w_ref, *refs):
+    devices = len(refs) - 4
+    xn_ref, own_ref, o_own_ref, acc_ref = refs[devices:]
     n = pl.program_id(0)
-    _, group, QD = o_ref.shape
-    places, width, columns = we_ref.shape
-    each = QD // width
+    group, QD = refs[0].shape
+    columns = w_ref.shape[1]
     rows = group // devices
 
     @pl.when(n == 0)
     def _():
+        at = pl.ds(pl.multiple_of(s[1] * rows, rows), rows)
         for k in range(devices):
-            o_ref[before(s, k, devices)] = refs[k][...]
-        at = pl.ds(pl.multiple_of(s[1] * rows, rows), rows)
-        for h in range(devices):
-            o_own_ref[:, h * QD : (h + 1) * QD] = o_ref[h, at, :]
+            lanes = pl.ds(pl.multiple_of(before(s, k, devices) * QD, LANES), QD)
+            o_own_ref[:, lanes] = refs[k][at, :]
 
     got = jnp.zeros((group, columns), F32)
-    for place in range(places):
-        for parity, w_ref in enumerate((we_ref, wo_ref)):
-            c = s[0] ^ (2 * place + parity)
-            lanes = pl.ds(pl.multiple_of((c % each) * width, LANES), width)
-            got = got + nn(o_ref[c // each, :, lanes], w_ref[place])
+    for k in range(devices):
+        first = pl.multiple_of(before(s, k, devices) * QD, QD)
+        got = got + nn(refs[k][...], w_ref[pl.ds(first, QD), :])
     acc_ref[:, pl.ds(pl.multiple_of(n * columns, LANES), columns)] = got
 
     @pl.when(n == pl.num_programs(0) - 1)
@@ -691,23 +741,23 @@
         lax.fori_loop(0, devices, finish, 0)
 
 
-def out_project(scalars, o_parts, x, gains, w_even, w_odd, wait):
+def out_project(scalars, o_parts, x, gains, w_out, wait):
     H = len(o_parts)
     group, QD = o_parts[0].shape
-    places, width, D = w_even.shape
+    D = w_out.shape[1]
     rows = group // H
     columns = 512
-    piece = pl.BlockSpec((places, width, columns), lambda n, s: (0, 0, n))
+    piece = pl.BlockSpec((H * QD, columns), lambda n, s: (0, n))
     return call(
         out_kernel,
         (D // columns,),
-        [whole(x.shape), whole(gains.shape), piece, piece] + [whole((group, QD))] * H,
+        [whole(x.shape), whole(gains.shape), piece] + [whole((group, QD))] * H,
         [whole((group, D)), whole((rows, D)), whole((rows, H * QD))],
         [shape_of((group, D), BF), shape_of((rows, D), F32), shape_of((rows, H * QD), BF)],
-        [pltpu.VMEM((group, D), F32), pltpu.VMEM((H, group, QD), BF)],
+        [pltpu.VMEM((group, D), F32)],
         2 * group * H * QD * D,
-        2 * (H * group * QD + 2 * x.size + 2 * w_even.size),
-        (scalars, x, gains, w_even, w_odd, *o_parts),
+        2 * (H * group * QD + 2 * x.size + w_out.size),
+        (scalars, x, gains, w_out, *o_parts),
         wait,
     )
 
@@ -743,26 +793,33 @@
     )
 
 
-def down_kernel(s, hidden_ref, w_ref, out_ref):
-    out_ref[...] = nn(hidden_ref[...], w_ref[...]).astype(BF)
-
-
-def down_project(scalars, hidden, w_down, wait):
+def down_kernel(s, hidden_ref, w_ref, *outs):
+    got_ref = outs[-1]
+    rows = outs[0].shape[0]
+    devices = got_ref.shape[0] // rows
+    got_ref[...] = nn(hidden_ref[...], w_ref[...]).astype(BF)
+    for k in range(devices):
+        at = pl.ds(pl.multiple_of(after(s, k, devices) * rows, rows), rows)
+        outs[k][...] = got_ref[at, :]
+
+
+def down_project(scalars, hidden, w_down, devices, wait):
     group, F = hidden.shape
     D = w_down.shape[1]
     width = 512
+    rows = group // devices
     return call(
         down_kernel,
         (D // width,),
         [whole(hidden.shape), pl.BlockSpec((F, width), lambda n, s: (0, n))],
-        [pl.BlockSpec((group, width), lambda n, s: (0, n))],
-        [shape_of((group, D), BF)],
-        [],
+        [pl.BlockSpec((rows, width), lambda n, s: (0, n))] * devices,
+        [shape_of((rows, D), BF)] * devices,
+        [pltpu.VMEM((group, width), BF)],
         2 * group * D * F,
         2 * (group * D + D * F + group * F),
         (scalars, hidden, w_down),
         wait,
-    )[0]
+    )
 
 
 def mlp_backward_kernel(
@@ -898,15 +955,12 @@
     return inverse * (through - scaled * inner), scaled
 
 
-def branch_kernel(s, parts, resid_ref, up_ref, gain_ref, we_ref, wo_ref, *refs):
+def branch_kernel(s, parts, resid_ref, up_ref, gain_ref, w_ref, *refs):
     devices = len(refs) - 4
     dresid_ref, da_ref, gg_ref = refs[:3]
     outs = refs[3:-1]
     dattn_ref = refs[-1]
     p = pl.program_id(0)
-    _, tokens, QD = dattn_ref.shape
-    width = we_ref.shape[1]
-    each = QD // width
 
     @pl.when(p == 0)
     def _():
@@ -921,11 +975,7 @@
         dresid_ref[...] = d_resid
         da_ref[...] = (RESIDUAL_SCALE * d_resid).astype(BF)
 
-    for parity, w_ref in enumerate((we_ref, wo_ref)):
-        c = s[0] ^ (2 * p + parity)
-        dattn_ref[c // each, :, pl.ds(pl.multiple_of((c % each) * width, LANES), width)] = nt(
-            da_ref[...], w_ref[0]
-        ).astype(BF)
+    dattn_ref[p] = nt(da_ref[...], w_ref[...]).astype(BF)
 
     @pl.when(p == pl.num_programs(0) - 1)
     def _():
@@ -933,21 +983,21 @@
             outs[k][...] = dattn_ref[after(s, k, devices)]
 
 
-def branch_back(scalars, parts, resid, upstream, gains, w_even, w_odd, QD, H, wait):
+def branch_back(scalars, parts, resid, upstream, gains, w_out, H, wait):
     _, tokens, D = parts.shape
-    places, width, _ = w_even.shape
-    piece = pl.BlockSpec((1, width, D), lambda p, s: (p, 0, 0))
+    QD = w_out.shape[0] // H
     return call(
         branch_kernel,
-        (places,),
-        [whole(a.shape) for a in (parts, resid, upstream, gains)] + [piece, piece],
+        (H,),
+        [whole(a.shape) for a in (parts, resid, upstream, gains)]
+        + [pl.BlockSpec((QD, D), lambda p, s: (p, 0))],
         [whole((tokens, D)), whole((tokens, D)), whole((8, D))] + [whole((tokens, QD))] * H,
         [shape_of((tokens, D), F32), shape_of((tokens, D), BF), shape_of((8, D), F32)]
         + [shape_of((tokens, QD), BF)] * H,
         [pltpu.VMEM((H, tokens, QD), BF)],
         2 * tokens * D * H * QD,
-        2 * (H * tokens * D + 2 * w_even.size + 6 * tokens * D),
-        (scalars, parts, resid, upstream, gains, w_even, w_odd),
+        2 * (H * tokens * D + w_out.size + 6 * tokens * D),
+        (scalars, parts, resid, upstream, gains, w_out),
         wait,
     )
 
@@ -1007,6 +1057,44 @@
         (scalars, dq, dkv, cosine, sine, x, xn, gain_two, w_even, w_odd),
         wait,
     )
+
+
+def last_kernel(s, parts_ref, x_ref, resid_ref, gain_ref, place_ref, out_ref):
+    M, T, _ = out_ref.shape
+    for m in range(M):
+        at = pl.ds(m * T, T)
+        upstream = parts_ref[0, at, :].astype(F32)
+        for h in range(1, parts_ref.shape[0]):
+            upstream = upstream + parts_ref[h, at, :].astype(F32)
+        back, _ = through_norm(upstream, gain_ref[0:1, :], x_ref[at, :].astype(F32))
+        total = resid_ref[at, :] + back
+        rank = lax.broadcasted_iota(jnp.int32, (T, T), 0)
+        order = (place_ref[m] == rank).astype(F32)
+        out_ref[m] = lax.dot_general(
+            order,
+            total,
+            (((0,), (0,)), ((), ())),
+            precision=lax.Precision.HIGHEST,
+            preferred_element_type=F32,
+        )
+
+
+def input_gradient(scalars, parts, x, d_resid, gains, place):
+    M, T = place.shape
+    D = x.shape[1]
+    place = place.reshape(M, 1, T)
+    args = (scalars, parts, x, d_resid, gains, place)
+    return call(
+        last_kernel,
+        (1,),
+        [whole(a.shape) for a in args[1:]],
+        [whole((M, T, D))],
+        [shape_of((M, T, D), F32)],
+        [],
+        4 * M * T * T * D,
+        12 * M * T * D,
+        args,
+    )[0]
 
 
 def body(
@@ -1063,11 +1151,9 @@
     x = head_exchange(x_copies)
     qkv_even, qkv_odd = xor_gather(pack, B)
 
-    w_out_rows = lax.all_gather(w_out, "head", axis=0, tiled=True)
     w_gate_up = lax.all_gather(jnp.concatenate([w_gate, w_up], 1), "blk", axis=0, tiled=True)
-    w_d = lax.all_gather(w_down, "blk", axis=1, tiled=True)
-    dmo_copies = copies(scalars, upstream, H, RESIDUAL_SCALE, [x])
-    dmo = head_exchange(dmo_copies).reshape(group, D)
+    dmo_copies = copies(scalars, upstream, 0, H, RESIDUAL_SCALE, [x])
+    dmo_parts = [head_exchange(dmo_copies)]
 
     run_start = jnp.arange(H)[:, None, None] + me * H
     i = jnp.arange(half)[None, None, :]
@@ -1102,25 +1188,35 @@
     kv_even, kv_odd = xor_gather(kv.reshape(group, 2 * KD), B)
     kv_even = kv_even.reshape((B // 2,) + runs + (2 * KD,))
     kv_odd = kv_odd.reshape((B // 2,) + runs + (2 * KD,))
-    w_out_rows = hold(scalars, [w_out_rows], [kv_odd])[0]
-    o, lse = attention_forward(scalars, q, kv_even, kv_odd, heads, [w_out_rows])
+    w_o = lax.all_gather(
+        hold(scalars, [w_out], [w_gate_up, kv])[0], "head", axis=0, tiled=True
+    )
+    o, lse = attention_forward(scalars, q, kv_even, kv_odd, heads, dmo_parts)
     o_parts = head_gather(o.reshape(group, QD), H)
-    out_even, out_odd = xor_gather(
-        w_out_rows, B, lambda parts: join(scalars, parts, [o_parts[1], dmo])
-    )
+    w_o = lax.all_gather(hold(scalars, [w_o], [lse])[0], "blk", axis=0, tiled=True)
+    w_d = lax.all_gather(hold(scalars, [w_down], [lse])[0], "blk", axis=1, tiled=True)
+    later = [copies(scalars, upstream, m, H, RESIDUAL_SCALE, o_parts[1:]) for m in range(1, MICRO)]
+    dmo_parts = dmo_parts + [head_exchange(part) for part in later]
     xn2, resid, o_own = out_project(
-        scalars, o_parts, x, gain_rows, out_even, out_odd, [dmo]
+        scalars, o_parts, x, gain_rows, w_o, later
     )
     gate, up, hidden = mlp_forward(scalars, xn2, w_gate_up, tile, ())
-    d_gate, d_up, d_xn2 = mlp_backward(scalars, gate, up, dmo, w_gate_up, w_d, tile, ())
+    dmo = merge(scalars, dmo_parts, [hidden])
+    came_down = swap(grad_columns(scalars, hidden, dmo, B), 1, B)
+    sum_down = grad_columns(scalars, hidden, dmo, B, came_down)
+    down_first = first_step(sum_down, B)
+    d_gate, d_up, d_xn2 = mlp_backward(
+        scalars, gate, up, dmo, w_gate_up, w_d, tile, [sum_down]
+    )
     d_xn2 = lax.psum_scatter(d_xn2, "head", scatter_dimension=0, tiled=True)[None]
 
-    came = swap(grad_rows(scalars, xn2, (d_gate, d_up), B), 1, B)
-    came_down = swap(grad_columns(scalars, hidden, dmo, B), 1, B)
-    sum_gate_up = grad_rows(scalars, xn2, (d_gate, d_up), B, came)
+    came = swap(grad_rows(scalars, xn2, (d_gate, d_up), B, wait=down_first), 1, B)
+    down_second = second_step(sum_down, down_first, B)
+    grad_down = all_steps(sum_down, down_second)
+    sum_gate_up = grad_rows(scalars, xn2, (d_gate, d_up), B, came, wait=down_second)
     grad_gate_up = plane_scatter(sum_gate_up, B, 0)
-    sum_down = grad_columns(scalars, hidden, dmo, B, came_down, [sum_gate_up])
-    grad_down = core_scatter_steps(sum_down, B)
+    mlp_sum = down_project(scalars, hidden, w_d, H, [sum_gate_up])
+
 
     d_resid, d_branch, gain_two, *d_attn = branch_back(
         scalars,
@@ -1128,37 +1224,21 @@
         resid,
         upstream,
         gain_rows,
-        out_even,
-        out_odd,
-        QD,
+        w_o,
         H,
-        [sum_gate_up],
-    )
-    mlp_out = down_project(scalars, hidden, w_d, [d_branch])
+        [sum_gate_up, mlp_sum[0]],
+    )
     d_attn = head_deal(d_attn, H)
-    mlp_held = hold(scalars, [mlp_out], d_attn[1:])[0]
-    mlp_out = head_exchange(mlp_held.reshape(H, tokens, D))
+    mlp_out = head_deal(mlp_sum, H)
     d_attn = [part.reshape(MICRO, 2, half, QD) for part in d_attn]
     tables = (H, 2, half, LANES)
     dq, dkv_even, dkv_odd = attention_backward(
         scalars, q, kv_even, kv_odd, d_attn, o, lse, cosine.reshape(tables), sine.reshape(tables), heads,
-        [sum_down, mlp_held],
-    )
-    out_away = grad_rows(scalars, o_own, (d_branch,), B, near=True, wait=[dq])
-    sum_out = grad_rows(
-        scalars, o_own, (d_branch,), B, came=swap(out_away, 1, B), near=True
-    ).reshape(B // 2, block, D)
-
-    def by_distance(values):
-        values = values.astype(BF).reshape(H, wrows, -1)
-        return head_deal(
-            [lax.dynamic_index_in_dim(values, (mine + k) % H, 0, False) for k in range(H)], H
-        )
-
-    grad_out = by_distance(core_scatter_steps(sum_out, B))
-    grad_out = sum(part.astype(F32) for part in grad_out)
+        mlp_out[1:2],
+    )
     pieces = (B // 2, group, 2 * KD)
-    dkv = xor_scatter(dkv_even.reshape(pieces), dkv_odd.reshape(pieces), B)
+    came = swap(dkv_odd.reshape(pieces), 1, B)
+    dkv = core_scatter(add_up(scalars, dkv_even.reshape(pieces), came, ()), B)
     d_xn1, grad_even, grad_odd = input_back(
         scalars,
         dq.reshape(group, QD),
@@ -1170,28 +1250,34 @@
         gain_two,
         qkv_even,
         qkv_odd,
-        [sum_out, mlp_out, grad_gate_up],
-    )
-    d_xn1 = lax.psum_scatter(d_xn1, "head", scatter_dimension=0, tiled=True)
-    grad_gate_up = wide(scalars, grad_gate_up, [d_xn1])
+        mlp_out[3:4],
+    )
+    out_away = grad_rows(scalars, o_own, (d_branch,), B, near=True, wait=[d_xn1])
+    sum_out = grad_rows(
+        scalars, o_own, (d_branch,), B, came=swap(out_away, 1, B), near=True, wait=[grad_gate_up]
+    ).reshape(B // 2, block, D)
+
+    def by_distance(values):
+        values = values.astype(BF).reshape(H, wrows, -1)
+        return head_deal(
+            [lax.dynamic_index_in_dim(values, (mine + k) % H, 0, False) for k in range(H)], H
+        )
+
+    grad_out = by_distance(core_scatter_steps(sum_out, B))
+    grad_gate_up = wide(scalars, grad_gate_up, grad_out[1:2])
+    d_xn1 = head_exchange(d_xn1.reshape(H, tokens, D))
+    grad_out = sum(part.astype(F32) for part in grad_out)
     grad_qkv = arrange(scalars, by_distance(xor_scatter(grad_even, grad_odd, B))).astype(F32)
     grad_gains = jnp.sum(grad_qkv[:, :, used : used + 2], 0)
 
     def side_by_side(values):
         return values.transpose(1, 0, 2).reshape(wrows, -1)
 
-    output = (resid + RESIDUAL_SCALE * jnp.sum(mlp_out.astype(F32), 0)).astype(BF)
+    output = (resid + RESIDUAL_SCALE * sum(part.astype(F32) for part in mlp_out)).astype(BF)
     output = jnp.einsum(
         "mrs,mrd->msd", order, output.reshape(MICRO, T, D), preferred_element_type=F32
     ).astype(BF)
-    back, _ = through_norm(d_xn1.astype(F32), gain_rows[0:1], x_own.astype(F32))
-    d_input = jnp.einsum(
-        "mrs,mrd->msd",
-        order.astype(F32),
-        (d_resid + back).reshape(MICRO, T, D),
-        precision=lax.Precision.HIGHEST,
-        preferred_element_type=F32,
-    )
+    d_input = input_gradient(scalars, d_xn1, x_own, d_resid, gain_rows, place)
     return (
         output,
         d_input,

time: 647 us -> 607 us (0.938)
  waiting for transfers between devices: 274 us -> 224 us
  Pallas kernels: 207 us -> 220 us
  other arithmetic: 39.5 us -> 29.6 us
  local copies, waits for them, and re-layouts: 25.8 us -> 34 us
    ppermute x31 -> x27, waiting for transfers between devices: 178 us -> 106 us  [swap(): return lax.ppermute(x, 'blk', [(i, i ^ bit) for i in range(devices)])]
    ppermute x15 -> x18, waiting for transfers between devices: 66.2 us -> 88.7 us  [head_shift(): lax.ppermute(x, 'head', [(i, (i + by) % devices) for i in range(devices)])]
    reduce_scatter x1, waiting for transfers between devices: 20.2 us -> 0.02 us  [body(): lax.psum_scatter(d_xn2, 'head', scatter_dimension=0, tiled=True)[None]]
    pallas_call x24 -> x28, Pallas kernels: 207 us -> 220 us  [call(): pl.pallas_call(run, grid_spec=pltpu.PrefetchScalarGridSpec(num_scalar_pre...]
    all_gather x1, waiting for transfers between devices: 0.01 us -> 12 us  [body(): lax.all_gather(jnp.concatenate([w_gate, w_up], 1), 'blk', axis=0, tiled=T...]
    all_to_all x3 -> x4, waiting for transfers between devices: 8.35 us -> 17.6 us  [head_exchange(): lax.all_to_all(parts, 'head', split_axis=0, concat_axis=0, tiled=True)]
    ppermute x15 -> x18, starting transfers between devices: 24.7 us -> 32 us  [head_shift(): lax.ppermute(x, 'head', [(i, (i + by) % devices) for i in range(devices)])]
    ppermute x31 -> x27, starting transfers between devices: 29.7 us -> 23.3 us  [swap(): return lax.ppermute(x, 'blk', [(i, i ^ bit) for i in range(devices)])]
  transfers between devices with their start and end apart: 55 -> 55, of which waited for: 27 -> 25; matrix products, arithmetic and copies ran while one was open for 8% -> 7% of each run, Pallas kernels for 26% -> 35%
where the time goes in v3:
time: 607 us; the launch traced here: 598 us
  waiting for transfers between devices  224 us (37%)
  Pallas kernels  220 us (36%)
  starting transfers between devices  73 us (12%)
  local copies, waits for them, and re-layouts  34 us (6%)
  other arithmetic  29.6 us (5%)
  between operations  15 us (2%)
    pallas_call x28, Pallas kernels, call(): pl.pallas_call(run, grid_spec=pltpu.PrefetchScalarGridSpec(num_scalar_pre...  220 us
    ppermute x27, waiting for transfers between devices, swap(): return lax.ppermute(x, 'blk', [(i, i ^ bit) for i in range(devices)])  106 us
    ppermute x18, waiting for transfers between devices, head_shift(): lax.ppermute(x, 'head', [(i, (i + by) % devices) for i in range(devices)])  88.7 us
    ppermute x18, starting transfers between devices, head_shift(): lax.ppermute(x, 'head', [(i, (i + by) % devices) for i in range(devices)])  32 us
    ppermute x27, starting transfers between devices, swap(): return lax.ppermute(x, 'blk', [(i, i ^ bit) for i in range(devices)])  23.3 us
    all_to_all x4, waiting for transfers between devices, head_exchange(): lax.all_to_all(parts, 'head', split_axis=0, concat_axis=0, tiled=True)  17.6 us
    all_to_all x4, starting transfers between devices, head_exchange(): lax.all_to_all(parts, 'head', split_axis=0, concat_axis=0, tiled=True)  17.3 us
    unnamed x96, local copies, waits for them, and re-layouts  16.2 us
  transfers between devices with their start and end apart: 55, of which 25 were waited for; matrix products, arithmetic and copies ran while one was open for 7% of the time, Pallas kernels for 35%

profile of v3, /device:TPU:0, one launch (start us, length us, event | category | flops | bytes accessed | tf_op | source)
XLA Modules:
  0.0 597.7 jit_solution(4263645825859319215)
XLA Ops:
  44.4 14.4 %collective-permute-done.5 = bf16[256,896]{1,0:T(8,128)(2,1)S(1)} collective-permute-done((bf16[256,896]{1,0:T(8,128)(2,1)S(1)}, bf16[256,896]{1,0:T(8,128)(2,1)S(1)}, u32[]{:S(2)}, u32[]{:S(2)}) %collective-permute-start.5) | collective-permute-done | bytes 458784 | tf_op jit(solution)/shard_map/ppermute | solution.py:47
  58.8 8.7 %collective-permute-done.4 = bf16[256,896]{1,0:T(8,128)(2,1)S(1)} collective-permute-done((bf16[256,896]{1,0:T(8,128)(2,1)S(1)}, bf16[256,896]{1,0:T(8,128)(2,1)S(1)}, u32[]{:S(2)}, u32[]{:S(2)}) %collective-permute-start.4) | collective-permute-done | bytes 458784 | tf_op jit(solution)/shard_map/ppermute | solution.py:47
  70.7 17.6 %all-to-all-done.refs_2_ = bf16[4,128,2048]{2,1,0:T(8,128)(2,1)S(1)} async-done(((bf16[4,128,2048]{2,1,0:T(8,128)(2,1)}), bf16[4,128,2048]{2,1,0:T(8,128)(2,1)S(1)}, u32[]{:S(2)}, u32[]{:S(2)}) %all-to-all-start) | async-done | bytes 2097184 | tf_op jit(solution)/shard_map/all_to_all | solution.py:95
  96.6 8.1 %shard_map.216 = (bf16[4,2,64,2048]{3,2,1,0:T(8,128)(2,1)}, bf16[4,2,64,512]{3,2,1,0:T(8,128)(2,1)}, bf16[4,2,64,256]{3,2,1,0:T(8,128)(2,1)}, f32[8,2048]{1,0:T(8,128)}) custom-call(s32[4]{0:T(128)} %pad_add_fusion.refs_0_, bf16[4,2,64,2048]{3,2,1,0:T(8,128)(2,1)} %bitcast.147, bf16[4,256,896]{2,1,0:T(8,128)(2,1)} %pad_maximum_fusion.1.refs_2_.refs_8_, ...), custom_call_target="tpu_custom_call" | custom-call | flops 161061280 | bytes 786432 | tf_op jit(solution)/shard_map/pallas_call | solution.py:133
  104.8 12.0 %all-gather.5.cloned.1.call-done.refs_2_.refs_3_.refs_4_ = bf16[2048,4096]{1,0:T(8,128)(2,1)} async-done(((bf16[256,4096]{1,0:T(8,128)(2,1)}), bf16[2048,4096]{1,0:T(8,128)(2,1)}) %all-gather.5.cloned.1.call-update) | async-done | bytes 16777232 | tf_op jit(solution)/shard_map/all_gather | solution.py:1154
  138.6 16.0 %shard_map.218 = (bf16[4,2,2,32,512]{4,3,2,1,0:T(8,128)(2,1)}, f32[2,2,2,1,512]{4,3,2,1,0:T(1,128)}) custom-call(s32[4]{0:T(128)} %pad_add_fusion.refs_0_, bf16[4,2,2,32,512]{4,3,2,1,0:T(8,128)(2,1)} %bitcast.172, bf16[4,4,2,2,32,256]{5,4,3,2,1,0:T(8,128)(2,1)} %pad_maximum_fusion.2.refs_2_, bf16[4,4,2,2,32,256]{5,4,3,2,1,0:T(8,128)(2,1)} %bitcast.156, ...), custom_call_target="tpu_custom_call" | custom-call | flops 214748368 | bytes 314572 | tf_op jit(solution)/shard_map/pallas_call | solution.py:133
  165.2 11.3 %collective-permute-done.13.refs_4_.refs_7_ = bf16[512,512]{1,0:T(8,128)(2,1)S(1)} collective-permute-done((bf16[512,512]{1,0:T(8,128)(2,1)S(1)}, bf16[512,512]{1,0:T(8,128)(2,1)S(1)}, u32[]{:S(2)}, u32[]{:S(2)}) %collective-permute-start.13) | collective-permute-done | bytes 524320 | tf_op jit(solution)/shard_map/ppermute | solution.py:99
  176.5 32.8 %collective-permute-done.12.refs_3_.refs_6_ = bf16[512,512]{1,0:T(8,128)(2,1)S(1)} collective-permute-done((bf16[512,512]{1,0:T(8,128)(2,1)S(1)}, bf16[512,512]{1,0:T(8,128)(2,1)S(1)}, u32[]{:S(2)}, u32[]{:S(2)}) %collective-permute-start.12) | collective-permute-done | bytes 524320 | tf_op jit(solution)/shard_map/ppermute | solution.py:99
  217.3 12.6 %shard_map.221 = (bf16[512,2048]{1,0:T(8,128)(2,1)}, f32[128,2048]{1,0:T(8,128)}, bf16[128,2048]{1,0:T(8,128)(2,1)}) custom-call(s32[4]{0:T(128)} %pad_add_fusion.refs_0_, bf16[512,2048]{1,0:T(8,128)(2,1)} %bitcast.148, f32[8,2048]{1,0:T(8,128)} %get-tuple-element.55.refs_2_.refs_4_, bf16[2048,2048]{1,0:T(8,128)(2,1)} %all-gather.9.cloned.1.call-done.refs_3_.refs_5_, ...), custom_call_target="tpu_custom_call" | custom-call | flops 429496736 | bytes 1468006 | tf_op jit(solution)/shard_map/pallas_call | solution.py:133
  229.9 15.7 %shard_map.222 = (f32[512,2048]{1,0:T(8,128)}, f32[512,2048]{1,0:T(8,128)}, bf16[512,2048]{1,0:T(8,128)(2,1)}) custom-call(s32[4]{0:T(128)} %pad_add_fusion.refs_0_, bf16[512,2048]{1,0:T(8,128)(2,1)} %get-tuple-element.61.refs_1_, bf16[2048,4096]{1,0:T(8,128)(2,1)} %all-gather.5.cloned.1.call-done.refs_2_.refs_3_.refs_4_, ...), custom_call_target="tpu_custom_call" | custom-call | flops 858993472 | bytes 2936012 | tf_op jit(solution)/shard_map/pallas_call | solution.py:133
  257.6 7.4 %collective-permute-done.14.refs_3_ = bf16[4,2048,256]{2,1,0:T(8,128)(2,1)S(1)} collective-permute-done((bf16[4,2048,256]{2,1,0:T(8,128)(2,1)}, bf16[4,2048,256]{2,1,0:T(8,128)(2,1)S(1)}, u32[]{:S(2)}, u32[]{:S(2)}) %collective-permute-start.14) | collective-permute-done | bytes 4194336 | tf_op jit(solution)/shard_map/ppermute | solution.py:47
  266.9 8.2 %shard_map.226.refs_7_ = bf16[4,2048,256]{2,1,0:T(8,128)(2,1)} custom-call(s32[4]{0:T(128)} %pad_add_fusion.refs_0_, bf16[512,2048]{1,0:T(8,128)(2,1)} %get-tuple-element.62.refs_3_.refs_1_, bf16[512,2048]{1,0:T(8,128)(2,1)} %bitcast.151, bf16[4,2048,256]{2,1,0:T(8,128)(2,1)} %copy-done.10), custom_call_target="tpu_custom_call" | custom-call | flops 214748368 | bytes 1258291 | tf_op jit(solution)/shard_map/pallas_call | solution.py:133
  278.8 24.5 %shard_map.227 = (bf16[512,2048]{1,0:T(8,128)(2,1)}, bf16[512,2048]{1,0:T(8,128)(2,1)}, bf16[512,2048]{1,0:T(8,128)(2,1)}) custom-call(s32[4]{0:T(128)} %pad_add_fusion.refs_0_, f32[512,2048]{1,0:T(8,128)} %get-tuple-element.63.refs_1_, f32[512,2048]{1,0:T(8,128)} %get-tuple-element.64.refs_2_, ...), custom_call_target="tpu_custom_call" | custom-call | flops 1288490240 | bytes 4404019 | tf_op jit(solution)/shard_map/pallas_call | solution.py:133
  304.3 10.2 %shard_map.228 = bf16[1024,4096]{1,0:T(8,128)(2,1)} custom-call(s32[4]{0:T(128)} %pad_add_fusion.refs_0_, bf16[512,2048]{1,0:T(8,128)(2,1)} %get-tuple-element.61.refs_1_, bf16[512,2048]{1,0:T(8,128)(2,1)} %get-tuple-element.65.refs_2_, bf16[512,2048]{1,0:T(8,128)(2,1)} %get-tuple-element.66.refs_3_, bf16[1024,256]{1,0:T(8,128)(2,1)} %copy-done.21, ...), custom_call_target="tpu_custom_call" | custom-call | flops 429496736 | bytes 2306867 | tf_op jit(solution)/shard_map/pallas_call | solution.py:133
  319.5 22.4 %collective-permute-done.18.refs_5_ = bf16[2048,256]{1,0:T(8,128)(2,1)S(1)} collective-permute-done((bf16[2048,256]{1,0:T(8,128)(2,1)S(1)}, bf16[2048,256]{1,0:T(8,128)(2,1)S(1)}, u32[]{:S(2)}, u32[]{:S(2)}) %collective-permute-start.18) | collective-permute-done | bytes 1048608 | tf_op jit(solution)/shard_map/ppermute | solution.py:47
  343.4 12.1 %shard_map.229.refs_3_.refs_6_ = bf16[1024,4096]{1,0:T(8,128)(2,1)} custom-call(s32[4]{0:T(128)} %pad_add_fusion.refs_0_, bf16[512,2048]{1,0:T(8,128)(2,1)} %get-tuple-element.61.refs_1_, bf16[512,2048]{1,0:T(8,128)(2,1)} %get-tuple-element.65.refs_2_, bf16[512,2048]{1,0:T(8,128)(2,1)} %get-tuple-element.66.refs_3_, ...), custom_call_target="tpu_custom_call" | custom-call | flops 429496736 | bytes 2306867 | tf_op jit(solution)/shard_map/pallas_call | solution.py:133
  355.5 9.5 %shard_map.230 = (bf16[128,2048]{1,0:T(8,128)(2,1)}, bf16[128,2048]{1,0:T(8,128)(2,1)}, bf16[128,2048]{1,0:T(8,128)(2,1)}, bf16[128,2048]{1,0:T(8,128)(2,1)}) custom-call(s32[4]{0:T(128)} %pad_add_fusion.refs_0_, bf16[512,2048]{1,0:T(8,128)(2,1)} %get-tuple-element.62.refs_3_.refs_1_, bf16[2048,2048]{1,0:T(8,128)(2,1)} %all-gather.11.cloned.1.call-done.refs_5_.refs_2_, ...), custom_call_target="tpu_custom_call" | custom-call | flops 429496736 | bytes 1258291 | tf_op jit(solution)/shard_map/pallas_call | solution.py:133
  367.5 9.5 %shard_map.231 = (f32[128,2048]{1,0:T(8,128)}, bf16[128,2048]{1,0:T(8,128)(2,1)}, f32[8,2048]{1,0:T(8,128)}, bf16[128,512]{1,0:T(8,128)(2,1)}, bf16[128,512]{1,0...) custom-call(s32[4]{0:T(128)} %pad_add_fusion.refs_0_, bf16[1,128,2048]{2,1,0:T(8,128)(2,1)} %bitcast.189, ...), custom_call_target="tpu_custom_call" | custom-call | flops 107374184 | bytes 1363148 | tf_op jit(solution)/shard_map/pallas_call | solution.py:133
  389.6 21.4 %shard_map.232 = (bf16[4,2,2,32,512]{4,3,2,1,0:T(8,128)(2,1)}, bf16[4,4,2,2,32,256]{5,4,3,2,1,0:T(8,128)(2,1)}, bf16[4,4,2,2,32,256]{5,4,3,2,1,0:T(8,128)(2,1)}) custom-call(s32[4]{0:T(128)} %pad_add_fusion.refs_0_, bf16[4,2,2,32,512]{4,3,2,1,0:T(8,128)(2,1)} %bitcast.173, bf16[4,4,2,2,32,256]{5,4,3,2,1,0:T(8,128)(2,1)} %pad_maximum_fusion.2.refs_2_, ...), custom_call_target="tpu_custom_call" | custom-call | flops 536870912 | bytes 629145 | tf_op jit(solution)/shard_map/pallas_call | solution.py:133
  425.6 9.8 %collective-permute-done.27 = bf16[512,256]{1,0:T(8,128)(2,1)S(1)} collective-permute-done((bf16[512,256]{1,0:T(8,128)(2,1)S(1)}, bf16[512,256]{1,0:T(8,128)(2,1)S(1)}, u32[]{:S(2)}, u32[]{:S(2)}) %collective-permute-start.27) | collective-permute-done | bytes 262176 | tf_op jit(solution)/shard_map/ppermute | solution.py:47
  435.4 11.9 %collective-permute-done.29 = bf16[512,256]{1,0:T(8,128)(2,1)S(1)} collective-permute-done((bf16[512,256]{1,0:T(8,128)(2,1)S(1)}, bf16[512,256]{1,0:T(8,128)(2,1)S(1)}, u32[]{:S(2)}, u32[]{:S(2)}) %collective-permute-start.29) | collective-permute-done | bytes 262176 | tf_op jit(solution)/shard_map/ppermute | solution.py:47
  450.7 10.8 %shard_map.234 = (bf16[512,2048]{1,0:T(8,128)(2,1)}, bf16[4,256,896]{2,1,0:T(8,128)(2,1)}, bf16[4,256,896]{2,1,0:T(8,128)(2,1)}) custom-call(s32[4]{0:T(128)} %pad_add_fusion.refs_0_, bf16[512,512]{1,0:T(8,128)(2,1)} %bitcast.188, f32[512,256]{1,0:T(8,128)} %fusion.11.refs_2_, f32[512,128]{1,0:T(8,128)} %bitcast.180, f32[512,128]{1,0:T(8,128)} %bitcast.179, ...), custom_call_target="tpu_custom_call" | custom-call | flops 322122560 | bytes 1363148 | tf_op jit(solution)/shard_map/pallas_call | solution.py:133
  492.4 8.1 %collective-permute-done.40 = bf16[128,2048]{1,0:T(8,128)(2,1)S(1)} collective-permute-done((bf16[128,2048]{1,0:T(8,128)(2,1)S(1)}, bf16[128,2048]{1,0:T(8,128)(2,1)S(1)}, u32[]{:S(2)}, u32[]{:S(2)}) %collective-permute-start.40) | collective-permute-done | bytes 524320 | tf_op jit(solution)/shard_map/ppermute | solution.py:47
  530.9 22.4 %collective-permute-done.35.refs_3_ = bf16[64,896]{1,0:T(8,128)(2,1)S(1)} collective-permute-done((bf16[64,896]{1,0:T(8,128)(2,1)S(1)}, bf16[64,896]{1,0:T(8,128)(2,1)S(1)}, u32[]{:S(2)}, u32[]{:S(2)}) %collective-permute-start.35) | collective-permute-done | bytes 114720 | tf_op jit(solution)/shard_map/ppermute | solution.py:99
  (273 shorter events, 245.4 us)
Async XLA Ops:
  7.2 109.6 %all-gather.5.cloned.1.call-start = ((), (), s32[]{:S(2)}) async-start(), calls=%async_computation.6 | async-start | bytes 18874368 | tf_op jit(solution)/shard_map/all_gather | solution.py:1154
  35.5 52.8 %all-to-all-start = ((bf16[4,128,2048]{2,1,0:T(8,128)(2,1)}), bf16[4,128,2048]{2,1,0:T(8,128)(2,1)S(1)}, u32[]{:S(2)}, u32[]{:S(2)}) async-start(bf16[4,128,2048]{2,1,0:T(8,128)(2,1)} %get-tuple-element.53), calls=%async_computation | async-start | bytes 4194304 | tf_op jit(solution)/shard_map/all_to_all | solution.py:95
  69.0 27.6 %collective-permute-start.6 = (bf16[4,256,896]{2,1,0:T(8,128)(2,1)}, bf16[4,256,896]{2,1,0:T(8,128)(2,1)}, u32[]{:S(2)}, u32[]{:S(2)}) collective-permute-start(bf16[4,256,896]{2,1,0:T(8,128)(2,1)} %pad_maximum_fusion.1.refs_2_.refs_8_), channel_id=1, source_target_pairs={{0,4},{4,0},{8,12},{12,8},{16,20},{20,16},{24,28},{28,24},{1,5},{5... | collective-permute-start | bytes 5505032 | tf_op jit(solution)/shard_map/ppermute | solution.py:47
  92.2 45.0 %all-to-all-start.1 = ((bf16[4,64,2048]{2,1,0:T(8,128)(2,1)}), bf16[4,64,2048]{2,1,0:T(8,128)(2,1)S(1)}, u32[]{:S(2)}, u32[]{:S(2)}) async-start(bf16[4,64,2048]{2,1,0:T(8,128)(2,1)} %shard_map.215.refs_6_), calls=%async_computation.1 | async-start | bytes 2097152 | tf_op jit(solution)/shard_map/all_to_all | solution.py:95
  95.8 58.7 %all-gather.7.cloned.1.call-start = ((), (), s32[]{:S(2)}) async-start(), calls=%async_computation.7 | async-start | bytes 1310720 | tf_op jit(solution)/shard_map/all_gather | solution.py:1191
  119.3 98.1 %all-gather.9.cloned.1.call-start = ((), (), s32[]{:S(2)}) async-start(), calls=%async_computation.8 | async-start | bytes 9437184 | tf_op jit(solution)/shard_map/all_gather | solution.py:1196
  157.5 121.3 %all-gather.11.cloned.1.call-start = ((), (), s32[]{:S(2)}) async-start(), calls=%async_computation.9 | async-start | bytes 9437184 | tf_op jit(solution)/shard_map/all_gather | solution.py:1197
  164.1 45.2 %collective-permute-start.12 = (bf16[512,512]{1,0:T(8,128)(2,1)S(1)}, bf16[512,512]{1,0:T(8,128)(2,1)S(1)}, u32[]{:S(2)}, u32[]{:S(2)}) collective-permute-start(bf16[512,512]{1,0:T(8,128)(2,1)S(1)} %bitcast.176), channel_id=1, source_target_pairs={{0,2},{1,3},{2,0},{3,1},{4,6},{5,7},{6,4},{7,5},{8,10},{9,11},{10,... | collective-permute-start | bytes 1572872 | tf_op jit(solution)/shard_map/ppermute | solution.py:99
  164.1 45.2 %collective-permute-start.11 = (bf16[512,512]{1,0:T(8,128)(2,1)S(1)}, bf16[512,512]{1,0:T(8,128)(2,1)S(1)}, u32[]{:S(2)}, u32[]{:S(2)}) collective-permute-start(bf16[512,512]{1,0:T(8,128)(2,1)S(1)} %bitcast.177), channel_id=1, source_target_pairs={{0,1},{1,2},{2,3},{3,0},{4,5},{5,6},{6,7},{7,4},{8,9},{9,10},{10,1... | collective-permute-start | bytes 1572872 | tf_op jit(solution)/shard_map/ppermute | solution.py:99
  213.6 32.1 %all-to-all-start.2 = ((bf16[4,64,2048]{2,1,0:T(8,128)(2,1)}), bf16[4,64,2048]{2,1,0:T(8,128)(2,1)S(1)}, u32[]{:S(2)}, u32[]{:S(2)}) async-start(bf16[4,64,2048]{2,1,0:T(8,128)(2,1)} %shard_map.220.refs_8_), calls=%async_computation.2 | async-start | bytes 2097152 | tf_op jit(solution)/shard_map/all_to_all | solution.py:95
  217.1 150.4 %reduce-scatter.3.cloned.1.call-start = ((), (), s32[]{:S(2)}) async-start(), calls=%async_computation.10 | async-start | bytes 2621440 | tf_op jit(solution)/shard_map/reduce_scatter | solution.py:1211
  276.8 26.5 %collective-permute-start.16 = (bf16[1024,256]{1,0:T(8,128)(2,1)S(1)}, bf16[1024,256]{1,0:T(8,128)(2,1)S(1)}, u32[]{:S(2)}, u32[]{:S(2)}) collective-permute-start(bf16[1024,256]{1,0:T(8,128)(2,1)S(1)} %get-tuple-element.101), channel_id=1, source_target_pairs={{0,16},{4,20},{8,24},{12,28},{16,0},{20,4},{24,8},{28,12},{1,17},{... | collective-permute-start | bytes 1572872 | tf_op jit(solution)/shard_map/ppermute | solution.py:47
  277.5 25.8 %collective-permute-start.15 = (bf16[1024,256]{1,0:T(8,128)(2,1)S(1)}, bf16[1024,256]{1,0:T(8,128)(2,1)S(1)}, u32[]{:S(2)}, u32[]{:S(2)}) collective-permute-start(bf16[1024,256]{1,0:T(8,128)(2,1)S(1)} %get-tuple-element.102), channel_id=1, source_target_pairs={{0,8},{4,12},{8,0},{12,4},{16,24},{20,28},{24,16},{28,20},{1,9},{5... | collective-permute-start | bytes 1572872 | tf_op jit(solution)/shard_map/ppermute | solution.py:47
  314.4 28.0 %collective-permute-start.17 = (bf16[1024,4096]{1,0:T(8,128)(2,1)}, bf16[1024,4096]{1,0:T(8,128)(2,1)}, u32[]{:S(2)}, u32[]{:S(2)}) collective-permute-start(bf16[1024,4096]{1,0:T(8,128)(2,1)} %shard_map.228), channel_id=1, source_target_pairs={{0,4},{4,0},{8,12},{12,8},{16,20},{20,16},{24,28},{28,24},{1,5},{5... | collective-permute-start | bytes 25165832 | tf_op jit(solution)/shard_map/ppermute | solution.py:47
  314.4 162.6 %reduce-scatter.5.cloned.1.call-start = ((), (), s32[]{:S(2)}) async-start(), calls=%async_computation.11 | async-start | bytes 10485760 | tf_op jit(solution)/shard_map/reduce_scatter | solution.py:115
  411.2 38.0 %collective-permute-start.22 = (bf16[128,2048]{1,0:T(8,128)(2,1)S(1)}, bf16[128,2048]{1,0:T(8,128)(2,1)S(1)}, u32[]{:S(2)}, u32[]{:S(2)}) collective-permute-start(bf16[128,2048]{1,0:T(8,128)(2,1)S(1)} %copy-done.46), channel_id=1, source_target_pairs={{0,3},{1,0},{2,1},{3,2},{4,7},{5,4},{6,5},{7,6},{8,11},{9,8},{10,9... | collective-permute-start | bytes 1572872 | tf_op jit(solution)/shard_map/ppermute | solution.py:99
  422.5 24.8 %collective-permute-start.29 = (bf16[512,256]{1,0:T(8,128)(2,1)S(1)}, bf16[512,256]{1,0:T(8,128)(2,1)S(1)}, u32[]{:S(2)}, u32[]{:S(2)}) collective-permute-start(bf16[512,256]{1,0:T(8,128)(2,1)S(1)} %get-tuple-element.110), channel_id=1, source_target_pairs={{0,24},{4,28},{8,16},{12,20},{16,8},{20,12},{24,0},{28,4},{1,25},{... | collective-permute-start | bytes 786440 | tf_op jit(solution)/shard_map/ppermute | solution.py:47
  472.2 39.2 %collective-permute-start.21 = (bf16[128,2048]{1,0:T(8,128)(2,1)}, bf16[128,2048]{1,0:T(8,128)(2,1)}, u32[]{:S(2)}, u32[]{:S(2)}) collective-permute-start(bf16[128,2048]{1,0:T(8,128)(2,1)} %get-tuple-element.69), channel_id=1, source_target_pairs={{0,2},{1,3},{2,0},{3,1},{4,6},{5,7},{6,4},{7,5},{8,10},{9,11},{10,... | collective-permute-start | bytes 1572872 | tf_op jit(solution)/shard_map/ppermute | solution.py:99
  472.2 91.3 %all-to-all-start.3 = ((bf16[4,128,2048]{2,1,0:T(8,128)(2,1)}), bf16[4,128,2048]{2,1,0:T(8,128)(2,1)S(1)}, u32[]{:S(2)}, u32[]{:S(2)}) async-start(bf16[4,128,2048]{2,1,0:T(8,128)(2,1)} %bitcast.155), calls=%async_computation.4 | async-start | bytes 4194304 | tf_op jit(solution)/shard_map/all_to_all | solution.py:95
  490.9 29.6 %collective-permute-start.33 = (bf16[256,896]{1,0:T(8,128)(2,1)S(1)}, bf16[256,896]{1,0:T(8,128)(2,1)S(1)}, u32[]{:S(2)}, u32[]{:S(2)}) collective-permute-start(bf16[256,896]{1,0:T(8,128)(2,1)S(1)} %get-tuple-element.104), channel_id=1, source_target_pairs={{0,24},{4,28},{8,16},{12,20},{16,8},{20,12},{24,0},{28,4},{1,25},{... | collective-permute-start | bytes 1376264 | tf_op jit(solution)/shard_map/ppermute | solution.py:47
  502.0 55.6 %collective-permute-start.41 = (bf16[256,2048]{1,0:T(8,128)(2,1)S(1)}, bf16[256,2048]{1,0:T(8,128)(2,1)}, u32[]{:S(2)}, u32[]{:S(2)}) collective-permute-start(bf16[256,2048]{1,0:T(8,128)(2,1)S(1)} %pad_maximum_fusion.7), channel_id=1, source_target_pairs={{0,16},{4,20},{8,24},{12,28},{16,0},{20,4},{24,8},{28,12},{1,17},{... | collective-permute-start | bytes 3145736 | tf_op jit(solution)/shard_map/ppermute | solution.py:47
  511.4 46.2 %collective-permute-start.39 = (bf16[256,2048]{1,0:T(8,128)(2,1)}, bf16[256,2048]{1,0:T(8,128)(2,1)}, u32[]{:S(2)}, u32[]{:S(2)}) collective-permute-start(bf16[256,2048]{1,0:T(8,128)(2,1)} %pad_maximum_fusion.6), channel_id=1, source_target_pairs={{0,8},{4,12},{8,0},{12,4},{16,24},{20,28},{24,16},{28,20},{1,9},{5... | collective-permute-start | bytes 3145736 | tf_op jit(solution)/shard_map/ppermute | solution.py:47
  528.5 24.7 %collective-permute-start.35 = (bf16[64,896]{1,0:T(8,128)(2,1)S(1)}, bf16[64,896]{1,0:T(8,128)(2,1)S(1)}, u32[]{:S(2)}, u32[]{:S(2)}) collective-permute-start(bf16[64,896]{1,0:T(8,128)(2,1)S(1)} %get-tuple-element.115), channel_id=1, source_target_pairs={{0,2},{1,3},{2,0},{3,1},{4,6},{5,7},{6,4},{7,5},{8,10},{9,11},{10,... | collective-permute-start | bytes 344072 | tf_op jit(solution)/shard_map/ppermute | solution.py:99
  528.5 24.7 %collective-permute-start.34 = (bf16[64,896]{1,0:T(8,128)(2,1)S(1)}, bf16[64,896]{1,0:T(8,128)(2,1)S(1)}, u32[]{:S(2)}, u32[]{:S(2)}) collective-permute-start(bf16[64,896]{1,0:T(8,128)(2,1)S(1)} %get-tuple-element.116), channel_id=1, source_target_pairs={{0,1},{1,2},{2,3},{3,0},{4,5},{5,6},{6,7},{7,4},{8,9},{9,10},{10,1... | collective-permute-start | bytes 344072 | tf_op jit(solution)/shard_map/ppermute | solution.py:99
  (78 other events, 690.7 us)
Sparse Core Ops, SparseCore 0:
  10.4 106.3 all-gather.4
  119.4 27.9 all-gather.6
  157.6 54.3 all-gather.8
  213.7 55.9 all-gather.10
  314.6 44.5 reduce-scatter.2
  362.4 96.8 reduce-scatter.4

commit v4 on v3

--- a/solution.py
+++ b/solution.py
@@ -312,6 +312,28 @@
         0,
         4 * len(parts) * parts[0].size,
         (scalars, *parts),
+        wait,
+    )[0]
+
+
+def total_kernel(s, held_ref, *refs):
+    *came, out_ref = refs
+    out_ref[...] = sum((part[...].astype(F32) for part in came), held_ref[0].astype(F32))
+
+
+def total(scalars, held, came, wait):
+    _, rows, columns = held.shape
+    piece = pl.BlockSpec((rows // 4, columns), lambda i, s: (i, 0))
+    return call(
+        total_kernel,
+        (4,),
+        [pl.BlockSpec((1, rows // 4, columns), lambda i, s: (0, i, 0))] + [piece] * len(came),
+        [piece],
+        [shape_of((rows, columns), F32)],
+        [],
+        0,
+        10 * rows * columns,
+        (scalars, held, *came),
         wait,
     )[0]
 
@@ -1079,7 +1101,7 @@
         )
 
 
-def input_gradient(scalars, parts, x, d_resid, gains, place):
+def input_gradient(scalars, parts, x, d_resid, gains, place, wait):
     M, T = place.shape
     D = x.shape[1]
     place = place.reshape(M, 1, T)
@@ -1094,6 +1116,7 @@
         4 * M * T * T * D,
         12 * M * T * D,
         args,
+        wait,
     )[0]
 
 
@@ -1212,8 +1235,7 @@
 
     came = swap(grad_rows(scalars, xn2, (d_gate, d_up), B, wait=down_first), 1, B)
     down_second = second_step(sum_down, down_first, B)
-    grad_down = all_steps(sum_down, down_second)
-    sum_gate_up = grad_rows(scalars, xn2, (d_gate, d_up), B, came, wait=down_second)
+    sum_gate_up = grad_rows(scalars, xn2, (d_gate, d_up), B, came)
     grad_gate_up = plane_scatter(sum_gate_up, B, 0)
     mlp_sum = down_project(scalars, hidden, w_d, H, [sum_gate_up])
 
@@ -1250,7 +1272,7 @@
         gain_two,
         qkv_even,
         qkv_odd,
-        mlp_out[3:4],
+        mlp_out[2:],
     )
     out_away = grad_rows(scalars, o_own, (d_branch,), B, near=True, wait=[d_xn1])
     sum_out = grad_rows(
@@ -1264,9 +1286,9 @@
         )
 
     grad_out = by_distance(core_scatter_steps(sum_out, B))
-    grad_gate_up = wide(scalars, grad_gate_up, grad_out[1:2])
-    d_xn1 = head_exchange(d_xn1.reshape(H, tokens, D))
-    grad_out = sum(part.astype(F32) for part in grad_out)
+    grad_gate_up = wide(scalars, grad_gate_up, grad_out[2:3])
+    d_xn1 = lax.psum_scatter(d_xn1, "head", scatter_dimension=0, tiled=True)[None]
+    grad_down = total(scalars, sum_down, down_second, [d_xn1] + grad_out[1:2])
     grad_qkv = arrange(scalars, by_distance(xor_scatter(grad_even, grad_odd, B))).astype(F32)
     grad_gains = jnp.sum(grad_qkv[:, :, used : used + 2], 0)
 
@@ -1277,7 +1299,8 @@
     output = jnp.einsum(
         "mrs,mrd->msd", order, output.reshape(MICRO, T, D), preferred_element_type=F32
     ).astype(BF)
-    d_input = input_gradient(scalars, d_xn1, x_own, d_resid, gain_rows, place)
+    d_input = input_gradient(scalars, d_xn1, x_own, d_resid, gain_rows, place, grad_out[3:])
+    grad_out = sum(part.astype(F32) for part in grad_out)
     return (
         output,
         d_input,

time: 607 us -> 598 us (0.985)
  waiting for transfers between devices: 224 us -> 207 us
  starting transfers between devices: 73 us -> 83.1 us
    ppermute x18, waiting for transfers between devices: 88.7 us -> 72.6 us  [head_shift(): lax.ppermute(x, 'head', [(i, (i + by) % devices) for i in range(devices)])]
    ppermute x18, starting transfers between devices: 32 us -> 41.7 us  [head_shift(): lax.ppermute(x, 'head', [(i, (i + by) % devices) for i in range(devices)])]
    ppermute x27, waiting for transfers between devices: 106 us -> 96.5 us  [swap(): return lax.ppermute(x, 'blk', [(i, i ^ bit) for i in range(devices)])]
    reduce_scatter x1, waiting for transfers between devices: 0.02 us -> 8.14 us  [body(): lax.psum_scatter(d_xn2, 'head', scatter_dimension=0, tiled=True)[None]]
    all_to_all x4 -> x3, starting transfers between devices: 17.3 us -> 12.5 us  [head_exchange(): lax.all_to_all(parts, 'head', split_axis=0, concat_axis=0, tiled=True)]
    unnamed x96 -> x90, local copies, waits for them, and re-layouts: 16.2 us -> 14 us
    pallas_call x28 -> x29, Pallas kernels: 220 us -> 222 us  [call(): pl.pallas_call(run, grid_spec=pltpu.PrefetchScalarGridSpec(num_scalar_pre...]
    all_to_all x4 -> x3, waiting for transfers between devices: 17.6 us -> 17.6 us  [head_exchange(): lax.all_to_all(parts, 'head', split_axis=0, concat_axis=0, tiled=True)]
  transfers between devices with their start and end apart: 55 -> 55, of which waited for: 25 -> 28; matrix products, arithmetic and copies ran while one was open for 7% -> 7% of each run, Pallas kernels for 35% -> 34%
where the time goes in v4:
time: 598 us; the launch traced here: 588 us
  Pallas kernels  222 us (37%)
  waiting for transfers between devices  207 us (35%)
  starting transfers between devices  83.1 us (14%)
  local copies, waits for them, and re-layouts  31.1 us (5%)
  other arithmetic  28.8 us (5%)
  between operations  15.1 us (3%)
    pallas_call x29, Pallas kernels, call(): pl.pallas_call(run, grid_spec=pltpu.PrefetchScalarGridSpec(num_scalar_pre...  222 us
    ppermute x27, waiting for transfers between devices, swap(): return lax.ppermute(x, 'blk', [(i, i ^ bit) for i in range(devices)])  96.5 us
    ppermute x18, waiting for transfers between devices, head_shift(): lax.ppermute(x, 'head', [(i, (i + by) % devices) for i in range(devices)])  72.6 us
    ppermute x18, starting transfers between devices, head_shift(): lax.ppermute(x, 'head', [(i, (i + by) % devices) for i in range(devices)])  41.7 us
    ppermute x27, starting transfers between devices, swap(): return lax.ppermute(x, 'blk', [(i, i ^ bit) for i in range(devices)])  28.5 us
    all_to_all x3, waiting for transfers between devices, head_exchange(): lax.all_to_all(parts, 'head', split_axis=0, concat_axis=0, tiled=True)  17.6 us
    unnamed x90, local copies, waits for them, and re-layouts  14 us
    all_to_all x3, starting transfers between devices, head_exchange(): lax.all_to_all(parts, 'head', split_axis=0, concat_axis=0, tiled=True)  12.5 us
  transfers between devices with their start and end apart: 55, of which 28 were waited for; matrix products, arithmetic and copies ran while one was open for 7% of the time, Pallas kernels for 34%

profile of v4, /device:TPU:0, one launch (start us, length us, event | category | flops | bytes accessed | tf_op | source)
XLA Modules:
  0.0 588.2 jit_solution(14649696914201866094)
XLA Ops:
  44.4 14.5 %collective-permute-done.5 = bf16[256,896]{1,0:T(8,128)(2,1)S(1)} collective-permute-done((bf16[256,896]{1,0:T(8,128)(2,1)S(1)}, bf16[256,896]{1,0:T(8,128)(2,1)S(1)}, u32[]{:S(2)}, u32[]{:S(2)}) %collective-permute-start.5) | collective-permute-done | bytes 458784 | tf_op jit(solution)/shard_map/ppermute | solution.py:47
  58.8 8.7 %collective-permute-done.4 = bf16[256,896]{1,0:T(8,128)(2,1)S(1)} collective-permute-done((bf16[256,896]{1,0:T(8,128)(2,1)S(1)}, bf16[256,896]{1,0:T(8,128)(2,1)S(1)}, u32[]{:S(2)}, u32[]{:S(2)}) %collective-permute-start.4) | collective-permute-done | bytes 458784 | tf_op jit(solution)/shard_map/ppermute | solution.py:47
  70.7 17.6 %all-to-all-done.refs_2_ = bf16[4,128,2048]{2,1,0:T(8,128)(2,1)S(1)} async-done(((bf16[4,128,2048]{2,1,0:T(8,128)(2,1)}), bf16[4,128,2048]{2,1,0:T(8,128)(2,1)S(1)}, u32[]{:S(2)}, u32[]{:S(2)}) %all-to-all-start) | async-done | bytes 2097184 | tf_op jit(solution)/shard_map/all_to_all | solution.py:95
  96.6 8.1 %shard_map.216 = (bf16[4,2,64,2048]{3,2,1,0:T(8,128)(2,1)}, bf16[4,2,64,512]{3,2,1,0:T(8,128)(2,1)}, bf16[4,2,64,256]{3,2,1,0:T(8,128)(2,1)}, f32[8,2048]{1,0:T(8,128)}) custom-call(s32[4]{0:T(128)} %pad_add_fusion.refs_0_, bf16[4,2,64,2048]{3,2,1,0:T(8,128)(2,1)} %bitcast.142, bf16[4,256,896]{2,1,0:T(8,128)(2,1)} %pad_maximum_fusion.1.refs_2_.refs_8_, ...), custom_call_target="tpu_custom_call" | custom-call | flops 161061280 | bytes 786432 | tf_op jit(solution)/shard_map/pallas_call | solution.py:133
  104.8 12.0 %all-gather.5.cloned.1.call-done.refs_2_.refs_3_.refs_4_ = bf16[2048,4096]{1,0:T(8,128)(2,1)} async-done(((bf16[256,4096]{1,0:T(8,128)(2,1)}), bf16[2048,4096]{1,0:T(8,128)(2,1)}) %all-gather.5.cloned.1.call-update) | async-done | bytes 16777232 | tf_op jit(solution)/shard_map/all_gather | solution.py:1177
  138.6 14.7 %shard_map.218 = (bf16[4,2,2,32,512]{4,3,2,1,0:T(8,128)(2,1)}, f32[2,2,2,1,512]{4,3,2,1,0:T(1,128)}) custom-call(s32[4]{0:T(128)} %pad_add_fusion.refs_0_, bf16[4,2,2,32,512]{4,3,2,1,0:T(8,128)(2,1)} %bitcast.165, bf16[4,4,2,2,32,256]{5,4,3,2,1,0:T(8,128)(2,1)} %pad_maximum_fusion.2.refs_2_, bf16[4,4,2,2,32,256]{5,4,3,2,1,0:T(8,128)(2,1)} %bitcast.150, ...), custom_call_target="tpu_custom_call" | custom-call | flops 214748368 | bytes 314572 | tf_op jit(solution)/shard_map/pallas_call | solution.py:133
  163.9 11.3 %collective-permute-done.13.refs_4_.refs_7_ = bf16[512,512]{1,0:T(8,128)(2,1)S(1)} collective-permute-done((bf16[512,512]{1,0:T(8,128)(2,1)S(1)}, bf16[512,512]{1,0:T(8,128)(2,1)S(1)}, u32[]{:S(2)}, u32[]{:S(2)}) %collective-permute-start.13) | collective-permute-done | bytes 524320 | tf_op jit(solution)/shard_map/ppermute | solution.py:99
  175.2 32.9 %collective-permute-done.12.refs_3_.refs_6_ = bf16[512,512]{1,0:T(8,128)(2,1)S(1)} collective-permute-done((bf16[512,512]{1,0:T(8,128)(2,1)S(1)}, bf16[512,512]{1,0:T(8,128)(2,1)S(1)}, u32[]{:S(2)}, u32[]{:S(2)}) %collective-permute-start.12) | collective-permute-done | bytes 524320 | tf_op jit(solution)/shard_map/ppermute | solution.py:99
  216.1 12.4 %shard_map.221 = (bf16[512,2048]{1,0:T(8,128)(2,1)}, f32[128,2048]{1,0:T(8,128)}, bf16[128,2048]{1,0:T(8,128)(2,1)}) custom-call(s32[4]{0:T(128)} %pad_add_fusion.refs_0_, bf16[512,2048]{1,0:T(8,128)(2,1)} %bitcast.143, f32[8,2048]{1,0:T(8,128)} %get-tuple-element.55.refs_2_.refs_4_, bf16[2048,2048]{1,0:T(8,128)(2,1)} %all-gather.9.cloned.1.call-done.refs_3_.refs_5_, ...), custom_call_target="tpu_custom_call" | custom-call | flops 429496736 | bytes 1468006 | tf_op jit(solution)/shard_map/pallas_call | solution.py:133
  228.5 15.7 %shard_map.222 = (f32[512,2048]{1,0:T(8,128)}, f32[512,2048]{1,0:T(8,128)}, bf16[512,2048]{1,0:T(8,128)(2,1)}) custom-call(s32[4]{0:T(128)} %pad_add_fusion.refs_0_, bf16[512,2048]{1,0:T(8,128)(2,1)} %get-tuple-element.61.refs_1_, bf16[2048,4096]{1,0:T(8,128)(2,1)} %all-gather.5.cloned.1.call-done.refs_2_.refs_3_.refs_4_, ...), custom_call_target="tpu_custom_call" | custom-call | flops 858993472 | bytes 2936012 | tf_op jit(solution)/shard_map/pallas_call | solution.py:133
  256.3 7.4 %collective-permute-done.14.refs_3_ = bf16[4,2048,256]{2,1,0:T(8,128)(2,1)S(1)} collective-permute-done((bf16[4,2048,256]{2,1,0:T(8,128)(2,1)}, bf16[4,2048,256]{2,1,0:T(8,128)(2,1)S(1)}, u32[]{:S(2)}, u32[]{:S(2)}) %collective-permute-start.14) | collective-permute-done | bytes 4194336 | tf_op jit(solution)/shard_map/ppermute | solution.py:47
  265.6 8.8 %shard_map.226.refs_7_.refs_1_ = bf16[4,2048,256]{2,1,0:T(8,128)(2,1)} custom-call(s32[4]{0:T(128)} %pad_add_fusion.refs_0_, bf16[512,2048]{1,0:T(8,128)(2,1)} %get-tuple-element.62.refs_3_.refs_1_, bf16[512,2048]{1,0:T(8,128)(2,1)} %bitcast.146, bf16[4,2048,256]{2,1,0:T(8,128)(2,1)} %copy-done.5), custom_call_target="tpu_custom_call" | custom-call | flops 214748368 | bytes 1258291 | tf_op jit(solution)/shard_map/pallas_call | solution.py:133
  278.8 24.5 %shard_map.227 = (bf16[512,2048]{1,0:T(8,128)(2,1)}, bf16[512,2048]{1,0:T(8,128)(2,1)}, bf16[512,2048]{1,0:T(8,128)(2,1)}) custom-call(s32[4]{0:T(128)} %pad_add_fusion.refs_0_, f32[512,2048]{1,0:T(8,128)} %get-tuple-element.63.refs_1_, f32[512,2048]{1,0:T(8,128)} %get-tuple-element.64.refs_2_, ...), custom_call_target="tpu_custom_call" | custom-call | flops 1288490240 | bytes 4404019 | tf_op jit(solution)/shard_map/pallas_call | solution.py:133
  304.3 10.2 %shard_map.228 = bf16[1024,4096]{1,0:T(8,128)(2,1)} custom-call(s32[4]{0:T(128)} %pad_add_fusion.refs_0_, bf16[512,2048]{1,0:T(8,128)(2,1)} %get-tuple-element.61.refs_1_, bf16[512,2048]{1,0:T(8,128)(2,1)} %get-tuple-element.65.refs_2_, bf16[512,2048]{1,0:T(8,128)(2,1)} %get-tuple-element.66.refs_3_, bf16[1024,256]{1,0:T(8,128)(2,1)} %copy-done.14, ...), custom_call_target="tpu_custom_call" | custom-call | flops 429496736 | bytes 2306867 | tf_op jit(solution)/shard_map/pallas_call | solution.py:133
  314.6 13.4 %collective-permute-done.17.refs_4_ = bf16[1024,4096]{1,0:T(8,128)(2,1)} collective-permute-done((bf16[1024,4096]{1,0:T(8,128)(2,1)}, bf16[1024,4096]{1,0:T(8,128)(2,1)}, u32[]{:S(2)}, u32[]{:S(2)}) %collective-permute-start.17) | collective-permute-done | bytes 8388640 | tf_op jit(solution)/shard_map/ppermute | solution.py:47
  328.0 12.1 %shard_map.229.refs_3_.refs_6_ = bf16[1024,4096]{1,0:T(8,128)(2,1)} custom-call(s32[4]{0:T(128)} %pad_add_fusion.refs_0_, bf16[512,2048]{1,0:T(8,128)(2,1)} %get-tuple-element.61.refs_1_, bf16[512,2048]{1,0:T(8,128)(2,1)} %get-tuple-element.65.refs_2_, bf16[512,2048]{1,0:T(8,128)(2,1)} %get-tuple-element.66.refs_3_, ...), custom_call_target="tpu_custom_call" | custom-call | flops 429496736 | bytes 2306867 | tf_op jit(solution)/shard_map/pallas_call | solution.py:133
  340.1 9.5 %shard_map.230 = (bf16[128,2048]{1,0:T(8,128)(2,1)}, bf16[128,2048]{1,0:T(8,128)(2,1)}, bf16[128,2048]{1,0:T(8,128)(2,1)}, bf16[128,2048]{1,0:T(8,128)(2,1)}) custom-call(s32[4]{0:T(128)} %pad_add_fusion.refs_0_, bf16[512,2048]{1,0:T(8,128)(2,1)} %get-tuple-element.62.refs_3_.refs_1_, bf16[2048,2048]{1,0:T(8,128)(2,1)} %all-gather.11.cloned.1.call-done.refs_5_.refs_2_, ...), custom_call_target="tpu_custom_call" | custom-call | flops 429496736 | bytes 1258291 | tf_op jit(solution)/shard_map/pallas_call | solution.py:133
  352.2 8.1 %reduce-scatter.4.cloned.1.call-done = bf16[128,2048]{1,0:T(8,128)(2,1)} async-done(((bf16[512,2048]{1,0:T(8,128)(2,1)}), bf16[128,2048]{1,0:T(8,128)(2,1)}) %reduce-scatter.4.cloned.1.call-update) | async-done | bytes 524304 | tf_op jit(solution)/shard_map/reduce_scatter | solution.py:1234
  360.4 9.4 %shard_map.231 = (f32[128,2048]{1,0:T(8,128)}, bf16[128,2048]{1,0:T(8,128)(2,1)}, f32[8,2048]{1,0:T(8,128)}, bf16[128,512]{1,0:T(8,128)(2,1)}, bf16[128,512]{1,0...) custom-call(s32[4]{0:T(128)} %pad_add_fusion.refs_0_, bf16[1,128,2048]{2,1,0:T(8,128)(2,1)} %bitcast.184, ...), custom_call_target="tpu_custom_call" | custom-call | flops 107374184 | bytes 1363148 | tf_op jit(solution)/shard_map/pallas_call | solution.py:133
  383.0 19.7 %shard_map.232 = (bf16[4,2,2,32,512]{4,3,2,1,0:T(8,128)(2,1)}, bf16[4,4,2,2,32,256]{5,4,3,2,1,0:T(8,128)(2,1)}, bf16[4,4,2,2,32,256]{5,4,3,2,1,0:T(8,128)(2,1)}) custom-call(s32[4]{0:T(128)} %pad_add_fusion.refs_0_, bf16[4,2,2,32,512]{4,3,2,1,0:T(8,128)(2,1)} %bitcast.166, bf16[4,4,2,2,32,256]{5,4,3,2,1,0:T(8,128)(2,1)} %pad_maximum_fusion.2.refs_2_, ...), custom_call_target="tpu_custom_call" | custom-call | flops 536870912 | bytes 629145 | tf_op jit(solution)/shard_map/pallas_call | solution.py:133
  439.4 10.8 %shard_map.234 = (bf16[512,2048]{1,0:T(8,128)(2,1)}, bf16[4,256,896]{2,1,0:T(8,128)(2,1)}, bf16[4,256,896]{2,1,0:T(8,128)(2,1)}) custom-call(s32[4]{0:T(128)} %pad_add_fusion.refs_0_, bf16[512,512]{1,0:T(8,128)(2,1)} %bitcast.186, f32[512,256]{1,0:T(8,128)} %fusion.10.refs_2_, f32[512,128]{1,0:T(8,128)} %bitcast.183, f32[512,128]{1,0:T(8,128)} %bitcast.182, ...), custom_call_target="tpu_custom_call" | custom-call | flops 322122560 | bytes 1363148 | tf_op jit(solution)/shard_map/pallas_call | solution.py:133
  496.4 10.5 %collective-permute-done.37 = bf16[256,896]{1,0:T(8,128)(2,1)S(1)} collective-permute-done((bf16[256,896]{1,0:T(8,128)(2,1)S(1)}, bf16[256,896]{1,0:T(8,128)(2,1)S(1)}, u32[]{:S(2)}, u32[]{:S(2)}) %collective-permute-start.37) | collective-permute-done | bytes 458784 | tf_op jit(solution)/shard_map/ppermute | solution.py:47
  508.9 8.7 %collective-permute-start.40 = (bf16[64,896]{1,0:T(8,128)(2,1)S(1)}, bf16[64,896]{1,0:T(8,128)(2,1)S(1)}, u32[]{:S(2)}, u32[]{:S(2)}) collective-permute-start(bf16[64,896]{1,0:T(8,128)(2,1)S(1)} %get-tuple-element.114), channel_id=1, source_target_pairs={{0,3},{1,0},{2,1},{3,2},{4,7},{5,4},{6,5},{7,6},{8,11},{9,8},{10,9... | collective-permute-start | bytes 344072 | tf_op jit(solution)/shard_map/ppermute | solution.py:99
  545.0 12.9 %collective-permute-done.42.refs_2_ = bf16[64,2048]{1,0:T(8,128)(2,1)S(1)} collective-permute-done((bf16[64,2048]{1,0:T(8,128)(2,1)S(1)}, bf16[64,2048]{1,0:T(8,128)(2,1)S(1)}, u32[]{:S(2)}, u32[]{:S(2)}) %collective-permute-start.42) | collective-permute-done | bytes 262176 | tf_op jit(solution)/shard_map/ppermute | solution.py:99
  (268 shorter events, 259.4 us)
Async XLA Ops:
  7.2 109.6 %all-gather.5.cloned.1.call-start = ((), (), s32[]{:S(2)}) async-start(), calls=%async_computation.6 | async-start | bytes 18874368 | tf_op jit(solution)/shard_map/all_gather | solution.py:1177
  35.5 52.8 %all-to-all-start = ((bf16[4,128,2048]{2,1,0:T(8,128)(2,1)}), bf16[4,128,2048]{2,1,0:T(8,128)(2,1)S(1)}, u32[]{:S(2)}, u32[]{:S(2)}) async-start(bf16[4,128,2048]{2,1,0:T(8,128)(2,1)} %get-tuple-element.53), calls=%async_computation | async-start | bytes 4194304 | tf_op jit(solution)/shard_map/all_to_all | solution.py:95
  69.0 27.6 %collective-permute-start.6 = (bf16[4,256,896]{2,1,0:T(8,128)(2,1)}, bf16[4,256,896]{2,1,0:T(8,128)(2,1)}, u32[]{:S(2)}, u32[]{:S(2)}) collective-permute-start(bf16[4,256,896]{2,1,0:T(8,128)(2,1)} %pad_maximum_fusion.1.refs_2_.refs_8_), channel_id=1, source_target_pairs={{0,4},{4,0},{8,12},{12,8},{16,20},{20,16},{24,28},{28,24},{1,5},{5... | collective-permute-start | bytes 5505032 | tf_op jit(solution)/shard_map/ppermute | solution.py:47
  92.2 45.0 %all-to-all-start.1 = ((bf16[4,64,2048]{2,1,0:T(8,128)(2,1)}), bf16[4,64,2048]{2,1,0:T(8,128)(2,1)S(1)}, u32[]{:S(2)}, u32[]{:S(2)}) async-start(bf16[4,64,2048]{2,1,0:T(8,128)(2,1)} %shard_map.215.refs_6_), calls=%async_computation.1 | async-start | bytes 2097152 | tf_op jit(solution)/shard_map/all_to_all | solution.py:95
  95.8 57.4 %all-gather.7.cloned.1.call-start = ((), (), s32[]{:S(2)}) async-start(), calls=%async_computation.7 | async-start | bytes 1310720 | tf_op jit(solution)/shard_map/all_gather | solution.py:1214
  119.3 96.8 %all-gather.9.cloned.1.call-start = ((), (), s32[]{:S(2)}) async-start(), calls=%async_computation.8 | async-start | bytes 9437184 | tf_op jit(solution)/shard_map/all_gather | solution.py:1219
  156.2 122.6 %all-gather.11.cloned.1.call-start = ((), (), s32[]{:S(2)}) async-start(), calls=%async_computation.9 | async-start | bytes 9437184 | tf_op jit(solution)/shard_map/all_gather | solution.py:1220
  162.8 45.2 %collective-permute-start.12 = (bf16[512,512]{1,0:T(8,128)(2,1)S(1)}, bf16[512,512]{1,0:T(8,128)(2,1)S(1)}, u32[]{:S(2)}, u32[]{:S(2)}) collective-permute-start(bf16[512,512]{1,0:T(8,128)(2,1)S(1)} %bitcast.172), channel_id=1, source_target_pairs={{0,2},{1,3},{2,0},{3,1},{4,6},{5,7},{6,4},{7,5},{8,10},{9,11},{10,... | collective-permute-start | bytes 1572872 | tf_op jit(solution)/shard_map/ppermute | solution.py:99
  162.8 45.2 %collective-permute-start.11 = (bf16[512,512]{1,0:T(8,128)(2,1)S(1)}, bf16[512,512]{1,0:T(8,128)(2,1)S(1)}, u32[]{:S(2)}, u32[]{:S(2)}) collective-permute-start(bf16[512,512]{1,0:T(8,128)(2,1)S(1)} %bitcast.173), channel_id=1, source_target_pairs={{0,1},{1,2},{2,3},{3,0},{4,5},{5,6},{6,7},{7,4},{8,9},{9,10},{10,1... | collective-permute-start | bytes 1572872 | tf_op jit(solution)/shard_map/ppermute | solution.py:99
  212.4 31.8 %all-to-all-start.2 = ((bf16[4,64,2048]{2,1,0:T(8,128)(2,1)}), bf16[4,64,2048]{2,1,0:T(8,128)(2,1)S(1)}, u32[]{:S(2)}, u32[]{:S(2)}) async-start(bf16[4,64,2048]{2,1,0:T(8,128)(2,1)} %shard_map.220.refs_8_), calls=%async_computation.2 | async-start | bytes 2097152 | tf_op jit(solution)/shard_map/all_to_all | solution.py:95
  215.9 144.5 %reduce-scatter.4.cloned.1.call-start = ((), (), s32[]{:S(2)}) async-start(), calls=%async_computation.10 | async-start | bytes 2621440 | tf_op jit(solution)/shard_map/reduce_scatter | solution.py:1234
  276.0 27.3 %collective-permute-start.16 = (bf16[1024,256]{1,0:T(8,128)(2,1)S(1)}, bf16[1024,256]{1,0:T(8,128)(2,1)S(1)}, u32[]{:S(2)}, u32[]{:S(2)}) collective-permute-start(bf16[1024,256]{1,0:T(8,128)(2,1)S(1)} %get-tuple-element.93), channel_id=1, source_target_pairs={{0,16},{4,20},{8,24},{12,28},{16,0},{20,4},{24,8},{28,12},{1,17},{... | collective-permute-start | bytes 1572872 | tf_op jit(solution)/shard_map/ppermute | solution.py:47
  314.5 148.7 %reduce-scatter.8.cloned.1.call-start = ((), (), s32[]{:S(2)}) async-start(), calls=%async_computation.12 | async-start | bytes 10485760 | tf_op jit(solution)/shard_map/reduce_scatter | solution.py:115
  340.1 230.3 %reduce-scatter.6.cloned.1.call-start = ((), (), s32[]{:S(2)}) async-start(), calls=%async_computation.11 | async-start | bytes 2621440 | tf_op jit(solution)/shard_map/reduce_scatter | solution.py:1290
  349.7 32.5 %collective-permute-start.18 = (bf16[128,2048]{1,0:T(8,128)(2,1)}, bf16[128,2048]{1,0:T(8,128)(2,1)S(1)}, u32[]{:S(2)}, u32[]{:S(2)}) collective-permute-start(bf16[128,2048]{1,0:T(8,128)(2,1)} %get-tuple-element.68), channel_id=1, source_target_pairs={{0,1},{1,2},{2,3},{3,0},{4,5},{5,6},{6,7},{7,4},{8,9},{9,10},{10,1... | collective-permute-start | bytes 1572872 | tf_op jit(solution)/shard_map/ppermute | solution.py:99
  402.9 35.0 %collective-permute-start.19 = (bf16[128,2048]{1,0:T(8,128)(2,1)}, bf16[128,2048]{1,0:T(8,128)(2,1)S(1)}, u32[]{:S(2)}, u32[]{:S(2)}) collective-permute-start(bf16[128,2048]{1,0:T(8,128)(2,1)} %get-tuple-element.69), channel_id=1, source_target_pairs={{0,2},{1,3},{2,0},{3,1},{4,6},{5,7},{6,4},{7,5},{8,10},{9,11},{10,... | collective-permute-start | bytes 1572872 | tf_op jit(solution)/shard_map/ppermute | solution.py:99
  405.6 32.3 %collective-permute-start.20 = (bf16[128,2048]{1,0:T(8,128)(2,1)}, bf16[128,2048]{1,0:T(8,128)(2,1)S(1)}, u32[]{:S(2)}, u32[]{:S(2)}) collective-permute-start(bf16[128,2048]{1,0:T(8,128)(2,1)} %get-tuple-element.70), channel_id=1, source_target_pairs={{0,3},{1,0},{2,1},{3,2},{4,7},{5,4},{6,5},{7,6},{8,11},{9,8},{10,9... | collective-permute-start | bytes 1572872 | tf_op jit(solution)/shard_map/ppermute | solution.py:99
  477.5 29.4 %collective-permute-start.37 = (bf16[256,896]{1,0:T(8,128)(2,1)S(1)}, bf16[256,896]{1,0:T(8,128)(2,1)S(1)}, u32[]{:S(2)}, u32[]{:S(2)}) collective-permute-start(bf16[256,896]{1,0:T(8,128)(2,1)S(1)} %get-tuple-element.104), channel_id=1, source_target_pairs={{0,24},{4,28},{8,16},{12,20},{16,8},{20,12},{24,0},{28,4},{1,25},{... | collective-permute-start | bytes 1376264 | tf_op jit(solution)/shard_map/ppermute | solution.py:47
  479.6 28.4 %collective-permute-start.36 = (bf16[256,896]{1,0:T(8,128)(2,1)S(1)}, bf16[256,896]{1,0:T(8,128)(2,1)S(1)}, u32[]{:S(2)}, u32[]{:S(2)}) collective-permute-start(bf16[256,896]{1,0:T(8,128)(2,1)S(1)} %get-tuple-element.105), channel_id=1, source_target_pairs={{0,16},{4,20},{8,24},{12,28},{16,0},{20,4},{24,8},{28,12},{1,17},{... | collective-permute-start | bytes 1376264 | tf_op jit(solution)/shard_map/ppermute | solution.py:47
  488.9 43.7 %collective-permute-start.32 = (bf16[256,2048]{1,0:T(8,128)(2,1)S(1)}, bf16[256,2048]{1,0:T(8,128)(2,1)}, u32[]{:S(2)}, u32[]{:S(2)}) collective-permute-start(bf16[256,2048]{1,0:T(8,128)(2,1)S(1)} %pad_maximum_fusion.5), channel_id=1, source_target_pairs={{0,16},{4,20},{8,24},{12,28},{16,0},{20,4},{24,8},{28,12},{1,17},{... | collective-permute-start | bytes 3145736 | tf_op jit(solution)/shard_map/ppermute | solution.py:47
  491.5 41.1 %collective-permute-start.30 = (bf16[256,2048]{1,0:T(8,128)(2,1)}, bf16[256,2048]{1,0:T(8,128)(2,1)}, u32[]{:S(2)}, u32[]{:S(2)}) collective-permute-start(bf16[256,2048]{1,0:T(8,128)(2,1)} %pad_maximum_fusion.4), channel_id=1, source_target_pairs={{0,8},{4,12},{8,0},{12,4},{16,24},{20,28},{24,16},{28,20},{1,9},{5... | collective-permute-start | bytes 3145736 | tf_op jit(solution)/shard_map/ppermute | solution.py:47
  521.3 49.1 %collective-permute-start.43 = (bf16[2048,256]{1,0:T(8,128)(2,1)}, bf16[2048,256]{1,0:T(8,128)(2,1)S(1)}, u32[]{:S(2)}, u32[]{:S(2)}) collective-permute-start(bf16[2048,256]{1,0:T(8,128)(2,1)} %pad_maximum_fusion.6), channel_id=1, source_target_pairs={{0,8},{4,12},{8,0},{12,4},{16,24},{20,28},{24,16},{28,20},{1,9},{5... | collective-permute-start | bytes 3145736 | tf_op jit(solution)/shard_map/ppermute | solution.py:47
  526.7 43.7 %collective-permute-start.44 = (bf16[2048,256]{1,0:T(8,128)(2,1)}, bf16[2048,256]{1,0:T(8,128)(2,1)S(1)}, u32[]{:S(2)}, u32[]{:S(2)}) collective-permute-start(bf16[2048,256]{1,0:T(8,128)(2,1)} %pad_maximum_fusion.7), channel_id=1, source_target_pairs={{0,16},{4,20},{8,24},{12,28},{16,0},{20,4},{24,8},{28,12},{1,17},{... | collective-permute-start | bytes 3145736 | tf_op jit(solution)/shard_map/ppermute | solution.py:47
  534.8 28.7 %collective-permute-start.41 = (bf16[64,2048]{1,0:T(8,128)(2,1)S(1)}, bf16[64,2048]{1,0:T(8,128)(2,1)S(1)}, u32[]{:S(2)}, u32[]{:S(2)}) collective-permute-start(bf16[64,2048]{1,0:T(8,128)(2,1)S(1)} %get-tuple-element.106), channel_id=1, source_target_pairs={{0,1},{1,2},{2,3},{3,0},{4,5},{5,6},{6,7},{7,4},{8,9},{9,10},{10,1... | collective-permute-start | bytes 786440 | tf_op jit(solution)/shard_map/ppermute | solution.py:99
  (75 other events, 593.6 us)
Sparse Core Ops, SparseCore 0:
  10.4 106.3 all-gather.4
  119.4 27.9 all-gather.6
  156.3 55.6 all-gather.8
  213.7 55.9 all-gather.10
  314.7 45.6 reduce-scatter.3
  363.6 93.6 reduce-scatter.7
  461.9 50.9 reduce-scatter.5

commit v5 on v4

--- a/solution.py
+++ b/solution.py
@@ -768,7 +768,7 @@
     group, QD = o_parts[0].shape
     D = w_out.shape[1]
     rows = group // H
-    columns = 512
+    columns = 1024
     piece = pl.BlockSpec((H * QD, columns), lambda n, s: (0, n))
     return call(
         out_kernel,

time: 598 us -> 598 us (level)
  no operation moved by 1% of the time
where the time goes in v5:
time: 598 us; the launch traced here: 588 us
  Pallas kernels  222 us (37%)
  waiting for transfers between devices  207 us (35%)
  starting transfers between devices  83.2 us (14%)
  local copies, waits for them, and re-layouts  31.1 us (5%)
  other arithmetic  28.8 us (5%)
  between operations  15.1 us (3%)
    pallas_call x29, Pallas kernels, call(): pl.pallas_call(run, grid_spec=pltpu.PrefetchScalarGridSpec(num_scalar_pre...  222 us
    ppermute x27, waiting for transfers between devices, swap(): return lax.ppermute(x, 'blk', [(i, i ^ bit) for i in range(devices)])  96.6 us
    ppermute x18, waiting for transfers between devices, head_shift(): lax.ppermute(x, 'head', [(i, (i + by) % devices) for i in range(devices)])  72.6 us
    ppermute x18, starting transfers between devices, head_shift(): lax.ppermute(x, 'head', [(i, (i + by) % devices) for i in range(devices)])  41.9 us
    ppermute x27, starting transfers between devices, swap(): return lax.ppermute(x, 'blk', [(i, i ^ bit) for i in range(devices)])  28.4 us
    all_to_all x3, waiting for transfers between devices, head_exchange(): lax.all_to_all(parts, 'head', split_axis=0, concat_axis=0, tiled=True)  17.6 us
    unnamed x90, local copies, waits for them, and re-layouts  14 us
    all_to_all x3, starting transfers between devices, head_exchange(): lax.all_to_all(parts, 'head', split_axis=0, concat_axis=0, tiled=True)  12.5 us
  transfers between devices with their start and end apart: 55, of which 28 were waited for; matrix products, arithmetic and copies ran while one was open for 7% of the time, Pallas kernels for 34%

profile of v5, /device:TPU:0, one launch (start us, length us, event | category | flops | bytes accessed | tf_op | source)
XLA Modules:
  0.0 588.1 jit_solution(8348837410858158857)
XLA Ops:
  44.4 14.5 %collective-permute-done.5 = bf16[256,896]{1,0:T(8,128)(2,1)S(1)} collective-permute-done((bf16[256,896]{1,0:T(8,128)(2,1)S(1)}, bf16[256,896]{1,0:T(8,128)(2,1)S(1)}, u32[]{:S(2)}, u32[]{:S(2)}) %collective-permute-start.5) | collective-permute-done | bytes 458784 | tf_op jit(solution)/shard_map/ppermute | solution.py:47
  58.8 8.7 %collective-permute-done.4 = bf16[256,896]{1,0:T(8,128)(2,1)S(1)} collective-permute-done((bf16[256,896]{1,0:T(8,128)(2,1)S(1)}, bf16[256,896]{1,0:T(8,128)(2,1)S(1)}, u32[]{:S(2)}, u32[]{:S(2)}) %collective-permute-start.4) | collective-permute-done | bytes 458784 | tf_op jit(solution)/shard_map/ppermute | solution.py:47
  70.7 17.6 %all-to-all-done.refs_2_ = bf16[4,128,2048]{2,1,0:T(8,128)(2,1)S(1)} async-done(((bf16[4,128,2048]{2,1,0:T(8,128)(2,1)}), bf16[4,128,2048]{2,1,0:T(8,128)(2,1)S(1)}, u32[]{:S(2)}, u32[]{:S(2)}) %all-to-all-start) | async-done | bytes 2097184 | tf_op jit(solution)/shard_map/all_to_all | solution.py:95
  96.6 8.1 %shard_map.216 = (bf16[4,2,64,2048]{3,2,1,0:T(8,128)(2,1)}, bf16[4,2,64,512]{3,2,1,0:T(8,128)(2,1)}, bf16[4,2,64,256]{3,2,1,0:T(8,128)(2,1)}, f32[8,2048]{1,0:T(8,128)}) custom-call(s32[4]{0:T(128)} %pad_add_fusion.refs_0_, bf16[4,2,64,2048]{3,2,1,0:T(8,128)(2,1)} %bitcast.142, bf16[4,256,896]{2,1,0:T(8,128)(2,1)} %pad_maximum_fusion.1.refs_2_.refs_8_, ...), custom_call_target="tpu_custom_call" | custom-call | flops 161061280 | bytes 786432 | tf_op jit(solution)/shard_map/pallas_call | solution.py:133
  104.8 12.0 %all-gather.5.cloned.1.call-done.refs_2_.refs_3_.refs_4_ = bf16[2048,4096]{1,0:T(8,128)(2,1)} async-done(((bf16[256,4096]{1,0:T(8,128)(2,1)}), bf16[2048,4096]{1,0:T(8,128)(2,1)}) %all-gather.5.cloned.1.call-update) | async-done | bytes 16777232 | tf_op jit(solution)/shard_map/all_gather | solution.py:1177
  138.6 14.7 %shard_map.218 = (bf16[4,2,2,32,512]{4,3,2,1,0:T(8,128)(2,1)}, f32[2,2,2,1,512]{4,3,2,1,0:T(1,128)}) custom-call(s32[4]{0:T(128)} %pad_add_fusion.refs_0_, bf16[4,2,2,32,512]{4,3,2,1,0:T(8,128)(2,1)} %bitcast.165, bf16[4,4,2,2,32,256]{5,4,3,2,1,0:T(8,128)(2,1)} %pad_maximum_fusion.2.refs_2_, bf16[4,4,2,2,32,256]{5,4,3,2,1,0:T(8,128)(2,1)} %bitcast.150, ...), custom_call_target="tpu_custom_call" | custom-call | flops 214748368 | bytes 314572 | tf_op jit(solution)/shard_map/pallas_call | solution.py:133
  163.9 11.3 %collective-permute-done.13.refs_4_.refs_7_ = bf16[512,512]{1,0:T(8,128)(2,1)S(1)} collective-permute-done((bf16[512,512]{1,0:T(8,128)(2,1)S(1)}, bf16[512,512]{1,0:T(8,128)(2,1)S(1)}, u32[]{:S(2)}, u32[]{:S(2)}) %collective-permute-start.13) | collective-permute-done | bytes 524320 | tf_op jit(solution)/shard_map/ppermute | solution.py:99
  175.2 32.9 %collective-permute-done.12.refs_3_.refs_6_ = bf16[512,512]{1,0:T(8,128)(2,1)S(1)} collective-permute-done((bf16[512,512]{1,0:T(8,128)(2,1)S(1)}, bf16[512,512]{1,0:T(8,128)(2,1)S(1)}, u32[]{:S(2)}, u32[]{:S(2)}) %collective-permute-start.12) | collective-permute-done | bytes 524320 | tf_op jit(solution)/shard_map/ppermute | solution.py:99
  216.1 12.1 %shard_map.221 = (bf16[512,2048]{1,0:T(8,128)(2,1)}, f32[128,2048]{1,0:T(8,128)}, bf16[128,2048]{1,0:T(8,128)(2,1)}) custom-call(s32[4]{0:T(128)} %pad_add_fusion.refs_0_, bf16[512,2048]{1,0:T(8,128)(2,1)} %bitcast.143, f32[8,2048]{1,0:T(8,128)} %get-tuple-element.55.refs_2_.refs_4_, bf16[2048,2048]{1,0:T(8,128)(2,1)} %all-gather.9.cloned.1.call-done.refs_3_.refs_5_, ...), custom_call_target="tpu_custom_call" | custom-call | flops 429496736 | bytes 1468006 | tf_op jit(solution)/shard_map/pallas_call | solution.py:133
  228.2 15.7 %shard_map.222 = (f32[512,2048]{1,0:T(8,128)}, f32[512,2048]{1,0:T(8,128)}, bf16[512,2048]{1,0:T(8,128)(2,1)}) custom-call(s32[4]{0:T(128)} %pad_add_fusion.refs_0_, bf16[512,2048]{1,0:T(8,128)(2,1)} %get-tuple-element.61.refs_1_, bf16[2048,4096]{1,0:T(8,128)(2,1)} %all-gather.5.cloned.1.call-done.refs_2_.refs_3_.refs_4_, ...), custom_call_target="tpu_custom_call" | custom-call | flops 858993472 | bytes 2936012 | tf_op jit(solution)/shard_map/pallas_call | solution.py:133
  256.0 7.4 %collective-permute-done.14.refs_3_ = bf16[4,2048,256]{2,1,0:T(8,128)(2,1)S(1)} collective-permute-done((bf16[4,2048,256]{2,1,0:T(8,128)(2,1)}, bf16[4,2048,256]{2,1,0:T(8,128)(2,1)S(1)}, u32[]{:S(2)}, u32[]{:S(2)}) %collective-permute-start.14) | collective-permute-done | bytes 4194336 | tf_op jit(solution)/shard_map/ppermute | solution.py:47
  265.3 8.8 %shard_map.226.refs_7_.refs_1_ = bf16[4,2048,256]{2,1,0:T(8,128)(2,1)} custom-call(s32[4]{0:T(128)} %pad_add_fusion.refs_0_, bf16[512,2048]{1,0:T(8,128)(2,1)} %get-tuple-element.62.refs_3_.refs_1_, bf16[512,2048]{1,0:T(8,128)(2,1)} %bitcast.146, bf16[4,2048,256]{2,1,0:T(8,128)(2,1)} %copy-done.5), custom_call_target="tpu_custom_call" | custom-call | flops 214748368 | bytes 1258291 | tf_op jit(solution)/shard_map/pallas_call | solution.py:133
  278.5 24.5 %shard_map.227 = (bf16[512,2048]{1,0:T(8,128)(2,1)}, bf16[512,2048]{1,0:T(8,128)(2,1)}, bf16[512,2048]{1,0:T(8,128)(2,1)}) custom-call(s32[4]{0:T(128)} %pad_add_fusion.refs_0_, f32[512,2048]{1,0:T(8,128)} %get-tuple-element.63.refs_1_, f32[512,2048]{1,0:T(8,128)} %get-tuple-element.64.refs_2_, ...), custom_call_target="tpu_custom_call" | custom-call | flops 1288490240 | bytes 4404019 | tf_op jit(solution)/shard_map/pallas_call | solution.py:133
  304.0 10.2 %shard_map.228 = bf16[1024,4096]{1,0:T(8,128)(2,1)} custom-call(s32[4]{0:T(128)} %pad_add_fusion.refs_0_, bf16[512,2048]{1,0:T(8,128)(2,1)} %get-tuple-element.61.refs_1_, bf16[512,2048]{1,0:T(8,128)(2,1)} %get-tuple-element.65.refs_2_, bf16[512,2048]{1,0:T(8,128)(2,1)} %get-tuple-element.66.refs_3_, bf16[1024,256]{1,0:T(8,128)(2,1)} %copy-done.14, ...), custom_call_target="tpu_custom_call" | custom-call | flops 429496736 | bytes 2306867 | tf_op jit(solution)/shard_map/pallas_call | solution.py:133
  314.3 13.4 %collective-permute-done.17.refs_4_ = bf16[1024,4096]{1,0:T(8,128)(2,1)} collective-permute-done((bf16[1024,4096]{1,0:T(8,128)(2,1)}, bf16[1024,4096]{1,0:T(8,128)(2,1)}, u32[]{:S(2)}, u32[]{:S(2)}) %collective-permute-start.17) | collective-permute-done | bytes 8388640 | tf_op jit(solution)/shard_map/ppermute | solution.py:47
  327.7 12.1 %shard_map.229.refs_3_.refs_6_ = bf16[1024,4096]{1,0:T(8,128)(2,1)} custom-call(s32[4]{0:T(128)} %pad_add_fusion.refs_0_, bf16[512,2048]{1,0:T(8,128)(2,1)} %get-tuple-element.61.refs_1_, bf16[512,2048]{1,0:T(8,128)(2,1)} %get-tuple-element.65.refs_2_, bf16[512,2048]{1,0:T(8,128)(2,1)} %get-tuple-element.66.refs_3_, ...), custom_call_target="tpu_custom_call" | custom-call | flops 429496736 | bytes 2306867 | tf_op jit(solution)/shard_map/pallas_call | solution.py:133
  339.9 9.5 %shard_map.230 = (bf16[128,2048]{1,0:T(8,128)(2,1)}, bf16[128,2048]{1,0:T(8,128)(2,1)}, bf16[128,2048]{1,0:T(8,128)(2,1)}, bf16[128,2048]{1,0:T(8,128)(2,1)}) custom-call(s32[4]{0:T(128)} %pad_add_fusion.refs_0_, bf16[512,2048]{1,0:T(8,128)(2,1)} %get-tuple-element.62.refs_3_.refs_1_, bf16[2048,2048]{1,0:T(8,128)(2,1)} %all-gather.11.cloned.1.call-done.refs_5_.refs_2_, ...), custom_call_target="tpu_custom_call" | custom-call | flops 429496736 | bytes 1258291 | tf_op jit(solution)/shard_map/pallas_call | solution.py:133
  352.2 8.2 %reduce-scatter.4.cloned.1.call-done = bf16[128,2048]{1,0:T(8,128)(2,1)} async-done(((bf16[512,2048]{1,0:T(8,128)(2,1)}), bf16[128,2048]{1,0:T(8,128)(2,1)}) %reduce-scatter.4.cloned.1.call-update) | async-done | bytes 524304 | tf_op jit(solution)/shard_map/reduce_scatter | solution.py:1234
  360.3 9.4 %shard_map.231 = (f32[128,2048]{1,0:T(8,128)}, bf16[128,2048]{1,0:T(8,128)(2,1)}, f32[8,2048]{1,0:T(8,128)}, bf16[128,512]{1,0:T(8,128)(2,1)}, bf16[128,512]{1,0...) custom-call(s32[4]{0:T(128)} %pad_add_fusion.refs_0_, bf16[1,128,2048]{2,1,0:T(8,128)(2,1)} %bitcast.184, ...), custom_call_target="tpu_custom_call" | custom-call | flops 107374184 | bytes 1363148 | tf_op jit(solution)/shard_map/pallas_call | solution.py:133
  383.0 19.7 %shard_map.232 = (bf16[4,2,2,32,512]{4,3,2,1,0:T(8,128)(2,1)}, bf16[4,4,2,2,32,256]{5,4,3,2,1,0:T(8,128)(2,1)}, bf16[4,4,2,2,32,256]{5,4,3,2,1,0:T(8,128)(2,1)}) custom-call(s32[4]{0:T(128)} %pad_add_fusion.refs_0_, bf16[4,2,2,32,512]{4,3,2,1,0:T(8,128)(2,1)} %bitcast.166, bf16[4,4,2,2,32,256]{5,4,3,2,1,0:T(8,128)(2,1)} %pad_maximum_fusion.2.refs_2_, ...), custom_call_target="tpu_custom_call" | custom-call | flops 536870912 | bytes 629145 | tf_op jit(solution)/shard_map/pallas_call | solution.py:133
  439.4 10.8 %shard_map.234 = (bf16[512,2048]{1,0:T(8,128)(2,1)}, bf16[4,256,896]{2,1,0:T(8,128)(2,1)}, bf16[4,256,896]{2,1,0:T(8,128)(2,1)}) custom-call(s32[4]{0:T(128)} %pad_add_fusion.refs_0_, bf16[512,512]{1,0:T(8,128)(2,1)} %bitcast.186, f32[512,256]{1,0:T(8,128)} %fusion.10.refs_2_, f32[512,128]{1,0:T(8,128)} %bitcast.183, f32[512,128]{1,0:T(8,128)} %bitcast.182, ...), custom_call_target="tpu_custom_call" | custom-call | flops 322122560 | bytes 1363148 | tf_op jit(solution)/shard_map/pallas_call | solution.py:133
  496.4 10.4 %collective-permute-done.37 = bf16[256,896]{1,0:T(8,128)(2,1)S(1)} collective-permute-done((bf16[256,896]{1,0:T(8,128)(2,1)S(1)}, bf16[256,896]{1,0:T(8,128)(2,1)S(1)}, u32[]{:S(2)}, u32[]{:S(2)}) %collective-permute-start.37) | collective-permute-done | bytes 458784 | tf_op jit(solution)/shard_map/ppermute | solution.py:47
  508.8 8.8 %collective-permute-start.40 = (bf16[64,896]{1,0:T(8,128)(2,1)S(1)}, bf16[64,896]{1,0:T(8,128)(2,1)S(1)}, u32[]{:S(2)}, u32[]{:S(2)}) collective-permute-start(bf16[64,896]{1,0:T(8,128)(2,1)S(1)} %get-tuple-element.114), channel_id=1, source_target_pairs={{0,3},{1,0},{2,1},{3,2},{4,7},{5,4},{6,5},{7,6},{8,11},{9,8},{10,9... | collective-permute-start | bytes 344072 | tf_op jit(solution)/shard_map/ppermute | solution.py:99
  544.9 12.9 %collective-permute-done.42.refs_2_ = bf16[64,2048]{1,0:T(8,128)(2,1)S(1)} collective-permute-done((bf16[64,2048]{1,0:T(8,128)(2,1)S(1)}, bf16[64,2048]{1,0:T(8,128)(2,1)S(1)}, u32[]{:S(2)}, u32[]{:S(2)}) %collective-permute-start.42) | collective-permute-done | bytes 262176 | tf_op jit(solution)/shard_map/ppermute | solution.py:99
  (268 shorter events, 259.6 us)
Async XLA Ops:
  7.2 109.6 %all-gather.5.cloned.1.call-start = ((), (), s32[]{:S(2)}) async-start(), calls=%async_computation.6 | async-start | bytes 18874368 | tf_op jit(solution)/shard_map/all_gather | solution.py:1177
  35.5 52.8 %all-to-all-start = ((bf16[4,128,2048]{2,1,0:T(8,128)(2,1)}), bf16[4,128,2048]{2,1,0:T(8,128)(2,1)S(1)}, u32[]{:S(2)}, u32[]{:S(2)}) async-start(bf16[4,128,2048]{2,1,0:T(8,128)(2,1)} %get-tuple-element.53), calls=%async_computation | async-start | bytes 4194304 | tf_op jit(solution)/shard_map/all_to_all | solution.py:95
  69.0 27.6 %collective-permute-start.6 = (bf16[4,256,896]{2,1,0:T(8,128)(2,1)}, bf16[4,256,896]{2,1,0:T(8,128)(2,1)}, u32[]{:S(2)}, u32[]{:S(2)}) collective-permute-start(bf16[4,256,896]{2,1,0:T(8,128)(2,1)} %pad_maximum_fusion.1.refs_2_.refs_8_), channel_id=1, source_target_pairs={{0,4},{4,0},{8,12},{12,8},{16,20},{20,16},{24,28},{28,24},{1,5},{5... | collective-permute-start | bytes 5505032 | tf_op jit(solution)/shard_map/ppermute | solution.py:47
  92.2 45.0 %all-to-all-start.1 = ((bf16[4,64,2048]{2,1,0:T(8,128)(2,1)}), bf16[4,64,2048]{2,1,0:T(8,128)(2,1)S(1)}, u32[]{:S(2)}, u32[]{:S(2)}) async-start(bf16[4,64,2048]{2,1,0:T(8,128)(2,1)} %shard_map.215.refs_6_), calls=%async_computation.1 | async-start | bytes 2097152 | tf_op jit(solution)/shard_map/all_to_all | solution.py:95
  95.8 57.4 %all-gather.7.cloned.1.call-start = ((), (), s32[]{:S(2)}) async-start(), calls=%async_computation.7 | async-start | bytes 1310720 | tf_op jit(solution)/shard_map/all_gather | solution.py:1214
  119.3 96.9 %all-gather.9.cloned.1.call-start = ((), (), s32[]{:S(2)}) async-start(), calls=%async_computation.8 | async-start | bytes 9437184 | tf_op jit(solution)/shard_map/all_gather | solution.py:1219
  156.2 122.3 %all-gather.11.cloned.1.call-start = ((), (), s32[]{:S(2)}) async-start(), calls=%async_computation.9 | async-start | bytes 9437184 | tf_op jit(solution)/shard_map/all_gather | solution.py:1220
  162.8 45.2 %collective-permute-start.12 = (bf16[512,512]{1,0:T(8,128)(2,1)S(1)}, bf16[512,512]{1,0:T(8,128)(2,1)S(1)}, u32[]{:S(2)}, u32[]{:S(2)}) collective-permute-start(bf16[512,512]{1,0:T(8,128)(2,1)S(1)} %bitcast.172), channel_id=1, source_target_pairs={{0,2},{1,3},{2,0},{3,1},{4,6},{5,7},{6,4},{7,5},{8,10},{9,11},{10,... | collective-permute-start | bytes 1572872 | tf_op jit(solution)/shard_map/ppermute | solution.py:99
  162.8 45.2 %collective-permute-start.11 = (bf16[512,512]{1,0:T(8,128)(2,1)S(1)}, bf16[512,512]{1,0:T(8,128)(2,1)S(1)}, u32[]{:S(2)}, u32[]{:S(2)}) collective-permute-start(bf16[512,512]{1,0:T(8,128)(2,1)S(1)} %bitcast.173), channel_id=1, source_target_pairs={{0,1},{1,2},{2,3},{3,0},{4,5},{5,6},{6,7},{7,4},{8,9},{9,10},{10,1... | collective-permute-start | bytes 1572872 | tf_op jit(solution)/shard_map/ppermute | solution.py:99
  212.4 31.6 %all-to-all-start.2 = ((bf16[4,64,2048]{2,1,0:T(8,128)(2,1)}), bf16[4,64,2048]{2,1,0:T(8,128)(2,1)S(1)}, u32[]{:S(2)}, u32[]{:S(2)}) async-start(bf16[4,64,2048]{2,1,0:T(8,128)(2,1)} %shard_map.220.refs_8_), calls=%async_computation.2 | async-start | bytes 2097152 | tf_op jit(solution)/shard_map/all_to_all | solution.py:95
  215.9 144.4 %reduce-scatter.4.cloned.1.call-start = ((), (), s32[]{:S(2)}) async-start(), calls=%async_computation.10 | async-start | bytes 2621440 | tf_op jit(solution)/shard_map/reduce_scatter | solution.py:1234
  275.8 27.3 %collective-permute-start.16 = (bf16[1024,256]{1,0:T(8,128)(2,1)S(1)}, bf16[1024,256]{1,0:T(8,128)(2,1)S(1)}, u32[]{:S(2)}, u32[]{:S(2)}) collective-permute-start(bf16[1024,256]{1,0:T(8,128)(2,1)S(1)} %get-tuple-element.93), channel_id=1, source_target_pairs={{0,16},{4,20},{8,24},{12,28},{16,0},{20,4},{24,8},{28,12},{1,17},{... | collective-permute-start | bytes 1572872 | tf_op jit(solution)/shard_map/ppermute | solution.py:47
  314.3 149.0 %reduce-scatter.8.cloned.1.call-start = ((), (), s32[]{:S(2)}) async-start(), calls=%async_computation.12 | async-start | bytes 10485760 | tf_op jit(solution)/shard_map/reduce_scatter | solution.py:115
  339.8 230.5 %reduce-scatter.6.cloned.1.call-start = ((), (), s32[]{:S(2)}) async-start(), calls=%async_computation.11 | async-start | bytes 2621440 | tf_op jit(solution)/shard_map/reduce_scatter | solution.py:1290
  349.4 32.7 %collective-permute-start.18 = (bf16[128,2048]{1,0:T(8,128)(2,1)}, bf16[128,2048]{1,0:T(8,128)(2,1)S(1)}, u32[]{:S(2)}, u32[]{:S(2)}) collective-permute-start(bf16[128,2048]{1,0:T(8,128)(2,1)} %get-tuple-element.68), channel_id=1, source_target_pairs={{0,1},{1,2},{2,3},{3,0},{4,5},{5,6},{6,7},{7,4},{8,9},{9,10},{10,1... | collective-permute-start | bytes 1572872 | tf_op jit(solution)/shard_map/ppermute | solution.py:99
  402.8 35.0 %collective-permute-start.19 = (bf16[128,2048]{1,0:T(8,128)(2,1)}, bf16[128,2048]{1,0:T(8,128)(2,1)S(1)}, u32[]{:S(2)}, u32[]{:S(2)}) collective-permute-start(bf16[128,2048]{1,0:T(8,128)(2,1)} %get-tuple-element.69), channel_id=1, source_target_pairs={{0,2},{1,3},{2,0},{3,1},{4,6},{5,7},{6,4},{7,5},{8,10},{9,11},{10,... | collective-permute-start | bytes 1572872 | tf_op jit(solution)/shard_map/ppermute | solution.py:99
  405.5 32.4 %collective-permute-start.20 = (bf16[128,2048]{1,0:T(8,128)(2,1)}, bf16[128,2048]{1,0:T(8,128)(2,1)S(1)}, u32[]{:S(2)}, u32[]{:S(2)}) collective-permute-start(bf16[128,2048]{1,0:T(8,128)(2,1)} %get-tuple-element.70), channel_id=1, source_target_pairs={{0,3},{1,0},{2,1},{3,2},{4,7},{5,4},{6,5},{7,6},{8,11},{9,8},{10,9... | collective-permute-start | bytes 1572872 | tf_op jit(solution)/shard_map/ppermute | solution.py:99
  477.4 29.4 %collective-permute-start.37 = (bf16[256,896]{1,0:T(8,128)(2,1)S(1)}, bf16[256,896]{1,0:T(8,128)(2,1)S(1)}, u32[]{:S(2)}, u32[]{:S(2)}) collective-permute-start(bf16[256,896]{1,0:T(8,128)(2,1)S(1)} %get-tuple-element.104), channel_id=1, source_target_pairs={{0,24},{4,28},{8,16},{12,20},{16,8},{20,12},{24,0},{28,4},{1,25},{... | collective-permute-start | bytes 1376264 | tf_op jit(solution)/shard_map/ppermute | solution.py:47
  479.5 28.4 %collective-permute-start.36 = (bf16[256,896]{1,0:T(8,128)(2,1)S(1)}, bf16[256,896]{1,0:T(8,128)(2,1)S(1)}, u32[]{:S(2)}, u32[]{:S(2)}) collective-permute-start(bf16[256,896]{1,0:T(8,128)(2,1)S(1)} %get-tuple-element.105), channel_id=1, source_target_pairs={{0,16},{4,20},{8,24},{12,28},{16,0},{20,4},{24,8},{28,12},{1,17},{... | collective-permute-start | bytes 1376264 | tf_op jit(solution)/shard_map/ppermute | solution.py:47
  488.8 43.8 %collective-permute-start.32 = (bf16[256,2048]{1,0:T(8,128)(2,1)S(1)}, bf16[256,2048]{1,0:T(8,128)(2,1)}, u32[]{:S(2)}, u32[]{:S(2)}) collective-permute-start(bf16[256,2048]{1,0:T(8,128)(2,1)S(1)} %pad_maximum_fusion.5), channel_id=1, source_target_pairs={{0,16},{4,20},{8,24},{12,28},{16,0},{20,4},{24,8},{28,12},{1,17},{... | collective-permute-start | bytes 3145736 | tf_op jit(solution)/shard_map/ppermute | solution.py:47
  491.5 41.1 %collective-permute-start.30 = (bf16[256,2048]{1,0:T(8,128)(2,1)}, bf16[256,2048]{1,0:T(8,128)(2,1)}, u32[]{:S(2)}, u32[]{:S(2)}) collective-permute-start(bf16[256,2048]{1,0:T(8,128)(2,1)} %pad_maximum_fusion.4), channel_id=1, source_target_pairs={{0,8},{4,12},{8,0},{12,4},{16,24},{20,28},{24,16},{28,20},{1,9},{5... | collective-permute-start | bytes 3145736 | tf_op jit(solution)/shard_map/ppermute | solution.py:47
  521.2 49.1 %collective-permute-start.43 = (bf16[2048,256]{1,0:T(8,128)(2,1)}, bf16[2048,256]{1,0:T(8,128)(2,1)S(1)}, u32[]{:S(2)}, u32[]{:S(2)}) collective-permute-start(bf16[2048,256]{1,0:T(8,128)(2,1)} %pad_maximum_fusion.6), channel_id=1, source_target_pairs={{0,8},{4,12},{8,0},{12,4},{16,24},{20,28},{24,16},{28,20},{1,9},{5... | collective-permute-start | bytes 3145736 | tf_op jit(solution)/shard_map/ppermute | solution.py:47
  526.6 43.7 %collective-permute-start.44 = (bf16[2048,256]{1,0:T(8,128)(2,1)}, bf16[2048,256]{1,0:T(8,128)(2,1)S(1)}, u32[]{:S(2)}, u32[]{:S(2)}) collective-permute-start(bf16[2048,256]{1,0:T(8,128)(2,1)} %pad_maximum_fusion.7), channel_id=1, source_target_pairs={{0,16},{4,20},{8,24},{12,28},{16,0},{20,4},{24,8},{28,12},{1,17},{... | collective-permute-start | bytes 3145736 | tf_op jit(solution)/shard_map/ppermute | solution.py:47
  534.8 28.7 %collective-permute-start.41 = (bf16[64,2048]{1,0:T(8,128)(2,1)S(1)}, bf16[64,2048]{1,0:T(8,128)(2,1)S(1)}, u32[]{:S(2)}, u32[]{:S(2)}) collective-permute-start(bf16[64,2048]{1,0:T(8,128)(2,1)S(1)} %get-tuple-element.106), channel_id=1, source_target_pairs={{0,1},{1,2},{2,3},{3,0},{4,5},{5,6},{6,7},{7,4},{8,9},{9,10},{10,1... | collective-permute-start | bytes 786440 | tf_op jit(solution)/shard_map/ppermute | solution.py:99
  (75 other events, 593.5 us)
Sparse Core Ops, SparseCore 0:
  10.4 106.3 all-gather.4
  119.4 27.9 all-gather.6
  156.3 55.6 all-gather.8
  213.7 55.9 all-gather.10
  314.4 45.9 reduce-scatter.3
  363.5 93.6 reduce-scatter.7
  461.8 50.8 reduce-scatter.5
